TPU v7x, 512 devices: a whole 4x4x16 slice. The times are simulated.
512 devices in a mesh: dp: 64 (over x, z_lo, core), tensor: 8 (over y, z_hi).
Axes of the slice: x: 4, y: 4, z: 16 (z_hi: 2, z_lo: 8; z = z_hi * 8 + z_lo), core: 2. Of those that a mesh axis runs over, the one named last changes fastest.
Arguments:
- hidden: bfloat16 [16384, 4096], P('dp', 'tensor'), may hold values from -12 to 12
- targets: int32 [16384], P('dp'), may hold values from 0 to 8191
- lengths: int32 [64], P('dp'), may hold values from 64 to 256
- layer_gain: float32 [2, 4096], P(None, 'tensor'), may hold values from 0.25 to 1.75
- down_codes: bfloat16 [2, 4096, 512], P(None, ('tensor', 'dp')), may hold values from -4 to 4
- down_scales: float32 [2, 32, 4], P(None, 'tensor'), may hold values from 0.0078125 to 0.03125
- up_codes: bfloat16 [2, 512, 4096], P(None, None, ('tensor', 'dp')), may hold values from -4 to 4
- up_scales: float32 [2, 4, 32], P(None, None, 'tensor'), may hold values from 0.022097087 to 0.088388346
- final_gain: float32 [4096], replicated, may hold values from 0.25 to 1.75
- head_codes: bfloat16 [4096, 8192], P('dp', 'tensor'), may hold values from -4 to 4
- head_scales: float32 [32, 64], P(None, 'tensor'), may hold values from 0.03125 to 2, as said below
Outputs:
- log_probs: float32 [16384], P('dp')
Inputs may be any that keep to these rules, and one draw needn't show every extreme that they name: `head_scales`: positive block scales of the output projection.
All inputs are finite; a program needn't handle non-finite values.
Results may differ from a plain program's by a relative error of at most 0.008.
Values may be sent and summed in bfloat16 or wider, within the bound.
No kernel may reach another device: no remote copies, remote signals or barrier semaphores. Data moves between devices by JAX's collectives and lax.ppermute only.
A program may use at most 64 MiB of HBM per device.

v0:
```python
import jax
import jax.numpy as jnp
from jax import lax
from jax.sharding import PartitionSpec as P

eps = 1e-06
tile_edge = 128


def dequant(codes, scales):
    rows_all, cols_all = codes.shape
    blocks = codes.astype(jnp.float32).reshape(
        rows_all // tile_edge, tile_edge, cols_all // tile_edge, tile_edge
    )
    blocks = blocks * scales[:, None, :, None]
    return blocks.reshape(rows_all, cols_all).astype(jnp.bfloat16)


def per_device(
    hidden,
    targets,
    lengths,
    layer_gain,
    down_codes,
    down_scales,
    up_codes,
    up_scales,
    final_gain,
    head_codes,
    head_scales,
):
    tok_rows = hidden.shape[0]
    model_width = hidden.shape[1] * lax.axis_size("tensor")
    stream = hidden
    for layer in range(down_codes.shape[0]):
        stream_f = stream.astype(jnp.float32)
        squares = lax.psum(jnp.sum(stream_f * stream_f, axis=1), "tensor")
        inv = lax.rsqrt(squares / model_width + eps)
        normed = (stream_f * inv[:, None] * layer_gain[layer]).astype(jnp.bfloat16)
        down_rows = lax.all_gather(down_codes[layer], "dp", axis=0, tiled=True)
        down_weight = dequant(down_rows, down_scales[layer])
        partial_value = jnp.dot(normed, down_weight, preferred_element_type=jnp.float32)
        latent = lax.psum(partial_value.astype(jnp.bfloat16), "tensor").astype(jnp.float32)
        act = jax.nn.silu(latent).astype(jnp.bfloat16)
        up_columns = lax.all_gather(up_codes[layer], "dp", axis=1, tiled=True)
        up_weight = dequant(up_columns, up_scales[layer])
        branch = jnp.dot(act, up_weight, preferred_element_type=jnp.float32)
        stream = (stream_f + branch).astype(jnp.bfloat16)
    gathered = lax.all_gather(stream, "tensor", axis=1, tiled=True).astype(jnp.float32)
    inv_final = lax.rsqrt(jnp.mean(gathered * gathered, axis=1) + eps)
    final = (gathered * inv_final[:, None] * final_gain).astype(jnp.bfloat16)
    row_scale = jnp.repeat(head_scales, tile_edge, axis=0)
    local_vocab = head_codes.shape[1]
    piece = lax.all_gather(head_codes, "dp", axis=0, tiled=True)
    count = piece.shape[0]
    weight = piece.astype(jnp.float32).reshape(count, -1, tile_edge) * row_scale[:, :, None]
    weight = weight.reshape(count, local_vocab).astype(jnp.bfloat16)
    logits = jnp.dot(final, weight, preferred_element_type=jnp.float32)
    vocab_share = logits.shape[1]
    offset = lax.axis_index("tensor") * vocab_share
    columns = lax.broadcasted_iota(jnp.int32, logits.shape, 1) + offset
    target_local = jnp.sum(jnp.where(columns == targets[:, None], logits, 0.0), axis=1)
    local_top = jnp.max(logits, axis=1)
    top = lax.pmax(local_top, "tensor")
    local_total = jnp.sum(jnp.exp(logits - top[:, None]), axis=1)
    total, picked = lax.psum((local_total, target_local), "tensor")
    scored = picked - (top + jnp.log(total))
    position = lax.broadcasted_iota(jnp.int32, (tok_rows,), 0)
    return jnp.where(position < lengths[0], scored, jnp.zeros_like(scored))


def solution(mesh):
    in_specs = (
        P("dp", "tensor"),
        P("dp"),
        P("dp"),
        P(None, "tensor"),
        P(None, ("tensor", "dp"), None),
        P(None, "tensor", None),
        P(None, None, ("tensor", "dp")),
        P(None, None, "tensor"),
        P(),
        P("dp", "tensor"),
        P(None, "tensor"),
    )
    out_specs = P("dp")
    return jax.shard_map(
        per_device, mesh=mesh, in_specs=in_specs, out_specs=out_specs, check_vma=False
    )
```

profile of v0, /device:TPU:6, one launch (start us, length us, event | category | flops | bytes accessed | tf_op | source)
XLA Modules:
  0.0 934.1 jit_solution(7823344876587678979)
XLA Ops:
  6.5 0.0 copy-start
  6.5 0.0 copy-start.1
  6.5 0.0 copy-start.3
  6.5 0.0 all-reduce.4.cloned.1.call-start
  6.5 0.7 slice_bitcast_fusion.1
  7.3 0.7 fusion.46
  8.0 116.0 %all-gather = bf16[1,512,512]{2,1,0:T(8,128)(2,1)S(1)} all-gather(bf16[1,8,512]{2,1,0:T(8,128)(2,1)S(1)} %get-tuple-element.10), channel_id=2, replica_groups=mesh['dp'=64,'tensor'=8] {'dp'}, dimensions={1}, use_global_device_ids=true | all-gather | bytes 532480 | tf_op jit(solution)/shard_map/all_gather | solution.py:40
  124.0 0.8 fusion.48
  124.8 1.1 fusion.24
  125.9 42.2 %psum.42 = f32[256]{0:T(256)S(1)} all-reduce(f32[256]{0:T(256)S(1)} %fusion.24), channel_id=1, replica_groups=mesh['dp'=64,'tensor'=8] {'tensor'}, use_global_device_ids=true, to_apply=%region_1.0 | all-reduce | flops 256 | bytes 2048 | tf_op jit(solution)/shard_map/psum | solution.py:37
  168.1 0.2 mul.144
  168.3 2.0 convolution_convert_fusion.1
  170.3 0.0 all-reduce.4.cloned.1.call-update
  170.3 0.0 all-reduce.6.cloned.1.call-start
  170.3 0.0 copy-done.1
  170.4 106.4 %all-gather.1 = bf16[1,512,512]{1,2,0:T(8,128)(2,1)S(1)} all-gather(bf16[1,512,8]{1,2,0:T(8,128)(2,1)S(1)} %get-tuple-element.12), channel_id=3, replica_groups=mesh['dp'=64,'tensor'=8] {'dp'}, dimensions={2}, use_global_device_ids=true | all-gather | bytes 532480 | tf_op jit(solution)/shard_map/all_gather | solution.py:45
  276.8 0.0 copy-done.3
  276.8 0.1 copy.12
  276.9 107.6 %all-gather.2 = bf16[1,512,512]{2,1,0:T(8,128)(2,1)S(1)} all-gather(bf16[1,8,512]{2,1,0:T(8,128)(2,1)S(1)} %get-tuple-element.9), channel_id=4, replica_groups=mesh['dp'=64,'tensor'=8] {'dp'}, dimensions={1}, use_global_device_ids=true | all-gather | bytes 532480 | tf_op jit(solution)/shard_map/all_gather | solution.py:40
  384.5 0.0 all-reduce.4.cloned.1.call-done
  384.5 0.2 mul.149
  384.7 0.0 copy-done
  384.7 1.4 multiply_reduce_fusion
  386.1 35.4 %psum.44 = f32[256]{0:T(256)S(1)} all-reduce(f32[256]{0:T(256)S(1)} %get-tuple-element.19), channel_id=1, replica_groups=mesh['dp'=64,'tensor'=8] {'tensor'}, use_global_device_ids=true, to_apply=%region_4.5 | all-reduce | flops 256 | bytes 2048 | tf_op jit(solution)/shard_map/psum | solution.py:37
  421.5 0.2 mul.159
  421.7 0.0 copy-start.2
  421.7 1.1 convolution_convert_fusion
  422.8 0.0 all-reduce.6.cloned.1.call-update
  422.8 0.0 all-gather.7.cloned.1.call-start
  422.9 0.1 copy.13
  422.9 116.0 %all-gather.3 = bf16[1,512,512]{1,2,0:T(8,128)(2,1)S(1)} all-gather(bf16[1,512,8]{1,2,0:T(8,128)(2,1)S(1)} %get-tuple-element.11), channel_id=5, replica_groups=mesh['dp'=64,'tensor'=8] {'dp'}, dimensions={2}, use_global_device_ids=true | all-gather | bytes 532480 | tf_op jit(solution)/shard_map/all_gather | solution.py:45
  539.0 62.8 %all-reduce.6.cloned.1.call-done = bf16[256,512]{1,0:T(8,128)(2,1)} async-done(((bf16[256,512]{1,0:T(8,128)(2,1)}), bf16[256,512]{1,0:T(8,128)(2,1)}) %all-reduce.6.cloned.1.call-update) | async-done | bytes 262160 | tf_op jit(solution)/shard_map/psum | solution.py:43
  601.7 0.2 mul.164
  601.9 2.0 fusion.11
  604.0 0.0 all-gather.7.cloned.1.call-update
  604.0 0.0 all-gather.9.cloned.1.call-start
  604.0 0.5 all-gather.9.cloned.1.call-update
  604.6 0.0 copy-done.2
  604.6 0.1 copy.14
  605.3 106.3 %all-gather.7.cloned.1.call-done = bf16[256,4096]{1,0:T(8,128)(2,1)} async-done(((bf16[256,512]{1,0:T(8,128)(2,1)}), bf16[256,4096]{1,0:T(8,128)(2,1)}) %all-gather.7.cloned.1.call-update) | async-done | bytes 2097168 | tf_op jit(solution)/shard_map/all_gather | solution.py:49
  711.6 2.1 fusion.3
  713.7 121.1 %all-gather.9.cloned.1.call-done = bf16[4096,1024]{1,0:T(8,128)(2,1)} async-done(((bf16[64,1024]{1,0:T(8,128)(2,1)}), bf16[4096,1024]{1,0:T(8,128)(2,1)}) %all-gather.9.cloned.1.call-update) | async-done | bytes 8388624 | tf_op jit(solution)/shard_map/all_gather | solution.py:54
  834.8 0.1 broadcast_in_dim.7
  834.9 4.6 mul.173
  839.5 8.6 fusion.49
  848.2 41.8 %pmax.7 = f32[256]{0:T(256)S(1)} all-reduce(f32[256]{0:T(256)S(1)} %get-tuple-element.21), channel_id=1, replica_groups=mesh['dp'=64,'tensor'=8] {'tensor'}, use_global_device_ids=true, to_apply=%region_10.11 | all-reduce | flops 256 | bytes 2048 | tf_op jit(solution)/shard_map/pmax | solution.py:64
  890.0 1.1 exponential_reduce_fusion
  891.1 35.9 %all-reduce = (f32[256]{0:T(256)S(1)}, f32[256]{0:T(256)S(1)}) all-reduce(f32[256]{0:T(256)S(1)} %get-tuple-element.6, f32[256]{0:T(256)S(1)} %get-tuple-element.5), channel_id=1, replica_groups=mesh['dp'=64,'tensor'=8] {'tensor'}, use_global_device_ids=true, to_apply=%region_8.9 | all-reduce | flops 512 | bytes 4096 | tf_op jit(solution)/shard_map/psum | solution.py:66
  927.0 0.6 compare_select_fusion
  (6 shorter events, 0.0 us)
Async XLA Ops:
  6.5 378.1 %copy-start = (bf16[256,512]{1,0:T(8,128)(2,1)S(1)}, bf16[256,512]{1,0:T(8,128)(2,1)}, u32[]{:S(2)}) copy-start(bf16[256,512]{1,0:T(8,128)(2,1)} %param.11) | copy-start | bytes 786436
  6.5 163.8 %copy-start.1 = (bf16[2,512,8]{1,2,0:T(8,128)(2,1)S(1)}, bf16[2,512,8]{1,2,0:T(8,128)(2,1)}, u32[]{:S(2)}) copy-start(bf16[2,512,8]{1,2,0:T(8,128)(2,1)} %param.17) | copy-start | bytes 49156
  6.5 270.3 %copy-start.3 = (f32[2,4,4]{2,1,0:T(4,128)S(1)}, f32[2,4,4]{2,1,0:T(4,128)}, u32[]{:S(2)}) copy-start(f32[2,4,4]{2,1,0:T(4,128)} %param.18) | copy-start | bytes 388
  6.5 377.9 %all-reduce.4.cloned.1.call-start = ((), (), s32[]{:S(2)}) async-start(), calls=%async_computation | async-start | bytes 524288 | tf_op jit(solution)/shard_map/psum | solution.py:43
  170.3 431.4 %all-reduce.6.cloned.1.call-start = ((), (), s32[]{:S(2)}) async-start(), calls=%async_computation.1 | async-start | bytes 524288 | tf_op jit(solution)/shard_map/psum | solution.py:43
  421.7 182.9 %copy-start.2 = (f32[32,8]{0,1:T(8,128)S(1)}, f32[32,8]{0,1:T(8,128)}, u32[]{:S(2)}) copy-start(f32[32,8]{0,1:T(8,128)} %param.21) | copy-start | bytes 3076
  422.8 288.8 %all-gather.7.cloned.1.call-start = ((), (), s32[]{:S(2)}) async-start(), calls=%async_computation.2 | async-start | bytes 2359296 | tf_op jit(solution)/shard_map/all_gather | solution.py:49
  604.0 230.8 %all-gather.9.cloned.1.call-start = ((), (), s32[]{:S(2)}) async-start(), calls=%async_computation.3 | async-start | bytes 8519680 | tf_op jit(solution)/shard_map/all_gather | solution.py:54
Sparse Core Ops, SparseCore 0:
  170.4 154.8 all-reduce.3
  422.9 178.7 all-reduce.5
  604.8 106.7 all-gather.6
  713.6 121.1 all-gather.8
where the time goes:
time: 936 us; the launch traced here: 934 us
  blocking collectives  601 us (64%)
  waiting for transfers between devices  291 us (31%)
  matrix products  15.1 us (2%)
  between operations  13.9 us (1%)
    all_gather x2, blocking collectives, per_device(): down_rows = lax.all_gather(down_codes[layer], 'dp', axis=0, tiled=True)  224 us
    all_gather x2, blocking collectives, per_device(): up_columns = lax.all_gather(up_codes[layer], 'dp', axis=1, tiled=True)  222 us
    all_gather x1, waiting for transfers between devices, per_device(): piece = lax.all_gather(head_codes, 'dp', axis=0, tiled=True)  121 us
    all_gather x1, waiting for transfers between devices, per_device(): lax.all_gather(stream, 'tensor', axis=1, tiled=True).astype(jnp.float32)  106 us
    psum x2, blocking collectives, per_device(): squares = lax.psum(jnp.sum(stream_f * stream_f, axis=1), 'tensor')  77.6 us
    psum x2, waiting for transfers between devices, per_device(): lax.psum(partial_value.astype(jnp.bfloat16), 'tensor').astype(jnp.float32)  62.8 us
    pmax x1, blocking collectives, per_device(): top = lax.pmax(local_top, 'tensor')  41.8 us
    psum x1, blocking collectives, per_device(): total, picked = lax.psum((local_total, target_local), 'tensor')  35.9 us
  transfers between devices with their start and end apart: 4, of which 3 were waited for; matrix products, arithmetic and copies ran while one was open for 0% of the time, Pallas kernels for 0%

commit v1 on v0

v1 whole, which is shorter than its diff:
```python
import jax
import jax.numpy as jnp
from jax import lax
from jax.sharding import PartitionSpec as P

eps = 1e-06
tile_edge = 128
n_x, n_z, n_core = 4, 8, 2
n_y, n_hi = 4, 2
f32 = jnp.float32
bf16 = jnp.bfloat16


def dp_of(x, z, c):
    return (x * n_z + z) * n_core + c


x_groups = [[dp_of(x, z, c) for x in range(n_x)] for z in range(n_z) for c in range(n_core)]
y_groups = [[y * n_hi + h for y in range(n_y)] for h in range(n_hi)]
z_groups = [
    [dp_of(x, z, c) * n_y * n_hi + y * n_hi + h for h in range(n_hi) for z in range(n_z)]
    for x in range(n_x)
    for c in range(n_core)
    for y in range(n_y)
]
core_pairs = [
    (dp_of(x, z, c), dp_of(x, z, 1 - c))
    for x in range(n_x)
    for z in range(n_z)
    for c in range(n_core)
]
hi_pairs = [(y * n_hi + h, y * n_hi + 1 - h) for y in range(n_y) for h in range(n_hi)]


def share(block, axis, groups):
    copies = jnp.broadcast_to(block[None], (len(groups[0]),) + block.shape)
    return lax.all_to_all(copies, axis, 0, 0, axis_index_groups=groups)


def swap_hi(value):
    return lax.ppermute(value, "tensor", hi_pairs)


def in_hi_order(own, peer, hi):
    first = jnp.where(hi == 0, own, peer)
    second = jnp.where(hi == 0, peer, own)
    return first, second


def split_sum(total):
    top = lax.reduce_precision(total, 8, 7)
    return top.astype(bf16), (total - top).astype(bf16)


def silu(value):
    return value / (1.0 + jnp.exp(-value))


def per_device(
    hidden,
    targets,
    lengths,
    layer_gain,
    down_codes,
    down_scales,
    up_codes,
    up_scales,
    final_gain,
    head_codes,
    head_scales,
):
    tok_rows, share_width = hidden.shape
    layers, _, rank = down_codes.shape
    model_width = share_width * n_y * n_hi
    hi = lax.axis_index("tensor") % n_hi
    core = lax.axis_index("dp") % n_core

    with jax.named_scope("head_rows"):
        piece = lax.all_gather(head_codes, "dp", axis=0, tiled=True)

    with jax.named_scope("hidden_hi"):
        hidden_peer = swap_hi(hidden)
        small = jnp.concatenate(
            [layer_gain.reshape(-1), down_scales.reshape(-1), up_scales.reshape(-1)]
        )
        small_peer = swap_hi(small)

    with jax.named_scope("layer_codes"):
        codes = jnp.stack([down_codes, jnp.swapaxes(up_codes, 1, 2)], axis=1)
        rows = codes.shape[2]
        codes = codes.reshape(-1, rank)
        codes = lax.all_gather(
            codes, ("dp", "tensor"), axis=0, tiled=False, axis_index_groups=z_groups
        )
        codes = codes.reshape(-1, rank)
        codes = share(codes, "dp", x_groups)
        other = lax.ppermute(codes, "dp", core_pairs)
        zero, one = jnp.where(core == 0, codes, other), jnp.where(core == 0, other, codes)
        codes = jnp.stack([zero, one])
        codes = codes.reshape(n_core, n_x, n_hi, n_z, layers, 2, rows, rank)
        codes = codes.transpose(4, 5, 2, 1, 3, 0, 6, 7)
        codes = codes.reshape(layers, 2, n_hi * share_width // tile_edge, tile_edge, rank // tile_edge, tile_edge)

    def unpack(flat):
        gain, down, up = jnp.split(flat, [layer_gain.size, layer_gain.size + down_scales.size])
        return (
            gain.reshape(layer_gain.shape),
            down.reshape(down_scales.shape),
            jnp.swapaxes(up.reshape(up_scales.shape), 1, 2),
        )

    flats = in_hi_order(small, small_peer, hi)
    (gain_a, down_a, up_a), (gain_b, down_b, up_b) = unpack(flats[0]), unpack(flats[1])
    gain = jnp.concatenate([gain_a, gain_b], axis=1)
    scales = jnp.stack(
        [jnp.concatenate([down_a, down_b], axis=1), jnp.concatenate([up_a, up_b], axis=1)], axis=1
    )
    weights = codes.astype(f32) * scales[:, :, :, None, :, None]
    weights = weights.astype(bf16).reshape(layers, 2, n_hi * share_width, rank)

    stream = jnp.concatenate(in_hi_order(hidden, hidden_peer, hi), axis=1)
    for layer in range(layers):
        with jax.named_scope("down"):
            stream_f = stream.astype(f32)
            squares = jnp.sum(stream_f * stream_f, axis=1)
            scaled = (stream_f * gain[layer]).astype(bf16)
            part = jnp.dot(scaled, weights[layer, 0], preferred_element_type=f32).astype(bf16)
            top, rest = split_sum(squares)
            extra = jnp.concatenate([top, rest]).reshape(-1, rank)
            extra = jnp.pad(extra, ((0, 16 - extra.shape[0]), (0, 0)))
            parts = share(jnp.concatenate([part, extra], axis=0), "tensor", y_groups)
            parts = jnp.sum(parts.astype(f32), axis=0)
            total = parts[tok_rows:].reshape(-1)
            total = total[:tok_rows] + total[tok_rows : 2 * tok_rows]
        with jax.named_scope("up"):
            inv = lax.rsqrt(total / model_width + eps)
            act = silu(parts[:tok_rows] * inv[:, None]).astype(bf16)
            branch = lax.dot_general(
                act, weights[layer, 1], (((1,), (1,)), ((), ())), preferred_element_type=f32
            )
            stream = (stream_f + branch).astype(bf16)

    with jax.named_scope("stream_y"):
        gathered = share(stream, "tensor", y_groups)
        gathered = jnp.swapaxes(gathered, 0, 1).reshape(tok_rows, model_width)
    with jax.named_scope("head"):
        gathered_f = gathered.astype(f32)
        inv_final = lax.rsqrt(jnp.mean(gathered_f * gathered_f, axis=1) + eps)
        final = (gathered_f * inv_final[:, None] * final_gain).astype(bf16)
        count, local_vocab = piece.shape
        weight = piece.astype(f32).reshape(
            count // tile_edge, tile_edge, local_vocab // tile_edge, tile_edge
        )
        weight = weight * head_scales[:, None, :, None]
        weight = weight.reshape(count, local_vocab).astype(bf16)
        logits = jnp.dot(final, weight, preferred_element_type=f32)
        offset = lax.axis_index("tensor") * local_vocab
        columns = lax.broadcasted_iota(jnp.int32, logits.shape, 1) + offset
        picked = jnp.sum(jnp.where(columns == targets[:, None], logits, 0.0), axis=1)
        top = jnp.max(logits, axis=1)
        total = jnp.sum(jnp.exp(logits - top[:, None]), axis=1)

    def merge(stats):
        tops, totals, picks = stats[:, 0], stats[:, 1], stats[:, 2]
        highest = jnp.max(tops, axis=0)
        total = jnp.sum(totals * jnp.exp(tops - highest), axis=0)
        return jnp.stack([highest, total, jnp.sum(picks, axis=0)])

    with jax.named_scope("stats"):
        mine = merge(share(jnp.stack([top, total, picked]), "tensor", y_groups))
        both = merge(jnp.stack([mine, swap_hi(mine)]))
        scored = both[2] - (both[0] + jnp.log(both[1]))
        position = lax.broadcasted_iota(jnp.int32, (tok_rows,), 0)
        return jnp.where(position < lengths[0], scored, jnp.zeros_like(scored))


def solution(mesh):
    in_specs = (
        P("dp", "tensor"),
        P("dp"),
        P("dp"),
        P(None, "tensor"),
        P(None, ("tensor", "dp"), None),
        P(None, "tensor", None),
        P(None, None, ("tensor", "dp")),
        P(None, None, "tensor"),
        P(),
        P("dp", "tensor"),
        P(None, "tensor"),
    )
    out_specs = P("dp")
    return jax.shard_map(
        per_device, mesh=mesh, in_specs=in_specs, out_specs=out_specs, check_vma=False
    )
```

time: 936 us -> 261 us (0.28)
  blocking collectives: 601 us -> 117 us
  waiting for transfers between devices: 291 us -> 49.4 us
  starting transfers between devices: 0.13 us -> 27.5 us
  local copies, waits for them, and re-layouts: 8.06 us -> 23.6 us
  other arithmetic: 4.82 us -> 15.9 us
    all_gather x4 -> x1, blocking collectives: 446 us -> 38.5 us  [per_device(): lax.all_gather(codes, ('dp', 'tensor'), axis=0, tiled=False, axis_index_g...]
    all_gather x1, waiting for transfers between devices: 121 us -> 0.01 us  [per_device(): piece = lax.all_gather(head_codes, 'dp', axis=0, tiled=True)]
    psum x3 -> x0, blocking collectives: 113 us -> none  [the longest x2 77.6 us: per_device(): squares = lax.psum(jnp.sum(stream_f * stream_f, axis=1), 'tensor')]
    all_gather x1 -> x0, waiting for transfers between devices: 106 us -> none  [per_device(): lax.all_gather(stream, 'tensor', axis=1, tiled=True).astype(jnp.float32)]
    all_to_all x0 -> x4, blocking collectives: none -> 78.4 us  [share(): return lax.all_to_all(copies, axis, 0, 0, axis_index_groups=groups)]
    psum x2 -> x0, waiting for transfers between devices: 62.8 us -> none  [per_device(): lax.psum(partial_value.astype(jnp.bfloat16), 'tensor').astype(jnp.float32)]
    pmax x1 -> x0, blocking collectives: 41.8 us -> none  [per_device(): top = lax.pmax(local_top, 'tensor')]
    ppermute x0 -> x4, waiting for transfers between devices: none -> 24.7 us  [the longest x3 24.7 us: swap_hi(): return lax.ppermute(value, 'tensor', hi_pairs)]
  transfers between devices with their start and end apart: 4 -> 6, of which waited for: 3 -> 3; matrix products, arithmetic and copies ran while one was open for 0% -> 15% of each run, Pallas kernels for 0% -> 0%
where the time goes in v1:
time: 261 us; the launch traced here: 258 us
  blocking collectives  117 us (45%)
  waiting for transfers between devices  49.4 us (19%)
  starting transfers between devices  27.5 us (11%)
  local copies, waits for them, and re-layouts  23.6 us (9%)
  other arithmetic  15.9 us (6%)
  between operations  14.5 us (6%)
  matrix products  10.1 us (4%)
    all_to_all x4, blocking collectives, share(): return lax.all_to_all(copies, axis, 0, 0, axis_index_groups=groups)  78.4 us
    all_gather x1, blocking collectives, per_device(): lax.all_gather(codes, ('dp', 'tensor'), axis=0, tiled=False, axis_index_g...  38.5 us
    ppermute x3, waiting for transfers between devices, swap_hi(): return lax.ppermute(value, 'tensor', hi_pairs)  24.7 us
    all_to_all x1, waiting for transfers between devices, share(): return lax.all_to_all(copies, axis, 0, 0, axis_index_groups=groups)  24 us
    ppermute x3, starting transfers between devices, swap_hi(): return lax.ppermute(value, 'tensor', hi_pairs)  21.8 us
    mul x2, local copies, waits for them, and re-layouts, per_device(): weights = codes.astype(f32) * scales[:, :, :, None, :, None]  14.7 us
    dot_general x1, matrix products, per_device(): logits = jnp.dot(final, weight, preferred_element_type=f32)  7.94 us
    convert_element_type x1, other arithmetic, per_device(): weights = weights.astype(bf16).reshape(layers, 2, n_hi * share_width, rank)  7.36 us
  transfers between devices with their start and end apart: 6, of which 3 were waited for; matrix products, arithmetic and copies ran while one was open for 15% of the time, Pallas kernels for 0%

profile of v1, /device:TPU:6, one launch (start us, length us, event | category | flops | bytes accessed | tf_op | source)
XLA Modules:
  0.0 257.8 jit_solution(4288766517282194697)
XLA Ops:
  6.5 0.0 all-gather.2.cloned.1.call-start
  6.6 0.7 all-gather.2.cloned.1.call-update
  7.3 0.7 pad_maximum_fusion.2
  8.0 38.5 %all_gather.6 = bf16[16,32,512]{2,1,0:T(8,128)(2,1)S(1)} all-gather(bf16[1,32,512]{2,1,0:T(8,128)(2,1)S(1)} %bitcast.99), channel_id=1, replica_groups={{0,16,32,48,64,80,96,112,1,17,33,49,65,81,97,113},{2,18,34,50,66,82,98,..., dimensions={0}, use_global_device_ids=true | all-gather | bytes 557056 | tf_op jit(solution)/shard_map/layer_codes/all_gather | solution.py:92
  46.5 0.2 broadcast_in_dim.18
  46.7 32.6 %all_to_all.25 = bf16[4,512,512]{2,1,0:T(8,128)(2,1)S(1)} all-to-all(bf16[4,512,512]{2,1,0:T(8,128)(2,1)S(1)} %broadcast_in_dim.18), channel_id=1, replica_groups={{0,128,256,384},{8,136,264,392},{16,144,272,400},{24,152,280,408},{32,1..., dimensions={0} | all-to-all | bytes 4194304 | tf_op jit(solution)/shard_map/layer_codes/all_to_all | solution.py:37
  79.3 1.9 collective-permute-start.2
  81.2 0.0 copy-done.6
  81.2 0.0 copy-done.4
  81.2 0.1 reshape.104
  81.3 0.0 copy-done.5
  81.3 0.1 reshape.105
  81.4 0.1 concatenate.29
  81.5 9.0 %collective-permute-start.1 = (f32[1088]{0:T(1024)S(1)}, f32[1088]{0:T(1024)S(1)}, u32[]{:S(2)}, u32[]{:S(2)}) collective-permute-start(f32[1088]{0:T(1024)S(1)} %concatenate.29), channel_id=1, source_target_pairs={{0,1},{1,0},{2,3},{3,2},{4,5},{5,4},{6,7},{7,6},{8,9},{9,8},{10,11... | collective-permute-start | bytes 13064 | tf_op jit(solution)/shard_map/hidden_hi/ppermute | solution.py:41
  90.5 0.0 copy-done.1
  90.5 5.6 %collective-permute-start = (bf16[256,512]{1,0:T(8,128)(2,1)S(1)}, bf16[256,512]{1,0:T(8,128)(2,1)S(1)}, u32[]{:S(2)}, u32[]{:S(2)}) collective-permute-start(bf16[256,512]{1,0:T(8,128)(2,1)S(1)} %copy-done.1), channel_id=1, source_target_pairs={{0,1},{1,0},{2,3},{3,2},{4,5},{5,4},{6,7},{7,6},{8,9},{9,8},{10,11... | collective-permute-start | bytes 786440 | tf_op jit(solution)/shard_map/hidden_hi/ppermute | solution.py:41
  96.1 0.0 collective-permute-done.1
  96.1 0.1 fusion.50
  96.2 0.1 split.29
  96.3 0.1 split.31
  96.4 0.1 copy.44
  96.5 0.1 split.33
  96.6 0.1 split.35
  96.7 0.1 maximum_bitcast_fusion
  96.8 0.1 copy.45
  96.9 4.4 %mul.97 = f32[2,2,8,128,4,128]{5,4,3,2,1,0:T(4,128)} broadcast(f32[2,2,8,4]{3,2,1,0:T(8,128)S(1)} %copy.45), dimensions={0,1,2,4} | broadcast | bytes 8389120 | tf_op jit(solution)/shard_map/mul | solution.py:118
  101.2 10.3 %mul.98 = f32[2,2,1024,512]{3,2,1,0:T(8,128)} reshape(f32[2,2,8,128,4,128]{5,4,3,2,1,0:T(4,128)} %mul.97) | data formatting | bytes 16777216 | tf_op jit(solution)/shard_map/mul | solution.py:118
  111.6 18.4 %collective-permute-done = bf16[256,512]{1,0:T(8,128)(2,1)S(1)} collective-permute-done((bf16[256,512]{1,0:T(8,128)(2,1)S(1)}, bf16[256,512]{1,0:T(8,128)(2,1)S(1)}, u32[]{:S(2)}, u32[]{:S(2)}) %collective-permute-start) | collective-permute-done | bytes 262176 | tf_op jit(solution)/shard_map/hidden_hi/ppermute | solution.py:41
  130.0 0.2 fusion.9
  130.2 0.0 collective-permute-done.2
  130.2 1.9 broadcast_select_fusion.1
  132.1 0.5 convert_bitcast_fusion
  132.6 4.2 %copy.43 = f32[2,2,2,4,8,2,8,512]{7,6,5,4,3,2,1,0:T(8,128)} copy(f32[2,2,2,4,8,2,8,512]{7,6,1,0,4,2,3,5:T(8,128)S(1)} %convert_bitcast_fusion) | data formatting | bytes 16777216 | tf_op jit(solution)/shard_map/convert_element_type | solution.py:118
  136.9 7.4 %fusion.3 = bf16[2,2,1024,512]{3,2,1,0:T(8,128)(2,1)S(1)} fusion(f32[2,2,1024,512]{3,2,1,0:T(8,128)} %mul.98, f32[2,2,2,4,8,2,8,512]{7,6,5,4,3,2,1,0:T(8,128)} %copy.43), kind=kLoop, calls=%fused_computation.4 | loop fusion | flops 4194304 | bytes 20971520 | tf_op jit(solution)/shard_map/convert_element_type | solution.py:119
  144.2 0.4 convolution_convert_fusion.1
  144.7 0.1 broadcast_in_dim.19
  144.8 20.6 %all_to_all.26 = bf16[4,272,512]{2,1,0:T(8,128)(2,1)S(1)} all-to-all(bf16[4,272,512]{2,1,0:T(8,128)(2,1)S(1)} %broadcast_in_dim.19), channel_id=1, replica_groups={{0,2,4,6},{1,3,5,7},{8,10,12,14},{9,11,13,15},{16,18,20,22},{17,19,21,2..., dimensions={0} | all-to-all | bytes 2228224 | tf_op jit(solution)/shard_map/down/all_to_all | solution.py:37
  165.5 0.2 convert_reduce_fusion.1
  165.7 0.7 fusion.11
  166.4 0.5 convolution_convert_fusion
  166.9 0.1 broadcast_in_dim.20
  166.9 17.4 %all_to_all.27 = bf16[4,272,512]{2,1,0:T(8,128)(2,1)S(1)} all-to-all(bf16[4,272,512]{2,1,0:T(8,128)(2,1)S(1)} %broadcast_in_dim.20), channel_id=1, replica_groups={{0,2,4,6},{1,3,5,7},{8,10,12,14},{9,11,13,15},{16,18,20,22},{17,19,21,2..., dimensions={0} | all-to-all | bytes 2228224 | tf_op jit(solution)/shard_map/down/all_to_all | solution.py:37
  184.4 0.2 convert_reduce_fusion
  184.6 0.6 fusion.7
  185.2 0.0 copy-start.3
  185.2 0.2 copy.46
  185.4 0.0 copy-start.2
  185.4 1.5 broadcast_in_dim.21
  187.0 3.8 %all-to-all-start.3 = ((bf16[4,256,1024]{1,2,0:T(8,128)(2,1)}), bf16[4,256,1024]{1,2,0:T(8,128)(2,1)S(1)}, u32[]{:S(2)}, u32[]{:S(2)}) async-start(bf16[4,256,1024]{1,2,0:T(8,128)(2,1)} %broadcast_in_dim.21), calls=%async_computation.3 | async-start | bytes 4194304 | tf_op jit(solution)/shard_map/stream_y/all_to_all | solution.py:37
  190.8 0.0 copy-done.3
  190.8 0.1 copy.47
  190.9 24.0 %all-to-all-done.3 = bf16[4,256,1024]{1,2,0:T(8,128)(2,1)S(1)} async-done(((bf16[4,256,1024]{1,2,0:T(8,128)(2,1)}), bf16[4,256,1024]{1,2,0:T(8,128)(2,1)S(1)}, u32[]{:S(2)}, u32[]{:S(2)}) %all-to-all-start.3) | async-done | bytes 2097184 | tf_op jit(solution)/shard_map/stream_y/all_to_all | solution.py:37
  214.9 0.6 multiply_reduce_fusion
  215.4 0.0 copy-done.2
  215.4 1.8 fusion.5
  217.2 1.1 mul.114
  218.4 0.4 copy-done
  218.8 7.9 %fusion.52 = (f32[256]{0:T(256)S(1)}, f32[256,1024]{1,0:T(8,128)}) fusion(bf16[256,4096]{0,1:T(8,128)(2,1)S(1)} %copy-done, f32[512,8,8,128]{3,2,1,0:T(8,128)S(1)} %bitcast.95, bf16[4096,1024]{1,0:T(8,128)(2,1)} %all-gather.2.cloned.1.call-done), kind=kOutput, calls=%fused_computation.111 | convolution fusion | flops 2160328448 | bytes 28312576 | tf_op jit(solution)/shard_map/head/dot_general | solution.py:156
  226.7 0.0 copy-done.7
  226.7 1.6 exponential_reduce_fusion
  228.4 7.7 %all_to_all.28 = f32[4,3,256]{2,1,0:T(4,128)S(1)} all-to-all(f32[4,3,256]{2,1,0:T(4,128)S(1)} %broadcast_in_dim.23), channel_id=1, replica_groups={{0,2,4,6},{1,3,5,7},{8,10,12,14},{9,11,13,15},{16,18,20,22},{17,19,21,2..., dimensions={0} | all-to-all | bytes 24576 | tf_op jit(solution)/shard_map/stats/all_to_all | solution.py:37
  236.2 7.2 %collective-permute-start.3 = (f32[3,256]{1,0:T(4,128)S(1)}, f32[3,256]{1,0:T(4,128)S(1)}, u32[]{:S(2)}, u32[]{:S(2)}) collective-permute-start(f32[3,256]{1,0:T(4,128)S(1)} %get-tuple-element.27), channel_id=1, source_target_pairs={{0,1},{1,0},{2,3},{3,2},{4,5},{5,4},{6,7},{7,6},{8,9},{9,8},{10,11... | collective-permute-start | bytes 9224 | tf_op jit(solution)/shard_map/stats/ppermute | solution.py:41
  244.0 6.3 %collective-permute-done.3 = f32[3,256]{1,0:T(4,128)S(1)} collective-permute-done((f32[3,256]{1,0:T(4,128)S(1)}, f32[3,256]{1,0:T(4,128)S(1)}, u32[]{:S(2)}, u32[]{:S(2)}) %collective-permute-start.3) | collective-permute-done | bytes 3104 | tf_op jit(solution)/shard_map/stats/ppermute | solution.py:41
  250.4 0.6 compare_select_fusion
  (44 shorter events, 0.4 us)
Async XLA Ops:
  6.5 74.7 %copy-start.6 = (f32[2,512]{1,0:T(2,128)S(1)}, f32[2,512]{1,0:T(2,128)}, u32[]{:S(2)}) copy-start(f32[2,512]{1,0:T(2,128)} %param.14) | copy-start | bytes 12292
  6.5 74.7 %copy-start.4 = (f32[2,4,4]{2,1,0:T(4,128)S(1)}, f32[2,4,4]{2,1,0:T(4,128)}, u32[]{:S(2)}) copy-start(f32[2,4,4]{2,1,0:T(4,128)} %param.16) | copy-start | bytes 388
  6.5 74.8 %copy-start.5 = (f32[2,4,4]{2,1,0:T(4,128)S(1)}, f32[2,4,4]{2,1,0:T(4,128)}, u32[]{:S(2)}) copy-start(f32[2,4,4]{2,1,0:T(4,128)} %param.18) | copy-start | bytes 388
  6.5 83.9 %copy-start.1 = (bf16[256,512]{1,0:T(8,128)(2,1)S(1)}, bf16[256,512]{1,0:T(8,128)(2,1)}, u32[]{:S(2)}) copy-start(bf16[256,512]{1,0:T(8,128)(2,1)} %param.11) | copy-start | bytes 786436
  6.5 210.7 %all-gather.2.cloned.1.call-start = ((), (), s32[]{:S(2)}) async-start(), calls=%async_computation.5 | async-start | bytes 8519680 | tf_op jit(solution)/shard_map/head_rows/all_gather | solution.py:79
  79.3 50.9 %collective-permute-start.2 = (bf16[4,512,512]{2,1,0:T(8,128)(2,1)S(1)}, bf16[4,512,512]{2,1,0:T(8,128)(2,1)}, u32[]{:S(2)}, u32[]{:S(2)}) collective-permute-start(bf16[4,512,512]{2,1,0:T(8,128)(2,1)S(1)} %all_to_all.25), channel_id=1, source_target_pairs={{0,8},{8,0},{16,24},{24,16},{32,40},{40,32},{48,56},{56,48},{64,72... | collective-permute-start | bytes 6291464 | tf_op jit(solution)/shard_map/layer_codes/ppermute | solution.py:97
  81.5 14.6 %collective-permute-start.1 = (f32[1088]{0:T(1024)S(1)}, f32[1088]{0:T(1024)S(1)}, u32[]{:S(2)}, u32[]{:S(2)}) collective-permute-start(f32[1088]{0:T(1024)S(1)} %concatenate.29), channel_id=1, source_target_pairs={{0,1},{1,0},{2,3},{3,2},{4,5},{5,4},{6,7},{7,6},{8,9},{9,8},{10,11... | collective-permute-start | bytes 13064 | tf_op jit(solution)/shard_map/hidden_hi/ppermute | solution.py:41
  90.5 39.5 %collective-permute-start = (bf16[256,512]{1,0:T(8,128)(2,1)S(1)}, bf16[256,512]{1,0:T(8,128)(2,1)S(1)}, u32[]{:S(2)}, u32[]{:S(2)}) collective-permute-start(bf16[256,512]{1,0:T(8,128)(2,1)S(1)} %copy-done.1), channel_id=1, source_target_pairs={{0,1},{1,0},{2,3},{3,2},{4,5},{5,4},{6,7},{7,6},{8,9},{9,8},{10,11... | collective-permute-start | bytes 786440 | tf_op jit(solution)/shard_map/hidden_hi/ppermute | solution.py:41
  185.2 5.6 %copy-start.3 = (f32[32,8]{0,1:T(8,128)S(1)}, f32[32,8]{0,1:T(8,128)}, u32[]{:S(2)}) copy-start(f32[32,8]{0,1:T(8,128)} %param.21) | copy-start | bytes 3076
  185.4 30.0 %copy-start.2 = (f32[4096]{0:T(1024)S(1)}, f32[4096]{0:T(1024)}, u32[]{:S(2)}) copy-start(f32[4096]{0:T(1024)} %param.19) | copy-start | bytes 49156
  187.0 27.9 %all-to-all-start.3 = ((bf16[4,256,1024]{1,2,0:T(8,128)(2,1)}), bf16[4,256,1024]{1,2,0:T(8,128)(2,1)S(1)}, u32[]{:S(2)}, u32[]{:S(2)}) async-start(bf16[4,256,1024]{1,2,0:T(8,128)(2,1)} %broadcast_in_dim.21), calls=%async_computation.3 | async-start | bytes 4194304 | tf_op jit(solution)/shard_map/stream_y/all_to_all | solution.py:37
  217.2 1.6 copy-start
  218.8 7.9 %copy-start.7 = (s32[256]{0:T(256)S(1)}, s32[256]{0:T(256)}, u32[]{:S(2)}) copy-start(s32[256]{0:T(256)} %param.12) | copy-start | bytes 3076
  236.2 14.2 %collective-permute-start.3 = (f32[3,256]{1,0:T(4,128)S(1)}, f32[3,256]{1,0:T(4,128)S(1)}, u32[]{:S(2)}, u32[]{:S(2)}) collective-permute-start(f32[3,256]{1,0:T(4,128)S(1)} %get-tuple-element.27), channel_id=1, source_target_pairs={{0,1},{1,0},{2,3},{3,2},{4,5},{5,4},{6,7},{7,6},{8,9},{9,8},{10,11... | collective-permute-start | bytes 9224 | tf_op jit(solution)/shard_map/stats/ppermute | solution.py:41
Sparse Core Ops, SparseCore 0:
  9.5 154.7 all-gather.1

commit v2 on v0

v2 whole, which is shorter than its diff:
```python
import functools

import jax
import jax.numpy as jnp
from jax import lax
from jax.experimental import pallas as pl
from jax.experimental.pallas import tpu as pltpu
from jax.sharding import PartitionSpec as P

eps = 1e-06
tile_edge = 128
n_x, n_z, n_core = 4, 8, 2
n_y, n_hi = 4, 2
f32 = jnp.float32
bf16 = jnp.bfloat16
extra_rows = 16
mib = 1 << 20


def dp_of(x, z, c):
    return (x * n_z + z) * n_core + c


x_groups = [[dp_of(x, z, c) for x in range(n_x)] for z in range(n_z) for c in range(n_core)]
y_groups = [[y * n_hi + h for y in range(n_y)] for h in range(n_hi)]
z_groups = [
    [dp_of(x, z, c) * n_y * n_hi + y * n_hi + h for h in range(n_hi) for z in range(n_z)]
    for x in range(n_x)
    for c in range(n_core)
    for y in range(n_y)
]
core_pairs = [
    (dp_of(x, z, c), dp_of(x, z, 1 - c))
    for x in range(n_x)
    for z in range(n_z)
    for c in range(n_core)
]
hi_pairs = [(y * n_hi + h, y * n_hi + 1 - h) for y in range(n_y) for h in range(n_hi)]


def send_alike(copies, axis, groups):
    return lax.all_to_all(copies, axis, 0, 0, axis_index_groups=groups)


def share(block, axis, groups):
    return send_alike(jnp.broadcast_to(block[None], (len(groups[0]),) + block.shape), axis, groups)


def swap_hi(value):
    return lax.ppermute(value, "tensor", hi_pairs)


def swap_core(value):
    return lax.ppermute(value, "dp", core_pairs)


def in_pieces(value):
    high = lax.reduce_precision(value, 8, 7)
    middle = lax.reduce_precision(value - high, 8, 7)
    return jnp.stack([high, middle, value - high - middle]).astype(bf16)


def in_hi_order(own, peer, hi):
    return jnp.where(hi == 0, own, peer), jnp.where(hi == 0, peer, own)


def dot_nt(a, b):
    return lax.dot_general(a, b, (((1,), (1,)), ((), ())), preferred_element_type=f32)


def weight_rows(core, own_ref, other_ref, scale_ref, at, pair):
    blocks = []
    rank = scale_ref.shape[2]
    lanes = pl.ds(at * rank, rank)
    for block in (2 * pair, 2 * pair + 1):
        h, x = divmod(block, n_x)
        rows = pl.ds(h * tile_edge // n_core, tile_edge // n_core)
        own = own_ref[x, rows, lanes].astype(f32)
        other = other_ref[x, rows, lanes].astype(f32)
        zero = jnp.where(core == 0, own, other)
        one = jnp.where(core == 0, other, own)
        cols = own.shape[1]
        both = jnp.concatenate(
            [zero.reshape(n_z, 1, -1, cols), one.reshape(n_z, 1, -1, cols)], axis=1
        ).reshape(tile_edge, cols)
        blocks.append((both * scale_ref[at, pl.ds(block, 1), :]).astype(bf16))
    return jnp.concatenate(blocks, axis=0)


def down_block(stream_block, gain_block, weight):
    values = stream_block.astype(f32)
    part = jnp.dot((values * gain_block).astype(bf16), weight, preferred_element_type=f32)
    square = values * values
    high = square.astype(bf16)
    low = (square - high.astype(f32)).astype(bf16)
    ones = jnp.ones((extra_rows, square.shape[1]), bf16)
    return part, dot_nt(ones, high) + dot_nt(ones, low)


def write_part(out_ref, part, squares):
    tok = part.shape[0]
    high = squares.astype(bf16)
    low = (squares - high.astype(f32)).astype(bf16)
    main = part.astype(bf16)
    rest = jnp.concatenate([high, low], axis=1)
    for y in range(n_y):
        out_ref[y, pl.ds(0, tok), :] = main
        out_ref[y, pl.ds(tok, extra_rows), :] = rest


def read_act(parts_ref, model_width):
    tok = parts_ref.shape[1] - extra_rows
    latent = parts_ref[0, pl.ds(0, tok), :].astype(f32)
    for y in range(1, n_y):
        latent += parts_ref[y, pl.ds(0, tok), :].astype(f32)
    rows = jnp.concatenate(
        [
            parts_ref[y, pl.ds(tok, extra_rows), pl.ds(half * tok, tok)].astype(f32)
            for y in range(n_y)
            for half in range(2)
        ],
        axis=0,
    )
    columns = rows.T.astype(bf16)
    ones = jnp.full((rows.shape[0], latent.shape[1]), 1.0 / extra_rows, bf16)
    total = jnp.dot(columns, ones, preferred_element_type=f32)
    value = latent * lax.rsqrt(total / model_width + eps)
    return (value / (1.0 + jnp.exp(-value))).astype(bf16)


def first_kernel(core_ref, stream_ref, gain_ref, own_ref, other_ref, scale_ref, out_ref):
    core = core_ref[0]
    part, squares = None, None
    for pair in range(stream_ref.shape[1] // (2 * tile_edge)):
        cols = pl.ds(pair * 2 * tile_edge, 2 * tile_edge)
        weight = weight_rows(core, own_ref, other_ref, scale_ref, 0, pair)
        more, more_squares = down_block(stream_ref[:, cols], gain_ref[:, cols], weight)
        part = more if part is None else part + more
        squares = more_squares if squares is None else squares + more_squares
    write_part(out_ref, part, squares)


def middle_kernel(
    core_ref, parts_ref, stream_ref, gain_ref, own_ref, other_ref, scale_ref,
    next_ref, out_ref, *, model_width,
):
    core = core_ref[0]
    act = read_act(parts_ref, model_width)
    part, squares = None, None
    for pair in range(stream_ref.shape[1] // (2 * tile_edge)):
        cols = pl.ds(pair * 2 * tile_edge, 2 * tile_edge)
        up = weight_rows(core, own_ref, other_ref, scale_ref, 1, pair)
        block = (stream_ref[:, cols].astype(f32) + dot_nt(act, up)).astype(bf16)
        next_ref[:, cols] = block
        down = weight_rows(core, own_ref, other_ref, scale_ref, 2, pair)
        more, more_squares = down_block(block, gain_ref[:, cols], down)
        part = more if part is None else part + more
        squares = more_squares if squares is None else squares + more_squares
    write_part(out_ref, part, squares)


def last_kernel(
    core_ref, parts_ref, stream_ref, own_ref, other_ref, scale_ref, out_ref, *, model_width
):
    core = core_ref[0]
    act = read_act(parts_ref, model_width)
    for pair in range(stream_ref.shape[1] // (2 * tile_edge)):
        cols = pl.ds(pair * 2 * tile_edge, 2 * tile_edge)
        up = weight_rows(core, own_ref, other_ref, scale_ref, 3, pair)
        block = (stream_ref[:, cols].astype(f32) + dot_nt(act, up)).astype(bf16)
        for y in range(n_y):
            out_ref[y, :, cols] = block


def head_kernel(
    offset_ref, stream_ref, gain_ref, codes_ref, scale_ref, target_ref, out_ref,
    logits_ref, squares_ref, *, model_width,
):
    step = pl.program_id(0)

    @pl.when(step == 0)
    def _():
        logits_ref[...] = jnp.zeros_like(logits_ref)
        squares_ref[...] = jnp.zeros_like(squares_ref)

    rows = codes_ref.shape[0]
    tok = stream_ref.shape[1]
    vocab = codes_ref.shape[1]
    for part in range(rows // (2 * tile_edge)):
        cols = pl.ds(part * 2 * tile_edge, 2 * tile_edge)
        values = stream_ref[0, :, cols].astype(f32)
        squares_ref[...] += jnp.sum(values * values, axis=1, keepdims=True)
        final = (values * gain_ref[:, cols]).astype(bf16)
        weight = jnp.concatenate(
            [
                (
                    codes_ref[pl.ds(at * tile_edge, tile_edge), :].astype(f32)
                    * scale_ref[at : at + 1, :]
                ).astype(bf16)
                for at in (2 * part, 2 * part + 1)
            ],
            axis=0,
        )
        logits_ref[...] += jnp.dot(final, weight, preferred_element_type=f32)

    @pl.when(step == pl.num_programs(0) - 1)
    def _():
        inv = lax.rsqrt(squares_ref[...] / model_width + eps)
        logits = logits_ref[...] * inv
        columns = lax.broadcasted_iota(jnp.int32, logits.shape, 1) + offset_ref[0]
        picked = jnp.sum(jnp.where(columns == target_ref[...], logits, 0.0), axis=1, keepdims=True)
        top = jnp.max(logits, axis=1, keepdims=True)
        total = jnp.sum(jnp.exp(logits - top), axis=1, keepdims=True)
        lane = lax.broadcasted_iota(jnp.int32, (tok, 128), 1)
        stats = jnp.where(lane == 0, top, jnp.where(lane == 1, total, picked))
        out_ref[...] = stats.T[: out_ref.shape[0], :]


vmem = pl.BlockSpec(memory_space=pltpu.VMEM)
smem = pl.BlockSpec(memory_space=pltpu.SMEM)


def call(kernel, out_shapes, n_operands, flops, **static):
    return pl.pallas_call(
        functools.partial(kernel, **static),
        out_shape=out_shapes,
        in_specs=[smem] + [vmem] * n_operands,
        out_specs=jax.tree.map(lambda _: vmem, out_shapes),
        compiler_params=pltpu.CompilerParams(vmem_limit_bytes=32 * mib),
        cost_estimate=pl.CostEstimate(flops=flops, bytes_accessed=4 * mib, transcendentals=0),
    )


def per_device(
    hidden,
    targets,
    lengths,
    layer_gain,
    down_codes,
    down_scales,
    up_codes,
    up_scales,
    final_gain,
    head_codes,
    head_scales,
):
    tok, share_width = hidden.shape
    layers, rows, rank = down_codes.shape
    assert layers == 2 and rank == 2 * tok
    width = n_hi * share_width
    model_width = share_width * n_y * n_hi
    hi = lax.axis_index("tensor") % n_hi
    core = (lax.axis_index("dp") % n_core).reshape(1)
    local_vocab = head_codes.shape[1]

    with jax.named_scope("head_rows"):
        piece = lax.all_gather(head_codes, "dp", axis=0, tiled=True)

    together = lax.optimization_barrier

    with jax.named_scope("codes_z"):
        codes = jnp.concatenate(
            [down_codes[0], up_codes[0].T, down_codes[1], up_codes[1].T], axis=1
        )
        codes = lax.all_gather(
            codes, ("dp", "tensor"), axis=0, tiled=True, axis_index_groups=z_groups
        )
        hidden, layer_gain, down_scales, up_scales, codes = together(
            (hidden, layer_gain, down_scales, up_scales, codes)
        )

    with jax.named_scope("hidden_hi"):
        small = jnp.concatenate(
            [layer_gain.reshape(-1), down_scales.reshape(-1), up_scales.reshape(-1)]
        )
        small_rows = -(-small.size // rank)
        pieces = jnp.pad(in_pieces(small), ((0, 0), (0, small_rows * rank - small.size)))
        pieces = pieces.reshape(-1, rank)
        pieces = jnp.pad(pieces, ((0, -pieces.shape[0] % extra_rows), (0, 0)))
        peer = swap_hi(jnp.concatenate([hidden, pieces], axis=0))

    with jax.named_scope("codes_x"):
        codes = share(codes, "dp", x_groups)
        codes, peer = together((codes, peer))
        other = swap_core(codes)
        hidden_peer = peer[:tok]
        small_peer = peer[tok : tok + 3 * small_rows].astype(f32).reshape(3, -1).sum(axis=0)
        small_peer = small_peer[: small.size]

    with jax.named_scope("layer_scales"):
        def unpack(flat):
            gain, down, up = jnp.split(
                flat, [layer_gain.size, layer_gain.size + down_scales.size]
            )
            return (
                gain.reshape(layer_gain.shape),
                down.reshape(down_scales.shape),
                jnp.swapaxes(up.reshape(up_scales.shape), 1, 2),
            )

        flats = in_hi_order(small, small_peer, hi)
        (gain_a, down_a, up_a), (gain_b, down_b, up_b) = unpack(flats[0]), unpack(flats[1])
        gain = jnp.concatenate([gain_a, gain_b], axis=1)
        down_s = jnp.concatenate([down_a, down_b], axis=1)
        up_s = jnp.concatenate([up_a, up_b], axis=1)
        scales = jnp.stack([down_s[0], up_s[0], down_s[1], up_s[1]])
        scales = jnp.repeat(scales, tile_edge, axis=2)

    stream = jnp.concatenate(in_hi_order(hidden, hidden_peer, hi), axis=1)
    matmul = 2 * tok * width * rank
    parts_shape = jax.ShapeDtypeStruct((n_y, tok + extra_rows, rank), bf16)
    stream_shape = jax.ShapeDtypeStruct((tok, width), bf16)
    with jax.named_scope("down"):
        parts = call(first_kernel, parts_shape, 5, matmul)(
            core, stream, gain[0:1], codes, other, scales
        )
        parts = send_alike(parts, "tensor", y_groups)
    with jax.named_scope("up_down"):
        stream, parts = call(
            middle_kernel, (stream_shape, parts_shape), 6, 2 * matmul,
            model_width=model_width,
        )(core, parts, stream, gain[1:2], codes, other, scales)
        parts = send_alike(parts, "tensor", y_groups)
    with jax.named_scope("up"):
        stream = call(
            last_kernel, jax.ShapeDtypeStruct((n_y, tok, width), bf16), 5, matmul,
            model_width=model_width,
        )(core, parts, stream, codes, other, scales)
        stream = send_alike(stream, "tensor", y_groups)

    with jax.named_scope("head"):
        offset = (lax.axis_index("tensor") * local_vocab).reshape(1)
        block = 4 * tile_edge
        steps = model_width // block
        per_y = width // block
        stats = pl.pallas_call(
            functools.partial(head_kernel, model_width=model_width),
            out_shape=jax.ShapeDtypeStruct((8, tok), f32),
            grid=(steps,),
            in_specs=[
                smem,
                pl.BlockSpec((1, tok, block), lambda k: (k // per_y, 0, k % per_y)),
                pl.BlockSpec((1, block), lambda k: (0, k)),
                pl.BlockSpec((block, local_vocab), lambda k: (k, 0)),
                pl.BlockSpec((None, block // tile_edge, local_vocab), lambda k: (k, 0, 0)),
                pl.BlockSpec((tok, 1), lambda k: (0, 0)),
            ],
            out_specs=pl.BlockSpec((8, tok), lambda k: (0, 0)),
            scratch_shapes=[pltpu.VMEM((tok, local_vocab), f32), pltpu.VMEM((tok, 1), f32)],
            compiler_params=pltpu.CompilerParams(vmem_limit_bytes=32 * mib),
            cost_estimate=pl.CostEstimate(
                flops=2 * tok * model_width * local_vocab,
                bytes_accessed=2 * model_width * local_vocab,
                transcendentals=0,
            ),
        )(
            offset,
            stream,
            final_gain[None],
            piece,
            jnp.repeat(head_scales, tile_edge, axis=1).reshape(steps, -1, local_vocab),
            targets[:, None],
        )

    def merge(all_stats):
        tops, totals, picks = all_stats[:, 0], all_stats[:, 1], all_stats[:, 2]
        highest = jnp.max(tops, axis=0)
        total = jnp.sum(totals * jnp.exp(tops - highest), axis=0)
        return jnp.stack([highest, total, jnp.sum(picks, axis=0)])

    with jax.named_scope("stats"):
        mine = merge(share(stats[:3], "tensor", y_groups))
        top, total, picked = merge(jnp.stack([mine, swap_hi(mine)]))
        scored = picked - (top + jnp.log(total))
        position = lax.broadcasted_iota(jnp.int32, (tok,), 0)
        return jnp.where(position < lengths[0], scored, jnp.zeros_like(scored))


def solution(mesh):
    in_specs = (
        P("dp", "tensor"),
        P("dp"),
        P("dp"),
        P(None, "tensor"),
        P(None, ("tensor", "dp"), None),
        P(None, "tensor", None),
        P(None, None, ("tensor", "dp")),
        P(None, None, "tensor"),
        P(),
        P("dp", "tensor"),
        P(None, "tensor"),
    )
    out_specs = P("dp")
    return jax.shard_map(
        per_device, mesh=mesh, in_specs=in_specs, out_specs=out_specs, check_vma=False
    )
```

time: 936 us -> 210 us (0.22)
  blocking collectives: 601 us -> 84.6 us
  waiting for transfers between devices: 291 us -> 60.3 us
  starting transfers between devices: 0.13 us -> 26 us
  matrix products: 15.1 us -> 0 us
  Pallas kernels: 0 us -> 12.9 us
    all_gather x4 -> x1, blocking collectives: 446 us -> 38.5 us  [per_device(): lax.all_gather(codes, ('dp', 'tensor'), axis=0, tiled=True, axis_index_gr...]
    all_gather x1, waiting for transfers between devices: 121 us -> 0.01 us  [per_device(): piece = lax.all_gather(head_codes, 'dp', axis=0, tiled=True)]
    psum x3 -> x0, blocking collectives: 113 us -> none  [the longest x2 77.6 us: per_device(): squares = lax.psum(jnp.sum(stream_f * stream_f, axis=1), 'tensor')]
    all_gather x1 -> x0, waiting for transfers between devices: 106 us -> none  [per_device(): lax.all_gather(stream, 'tensor', axis=1, tiled=True).astype(jnp.float32)]
    psum x2 -> x0, waiting for transfers between devices: 62.8 us -> none  [per_device(): lax.psum(partial_value.astype(jnp.bfloat16), 'tensor').astype(jnp.float32)]
    all_to_all x0 -> x3, blocking collectives: none -> 46.1 us  [send_alike(): return lax.all_to_all(copies, axis, 0, 0, axis_index_groups=groups)]
    pmax x1 -> x0, blocking collectives: 41.8 us -> none  [per_device(): top = lax.pmax(local_top, 'tensor')]
    ppermute x0 -> x3, waiting for transfers between devices: none -> 35.1 us  [the longest x2 32.2 us: swap_hi(): return lax.ppermute(value, 'tensor', hi_pairs)]
  transfers between devices with their start and end apart: 4 -> 6, of which waited for: 3 -> 4; matrix products, arithmetic and copies ran while one was open for 0% -> 2% of each run, Pallas kernels for 0% -> 4%
where the time goes in v2:
time: 210 us; the launch traced here: 209 us
  blocking collectives  84.6 us (40%)
  waiting for transfers between devices  60.3 us (29%)
  starting transfers between devices  26 us (12%)
  between operations  14.3 us (7%)
  Pallas kernels  12.9 us (6%)
  local copies, waits for them, and re-layouts  9.57 us (5%)
    all_to_all x3, blocking collectives, send_alike(): return lax.all_to_all(copies, axis, 0, 0, axis_index_groups=groups)  46.1 us
    all_gather x1, blocking collectives, per_device(): lax.all_gather(codes, ('dp', 'tensor'), axis=0, tiled=True, axis_index_gr...  38.5 us
    ppermute x2, waiting for transfers between devices, swap_hi(): return lax.ppermute(value, 'tensor', hi_pairs)  32.2 us
    all_to_all x2, waiting for transfers between devices, send_alike(): return lax.all_to_all(copies, axis, 0, 0, axis_index_groups=groups)  24.5 us
    ppermute x2, starting transfers between devices, swap_hi(): return lax.ppermute(value, 'tensor', hi_pairs)  15.5 us
    all_to_all x2, starting transfers between devices, send_alike(): return lax.all_to_all(copies, axis, 0, 0, axis_index_groups=groups)  8.65 us
    unnamed x22, local copies, waits for them, and re-layouts  4.85 us
    pallas_call x1, Pallas kernels, per_device(): pl.pallas_call(functools.partial(head_kernel, model_width=model_width), o...  4.72 us
  transfers between devices with their start and end apart: 6, of which 4 were waited for; matrix products, arithmetic and copies ran while one was open for 2% of the time, Pallas kernels for 4%

profile of v2, /device:TPU:6, one launch (start us, length us, event | category | flops | bytes accessed | tf_op | source)
XLA Modules:
  0.0 208.7 jit_solution(13396000537919843122)
XLA Ops:
  6.5 0.0 all-gather.2.cloned.1.call-start
  6.5 0.7 all-gather.2.cloned.1.call-update
  7.3 0.7 slice_bitcast_fusion.3
  8.0 0.7 slice_bitcast_fusion.2
  8.7 38.5 %all_gather.6 = bf16[128,2048]{1,0:T(8,128)(2,1)S(1)} all-gather(bf16[8,2048]{1,0:T(8,128)(2,1)S(1)} %pad_maximum_fusion.1), channel_id=1, replica_groups={{0,16,32,48,64,80,96,112,1,17,33,49,65,81,97,113},{2,18,34,50,66,82,98,..., dimensions={0}, use_global_device_ids=true | all-gather | bytes 557056 | tf_op jit(solution)/shard_map/codes_z/all_gather | solution.py:265
  47.2 1.6 broadcast_in_dim.14
  48.8 0.0 copy-start.6
  48.8 0.0 copy-start.4
  48.8 0.0 copy-start.5
  48.8 0.0 copy-start.3
  48.8 4.9 %all-to-all-start = ((bf16[4,128,2048]{2,1,0:T(8,128)(2,1)}), bf16[4,128,2048]{2,1,0:T(8,128)(2,1)S(1)}, u32[]{:S(2)}, u32[]{:S(2)}) async-start(bf16[4,128,2048]{2,1,0:T(8,128)(2,1)} %broadcast_in_dim.14), calls=%async_computation | async-start | bytes 4194304 | tf_op jit(solution)/shard_map/codes_x/all_to_all | solution.py:42
  53.8 0.0 copy-done.6
  53.8 0.0 copy-done.4
  53.8 0.1 concatenate.55
  53.9 0.0 copy-done.5
  53.9 0.1 concatenate.56
  54.0 0.1 concatenate.57
  54.1 0.0 copy-done.3
  54.2 6.9 %collective-permute-start = (bf16[272,512]{1,0:T(8,128)(2,1)S(1)}, bf16[272,512]{1,0:T(8,128)(2,1)S(1)}, u32[]{:S(2)}, u32[]{:S(2)}) collective-permute-start(bf16[272,512]{1,0:T(8,128)(2,1)S(1)} %fusion.1), channel_id=1, source_target_pairs={{0,1},{1,0},{2,3},{3,2},{4,5},{5,4},{6,7},{7,6},{8,9},{9,8},{10,11... | collective-permute-start | bytes 835592 | tf_op jit(solution)/shard_map/hidden_hi/ppermute | solution.py:50
  61.1 27.3 %collective-permute-done = bf16[272,512]{1,0:T(8,128)(2,1)S(1)} collective-permute-done((bf16[272,512]{1,0:T(8,128)(2,1)S(1)}, bf16[272,512]{1,0:T(8,128)(2,1)S(1)}, u32[]{:S(2)}, u32[]{:S(2)}) %collective-permute-start) | collective-permute-done | bytes 278560 | tf_op jit(solution)/shard_map/hidden_hi/ppermute | solution.py:50
  88.3 0.0 all-to-all-done.own_ref
  88.3 1.9 collective-permute-start.1
  90.3 0.1 reshape.234
  90.4 0.1 reshape.235
  90.4 0.1 concatenate.60
  90.6 0.1 fusion.28
  90.7 0.1 split.29
  90.8 0.1 split.31
  90.9 0.1 split.35
  91.0 0.1 copy.32
  91.1 0.1 split.33
  91.1 0.1 copy.31
  91.3 0.1 copy.33
  91.5 0.1 pad_maximum_fusion.stream_ref
  91.6 0.1 broadcast_bitcast_fusion.scale_ref
  91.6 2.9 %collective-permute-done.1.other_ref = bf16[4,128,2048]{2,1,0:T(8,128)(2,1)} collective-permute-done((bf16[4,128,2048]{2,1,0:T(8,128)(2,1)S(1)}, bf16[4,128,2048]{2,1,0:T(8,128)(2,1)}, u32[]{:S(2)}, u32[]{:S(2)}) %collective-permute-start.1) | collective-permute-done | bytes 2097184 | tf_op jit(solution)/shard_map/codes_x/ppermute | solution.py:54
  94.5 2.3 %down.1 = bf16[4,272,512]{2,1,0:T(8,128)(2,1)S(1)} custom-call(s32[1]{0:T(128)} %bitcast.2.core_ref, bf16[256,1024]{1,0:T(8,128)(2,1)S(1)} %pad_maximum_fusion.stream_ref, f32[1,1024]{1,0:T(1,128)S(1)} %get-tuple-element.38.gain_ref, bf16[4,128,2048]{2,1,0:T(8,128)(2,1)S(1)} %all-to-all-done.own_ref, bf16[4,128,2048]{2,1,0:T(8,128)(2,1)} %collective-permute-done.1.other_ref, ...), custom_call_target="tpu_custom_call" | custom-call | flops 268435456 | bytes 4194304 | tf_op jit(solution)/shard_map/down/pallas_call | solution.py:314
  96.9 20.7 %all_to_all.25.parts_ref = bf16[4,272,512]{2,1,0:T(8,128)(2,1)S(1)} all-to-all(bf16[4,272,512]{2,1,0:T(8,128)(2,1)S(1)} %down.1), channel_id=1, replica_groups={{0,2,4,6},{1,3,5,7},{8,10,12,14},{9,11,13,15},{16,18,20,22},{17,19,21,2..., dimensions={0} | all-to-all | bytes 2228224 | tf_op jit(solution)/shard_map/down/all_to_all | solution.py:42
  117.6 3.3 %up_down.1 = (bf16[256,1024]{1,0:T(8,128)(2,1)S(1)}, bf16[4,272,512]{2,1,0:T(8,128)(2,1)S(1)}) custom-call(s32[1]{0:T(128)} %bitcast.2.core_ref, bf16[4,272,512]{2,1,0:T(8,128)(2,1)S(1)} %all_to_all.25.parts_ref, bf16[256,1024]{1,0:T(8,128)(2,1)S(1)} %pad_maximum_fusion.stream_ref, f32[1,1024]{1,0:T(1,128)S(1)} %get-tuple-element.37.gain_ref, ...), custom_call_target="tpu_custom_call" | custom-call | flops 536870912 | bytes 4194304 | tf_op jit(solution)/shard_map/up_down/pallas_call | solution.py:319
  120.9 17.7 %all_to_all.26.parts_ref = bf16[4,272,512]{2,1,0:T(8,128)(2,1)S(1)} all-to-all(bf16[4,272,512]{2,1,0:T(8,128)(2,1)S(1)} %get-tuple-element.21), channel_id=1, replica_groups={{0,2,4,6},{1,3,5,7},{8,10,12,14},{9,11,13,15},{16,18,20,22},{17,19,21,2..., dimensions={0} | all-to-all | bytes 2228224 | tf_op jit(solution)/shard_map/up_down/all_to_all | solution.py:42
  138.6 2.5 %up.1 = bf16[4,256,1024]{2,1,0:T(8,128)(2,1)S(1)} custom-call(s32[1]{0:T(128)} %bitcast.2.core_ref, bf16[4,272,512]{2,1,0:T(8,128)(2,1)S(1)} %all_to_all.26.parts_ref, bf16[256,1024]{1,0:T(8,128)(2,1)S(1)} %get-tuple-element.22.stream_ref, bf16[4,128,2048]{2,1,0:T(8,128)(2,1)S(1)} %all-to-all-done.own_ref, ...), custom_call_target="tpu_custom_call" | custom-call | flops 268435456 | bytes 4194304 | tf_op jit(solution)/shard_map/up/pallas_call | solution.py:325
  141.1 0.0 copy-start.1
  141.1 1.4 copy-done.1
  142.4 0.0 copy-start.7
  142.4 0.0 copy-start.8
  142.4 0.0 copy-start.2
  142.4 3.7 %all-to-all-start.3 = ((bf16[4,256,1024]{2,1,0:T(8,128)(2,1)}), bf16[4,256,1024]{2,1,0:T(8,128)(2,1)S(1)}, u32[]{:S(2)}, u32[]{:S(2)}) async-start(bf16[4,256,1024]{2,1,0:T(8,128)(2,1)} %copy-done.1), calls=%async_computation.3 | async-start | bytes 4194304 | tf_op jit(solution)/shard_map/up/all_to_all | solution.py:42
  146.2 0.0 copy-done.7
  146.2 0.1 copy.34
  146.3 0.1 broadcast_in_dim.32
  146.4 0.0 copy-done.8
  146.4 0.1 copy.35.target_ref
  146.6 24.5 %all-to-all-done.3.stream_ref = bf16[4,256,1024]{2,1,0:T(8,128)(2,1)S(1)} async-done(((bf16[4,256,1024]{2,1,0:T(8,128)(2,1)}), bf16[4,256,1024]{2,1,0:T(8,128)(2,1)S(1)}, u32[]{:S(2)}, u32[]{:S(2)}) %all-to-all-start.3) | async-done | bytes 2097184 | tf_op jit(solution)/shard_map/up/all_to_all | solution.py:42
  171.0 0.0 all-gather.2.cloned.1.call-done.codes_ref
  171.0 0.0 copy-done.2
  171.0 0.0 copy-start
  171.1 3.4 %copy-done = bf16[4096,1024]{1,0:T(8,128)(2,1)S(1)} copy-done((bf16[4096,1024]{1,0:T(8,128)(2,1)S(1)}, bf16[4096,1024]{1,0:T(8,128)(2,1)}, u32[]{:S(2)}) %copy-start) | copy-done | bytes 8388632
  174.4 4.7 %head.1 = f32[8,256]{1,0:T(8,128)S(1)} custom-call(s32[1]{0:T(128)} %bitcast.1.offset_ref, bf16[4,256,1024]{2,1,0:T(8,128)(2,1)S(1)} %all-to-all-done.3.stream_ref, f32[1,4096]{1,0:T(1,128)S(1)} %bitcast.56, bf16[4096,1024]{1,0:T(8,128)(2,1)S(1)} %copy-done, f32[8,4,1024]{2,1,0:T(4,128)S(1)} %reshape.241.scale_ref, s32[256,1]{1,0:T(8,128)S(1)} %copy.35.target_ref), custom_call_target="tpu_custom_call" | custom-call | flops 2147483648 | bytes 8388608 | tf_op jit(solution)/shard_map/head/pallas_call | solution.py:336
  179.2 7.7 %all_to_all.27 = f32[4,3,256]{2,1,0:T(4,128)S(1)} all-to-all(f32[4,3,256]{2,1,0:T(4,128)S(1)} %broadcast_in_dim.34), channel_id=1, replica_groups={{0,2,4,6},{1,3,5,7},{8,10,12,14},{9,11,13,15},{16,18,20,22},{17,19,21,2..., dimensions={0} | all-to-all | bytes 24576 | tf_op jit(solution)/shard_map/stats/all_to_all | solution.py:42
  187.0 8.6 %collective-permute-start.2 = (f32[3,256]{1,0:T(4,128)S(1)}, f32[3,256]{1,0:T(4,128)S(1)}, u32[]{:S(2)}, u32[]{:S(2)}) collective-permute-start(f32[3,256]{1,0:T(4,128)S(1)} %get-tuple-element.48), channel_id=1, source_target_pairs={{0,1},{1,0},{2,3},{3,2},{4,5},{5,4},{6,7},{7,6},{8,9},{9,8},{10,11... | collective-permute-start | bytes 9224 | tf_op jit(solution)/shard_map/stats/ppermute | solution.py:50
  196.2 5.0 %collective-permute-done.2 = f32[3,256]{1,0:T(4,128)S(1)} collective-permute-done((f32[3,256]{1,0:T(4,128)S(1)}, f32[3,256]{1,0:T(4,128)S(1)}, u32[]{:S(2)}, u32[]{:S(2)}) %collective-permute-start.2) | collective-permute-done | bytes 3104 | tf_op jit(solution)/shard_map/stats/ppermute | solution.py:50
  201.2 0.6 compare_select_fusion
  (32 shorter events, 0.4 us)
Async XLA Ops:
  6.5 164.5 %all-gather.2.cloned.1.call-start = ((), (), s32[]{:S(2)}) async-start(), calls=%async_computation.5 | async-start | bytes 8519680 | tf_op jit(solution)/shard_map/head_rows/all_gather | solution.py:257
  48.8 4.9 %copy-start.6 = (f32[2,512]{1,0:T(2,128)S(1)}, f32[2,512]{1,0:T(2,128)}, u32[]{:S(2)}) copy-start(f32[2,512]{1,0:T(2,128)} %param.14) | copy-start | bytes 12292
  48.8 4.9 %copy-start.4 = (f32[2,4,4]{2,1,0:T(4,128)S(1)}, f32[2,4,4]{2,1,0:T(4,128)}, u32[]{:S(2)}) copy-start(f32[2,4,4]{2,1,0:T(4,128)} %param.16) | copy-start | bytes 388
  48.8 5.0 %copy-start.5 = (f32[2,4,4]{2,1,0:T(4,128)S(1)}, f32[2,4,4]{2,1,0:T(4,128)}, u32[]{:S(2)}) copy-start(f32[2,4,4]{2,1,0:T(4,128)} %param.18) | copy-start | bytes 388
  48.8 5.3 %copy-start.3 = (bf16[256,512]{1,0:T(8,128)(2,1)S(1)}, bf16[256,512]{1,0:T(8,128)(2,1)}, u32[]{:S(2)}) copy-start(bf16[256,512]{1,0:T(8,128)(2,1)} %param.11) | copy-start | bytes 786436
  48.8 39.5 %all-to-all-start = ((bf16[4,128,2048]{2,1,0:T(8,128)(2,1)}), bf16[4,128,2048]{2,1,0:T(8,128)(2,1)S(1)}, u32[]{:S(2)}, u32[]{:S(2)}) async-start(bf16[4,128,2048]{2,1,0:T(8,128)(2,1)} %broadcast_in_dim.14), calls=%async_computation | async-start | bytes 4194304 | tf_op jit(solution)/shard_map/codes_x/all_to_all | solution.py:42
  54.2 34.2 %collective-permute-start = (bf16[272,512]{1,0:T(8,128)(2,1)S(1)}, bf16[272,512]{1,0:T(8,128)(2,1)S(1)}, u32[]{:S(2)}, u32[]{:S(2)}) collective-permute-start(bf16[272,512]{1,0:T(8,128)(2,1)S(1)} %fusion.1), channel_id=1, source_target_pairs={{0,1},{1,0},{2,3},{3,2},{4,5},{5,4},{6,7},{7,6},{8,9},{9,8},{10,11... | collective-permute-start | bytes 835592 | tf_op jit(solution)/shard_map/hidden_hi/ppermute | solution.py:50
  88.3 6.2 %collective-permute-start.1 = (bf16[4,128,2048]{2,1,0:T(8,128)(2,1)S(1)}, bf16[4,128,2048]{2,1,0:T(8,128)(2,1)}, u32[]{:S(2)}, u32[]{:S(2)}) collective-permute-start(bf16[4,128,2048]{2,1,0:T(8,128)(2,1)S(1)} %all-to-all-done.own_ref), channel_id=1, source_target_pairs={{0,8},{8,0},{16,24},{24,16},{32,40},{40,32},{48,56},{56,48},{64,72... | collective-permute-start | bytes 6291464 | tf_op jit(solution)/shard_map/codes_x/ppermute | solution.py:54
  141.1 1.4 copy-start.1
  142.4 3.8 %copy-start.7 = (f32[32,8]{0,1:T(8,128)S(1)}, f32[32,8]{0,1:T(8,128)}, u32[]{:S(2)}) copy-start(f32[32,8]{0,1:T(8,128)} %param.21) | copy-start | bytes 3076
  142.4 4.0 %copy-start.8 = (s32[256]{0:T(256)S(1)}, s32[256]{0:T(256)}, u32[]{:S(2)}) copy-start(s32[256]{0:T(256)} %param.12) | copy-start | bytes 3076
  142.4 28.6 %copy-start.2 = (f32[4096]{0:T(1024)S(1)}, f32[4096]{0:T(1024)}, u32[]{:S(2)}) copy-start(f32[4096]{0:T(1024)} %param.19) | copy-start | bytes 49156
  142.4 28.6 %all-to-all-start.3 = ((bf16[4,256,1024]{2,1,0:T(8,128)(2,1)}), bf16[4,256,1024]{2,1,0:T(8,128)(2,1)S(1)}, u32[]{:S(2)}, u32[]{:S(2)}) async-start(bf16[4,256,1024]{2,1,0:T(8,128)(2,1)} %copy-done.1), calls=%async_computation.3 | async-start | bytes 4194304 | tf_op jit(solution)/shard_map/up/all_to_all | solution.py:42
  171.0 3.4 %copy-start = (bf16[4096,1024]{1,0:T(8,128)(2,1)S(1)}, bf16[4096,1024]{1,0:T(8,128)(2,1)}, u32[]{:S(2)}) copy-start(bf16[4096,1024]{1,0:T(8,128)(2,1)} %all-gather.2.cloned.1.call-done.codes_ref) | copy-start | bytes 25165828
  187.0 14.2 %collective-permute-start.2 = (f32[3,256]{1,0:T(4,128)S(1)}, f32[3,256]{1,0:T(4,128)S(1)}, u32[]{:S(2)}, u32[]{:S(2)}) collective-permute-start(f32[3,256]{1,0:T(4,128)S(1)} %get-tuple-element.48), channel_id=1, source_target_pairs={{0,1},{1,0},{2,3},{3,2},{4,5},{5,4},{6,7},{7,6},{8,9},{9,8},{10,11... | collective-permute-start | bytes 9224 | tf_op jit(solution)/shard_map/stats/ppermute | solution.py:50
Sparse Core Ops, SparseCore 0:
  9.5 152.0 all-gather.1

commit v3 on v2

--- a/solution.py
+++ b/solution.py
@@ -68,27 +68,32 @@
     return lax.dot_general(a, b, (((1,), (1,)), ((), ())), preferred_element_type=f32)
 
 
-def weight_rows(core, own_ref, other_ref, scale_ref, at, pair):
+def weight_rows(core, own_ref, other_ref, scale_ref, pair):
     blocks = []
-    rank = scale_ref.shape[2]
-    lanes = pl.ds(at * rank, rank)
     for block in (2 * pair, 2 * pair + 1):
         h, x = divmod(block, n_x)
         rows = pl.ds(h * tile_edge // n_core, tile_edge // n_core)
-        own = own_ref[x, rows, lanes].astype(f32)
-        other = other_ref[x, rows, lanes].astype(f32)
+        own = own_ref[x, rows, :].astype(f32)
+        other = other_ref[x, rows, :].astype(f32)
         zero = jnp.where(core == 0, own, other)
         one = jnp.where(core == 0, other, own)
         cols = own.shape[1]
         both = jnp.concatenate(
             [zero.reshape(n_z, 1, -1, cols), one.reshape(n_z, 1, -1, cols)], axis=1
         ).reshape(tile_edge, cols)
-        blocks.append((both * scale_ref[at, pl.ds(block, 1), :]).astype(bf16))
+        blocks.append((both * scale_ref[0, pl.ds(block, 1), :]).astype(bf16))
     return jnp.concatenate(blocks, axis=0)
 
 
+def hidden_columns(hi, own_ref, peer_ref, pair):
+    h, part = divmod(pair, own_ref.shape[1] // (2 * tile_edge))
+    cols = pl.ds(part * 2 * tile_edge, 2 * tile_edge)
+    own, peer = own_ref[:, cols].astype(f32), peer_ref[:, cols].astype(f32)
+    return jnp.where(hi == h, own, peer)
+
+
 def down_block(stream_block, gain_block, weight):
-    values = stream_block.astype(f32)
+    values = stream_block
     part = jnp.dot((values * gain_block).astype(bf16), weight, preferred_element_type=f32)
     square = values * values
     high = square.astype(bf16)
@@ -128,106 +133,101 @@
     return (value / (1.0 + jnp.exp(-value))).astype(bf16)
 
 
-def first_kernel(core_ref, stream_ref, gain_ref, own_ref, other_ref, scale_ref, out_ref):
-    core = core_ref[0]
-    part, squares = None, None
-    for pair in range(stream_ref.shape[1] // (2 * tile_edge)):
+def first_kernel(
+    place_ref, hidden_ref, peer_ref, gain_ref, own_ref, other_ref, scale_ref, out_ref
+):
+    part, squares = 0.0, 0.0
+    for pair in range(n_hi * hidden_ref.shape[1] // (2 * tile_edge)):
         cols = pl.ds(pair * 2 * tile_edge, 2 * tile_edge)
-        weight = weight_rows(core, own_ref, other_ref, scale_ref, 0, pair)
-        more, more_squares = down_block(stream_ref[:, cols], gain_ref[:, cols], weight)
-        part = more if part is None else part + more
-        squares = more_squares if squares is None else squares + more_squares
+        weight = weight_rows(place_ref[0], own_ref, other_ref, scale_ref, pair)
+        block = hidden_columns(place_ref[1], hidden_ref, peer_ref, pair)
+        more, more_squares = down_block(block, gain_ref[:, cols], weight)
+        part, squares = part + more, squares + more_squares
     write_part(out_ref, part, squares)
 
 
 def middle_kernel(
-    core_ref, parts_ref, stream_ref, gain_ref, own_ref, other_ref, scale_ref,
+    place_ref, parts_ref, hidden_ref, peer_ref, gain_ref,
+    up_own_ref, up_other_ref, up_scale_ref, down_own_ref, down_other_ref, down_scale_ref,
     next_ref, out_ref, *, model_width,
 ):
-    core = core_ref[0]
     act = read_act(parts_ref, model_width)
-    part, squares = None, None
-    for pair in range(stream_ref.shape[1] // (2 * tile_edge)):
+    part, squares = 0.0, 0.0
+    for pair in range(n_hi * hidden_ref.shape[1] // (2 * tile_edge)):
         cols = pl.ds(pair * 2 * tile_edge, 2 * tile_edge)
-        up = weight_rows(core, own_ref, other_ref, scale_ref, 1, pair)
-        block = (stream_ref[:, cols].astype(f32) + dot_nt(act, up)).astype(bf16)
+        up = weight_rows(place_ref[0], up_own_ref, up_other_ref, up_scale_ref, pair)
+        block = hidden_columns(place_ref[1], hidden_ref, peer_ref, pair)
+        block = (block + dot_nt(act, up)).astype(bf16)
         next_ref[:, cols] = block
-        down = weight_rows(core, own_ref, other_ref, scale_ref, 2, pair)
-        more, more_squares = down_block(block, gain_ref[:, cols], down)
-        part = more if part is None else part + more
-        squares = more_squares if squares is None else squares + more_squares
+        down = weight_rows(place_ref[0], down_own_ref, down_other_ref, down_scale_ref, pair)
+        more, more_squares = down_block(block.astype(f32), gain_ref[:, cols], down)
+        part, squares = part + more, squares + more_squares
     write_part(out_ref, part, squares)
 
 
 def last_kernel(
-    core_ref, parts_ref, stream_ref, own_ref, other_ref, scale_ref, out_ref, *, model_width
+    place_ref, parts_ref, stream_ref, own_ref, other_ref, scale_ref, out_ref, *, model_width
 ):
-    core = core_ref[0]
     act = read_act(parts_ref, model_width)
     for pair in range(stream_ref.shape[1] // (2 * tile_edge)):
         cols = pl.ds(pair * 2 * tile_edge, 2 * tile_edge)
-        up = weight_rows(core, own_ref, other_ref, scale_ref, 3, pair)
+        up = weight_rows(place_ref[0], own_ref, other_ref, scale_ref, pair)
         block = (stream_ref[:, cols].astype(f32) + dot_nt(act, up)).astype(bf16)
         for y in range(n_y):
             out_ref[y, :, cols] = block
 
 
-def head_kernel(
-    offset_ref, stream_ref, gain_ref, codes_ref, scale_ref, target_ref, out_ref,
-    logits_ref, squares_ref, *, model_width,
-):
-    step = pl.program_id(0)
-
-    @pl.when(step == 0)
-    def _():
-        logits_ref[...] = jnp.zeros_like(logits_ref)
-        squares_ref[...] = jnp.zeros_like(squares_ref)
-
-    rows = codes_ref.shape[0]
-    tok = stream_ref.shape[1]
-    vocab = codes_ref.shape[1]
-    for part in range(rows // (2 * tile_edge)):
-        cols = pl.ds(part * 2 * tile_edge, 2 * tile_edge)
-        values = stream_ref[0, :, cols].astype(f32)
-        squares_ref[...] += jnp.sum(values * values, axis=1, keepdims=True)
-        final = (values * gain_ref[:, cols]).astype(bf16)
-        weight = jnp.concatenate(
-            [
-                (
-                    codes_ref[pl.ds(at * tile_edge, tile_edge), :].astype(f32)
-                    * scale_ref[at : at + 1, :]
-                ).astype(bf16)
-                for at in (2 * part, 2 * part + 1)
-            ],
-            axis=0,
-        )
-        logits_ref[...] += jnp.dot(final, weight, preferred_element_type=f32)
-
-    @pl.when(step == pl.num_programs(0) - 1)
-    def _():
-        inv = lax.rsqrt(squares_ref[...] / model_width + eps)
-        logits = logits_ref[...] * inv
-        columns = lax.broadcasted_iota(jnp.int32, logits.shape, 1) + offset_ref[0]
-        picked = jnp.sum(jnp.where(columns == target_ref[...], logits, 0.0), axis=1, keepdims=True)
-        top = jnp.max(logits, axis=1, keepdims=True)
-        total = jnp.sum(jnp.exp(logits - top), axis=1, keepdims=True)
-        lane = lax.broadcasted_iota(jnp.int32, (tok, 128), 1)
-        stats = jnp.where(lane == 0, top, jnp.where(lane == 1, total, picked))
-        out_ref[...] = stats.T[: out_ref.shape[0], :]
+def unpack_head_kernel(codes_ref, scale_ref, out_ref):
+    for at in range(codes_ref.shape[0] // tile_edge):
+        rows = pl.ds(at * tile_edge, tile_edge)
+        out_ref[rows, :] = (codes_ref[rows, :].astype(f32) * scale_ref[at : at + 1, :]).astype(bf16)
+
+
+chunk = 4 * tile_edge
+
+
+def chunks(width):
+    return [pl.ds(at * chunk, chunk) for at in range(width // chunk)]
+
+
+def head_kernel(offset_ref, stream_ref, gain_ref, weight_ref, target_ref, out_ref, *, model_width):
+    tok, width = stream_ref.shape[1:]
+    logits, squares = 0.0, 0.0
+    for y in range(n_y):
+        for cols in chunks(width):
+            values = stream_ref[y, :, cols].astype(f32)
+            squares = squares + jnp.sum(values * values, axis=1, keepdims=True)
+            rows = pl.ds(y * width + cols.start, chunk)
+            final = (values * gain_ref[:, rows]).astype(bf16)
+            logits = logits + jnp.dot(final, weight_ref[rows, :], preferred_element_type=f32)
+    logits = logits * lax.rsqrt(squares / model_width + eps)
+    columns = lax.broadcasted_iota(jnp.int32, logits.shape, 1) + offset_ref[0]
+    picked = jnp.sum(jnp.where(columns == target_ref[...], logits, 0.0), axis=1, keepdims=True)
+    top = jnp.max(logits, axis=1, keepdims=True)
+    total = jnp.sum(jnp.exp(logits - top), axis=1, keepdims=True)
+    lane = lax.broadcasted_iota(jnp.int32, (tok, 128), 1)
+    stats = jnp.where(lane == 0, top, jnp.where(lane == 1, total, picked))
+    out_ref[...] = stats.T[: out_ref.shape[0], :]
 
 
 vmem = pl.BlockSpec(memory_space=pltpu.VMEM)
 smem = pl.BlockSpec(memory_space=pltpu.SMEM)
 
 
-def call(kernel, out_shapes, n_operands, flops, **static):
+def matrix(at, rank):
+    codes = pl.BlockSpec((n_x, n_hi * tile_edge // n_core, rank), lambda i: (0, 0, at))
+    return [codes, codes, pl.BlockSpec((1, n_hi * n_x, rank), lambda i: (at, 0, 0))]
+
+
+def call(kernel, out_shapes, in_specs, flops, steps={"grid": (1,)}, **static):
     return pl.pallas_call(
         functools.partial(kernel, **static),
         out_shape=out_shapes,
-        in_specs=[smem] + [vmem] * n_operands,
+        in_specs=[smem] + in_specs,
         out_specs=jax.tree.map(lambda _: vmem, out_shapes),
         compiler_params=pltpu.CompilerParams(vmem_limit_bytes=32 * mib),
         cost_estimate=pl.CostEstimate(flops=flops, bytes_accessed=4 * mib, transcendentals=0),
+        **steps,
     )
 
 
@@ -306,61 +306,53 @@
         scales = jnp.stack([down_s[0], up_s[0], down_s[1], up_s[1]])
         scales = jnp.repeat(scales, tile_edge, axis=2)
 
-    stream = jnp.concatenate(in_hi_order(hidden, hidden_peer, hi), axis=1)
+    place = jnp.concatenate([core, hi.reshape(1)])
     matmul = 2 * tok * width * rank
     parts_shape = jax.ShapeDtypeStruct((n_y, tok + extra_rows, rank), bf16)
     stream_shape = jax.ShapeDtypeStruct((tok, width), bf16)
     with jax.named_scope("down"):
-        parts = call(first_kernel, parts_shape, 5, matmul)(
-            core, stream, gain[0:1], codes, other, scales
+        parts = call(first_kernel, parts_shape, [vmem] * 3 + matrix(0, rank), matmul)(
+            place, hidden, hidden_peer, gain[0:1], codes, other, scales
         )
         parts = send_alike(parts, "tensor", y_groups)
     with jax.named_scope("up_down"):
         stream, parts = call(
-            middle_kernel, (stream_shape, parts_shape), 6, 2 * matmul,
-            model_width=model_width,
-        )(core, parts, stream, gain[1:2], codes, other, scales)
+            middle_kernel, (stream_shape, parts_shape),
+            [vmem] * 4 + matrix(1, rank) + matrix(2, rank), 2 * matmul, model_width=model_width,
+        )(
+            place, parts, hidden, hidden_peer, gain[1:2],
+            codes, other, scales, codes, other, scales,
+        )
         parts = send_alike(parts, "tensor", y_groups)
     with jax.named_scope("up"):
         stream = call(
-            last_kernel, jax.ShapeDtypeStruct((n_y, tok, width), bf16), 5, matmul,
-            model_width=model_width,
-        )(core, parts, stream, codes, other, scales)
+            last_kernel, jax.ShapeDtypeStruct((n_y, tok, width), bf16),
+            [vmem] * 2 + matrix(3, rank), matmul, model_width=model_width,
+        )(place, parts, stream, codes, other, scales)
         stream = send_alike(stream, "tensor", y_groups)
 
     with jax.named_scope("head"):
         offset = (lax.axis_index("tensor") * local_vocab).reshape(1)
         block = 4 * tile_edge
         steps = model_width // block
-        per_y = width // block
-        stats = pl.pallas_call(
-            functools.partial(head_kernel, model_width=model_width),
-            out_shape=jax.ShapeDtypeStruct((8, tok), f32),
+        weight = pl.pallas_call(
+            unpack_head_kernel,
+            out_shape=jax.ShapeDtypeStruct(piece.shape, bf16),
             grid=(steps,),
             in_specs=[
-                smem,
-                pl.BlockSpec((1, tok, block), lambda k: (k // per_y, 0, k % per_y)),
-                pl.BlockSpec((1, block), lambda k: (0, k)),
                 pl.BlockSpec((block, local_vocab), lambda k: (k, 0)),
                 pl.BlockSpec((None, block // tile_edge, local_vocab), lambda k: (k, 0, 0)),
-                pl.BlockSpec((tok, 1), lambda k: (0, 0)),
             ],
-            out_specs=pl.BlockSpec((8, tok), lambda k: (0, 0)),
-            scratch_shapes=[pltpu.VMEM((tok, local_vocab), f32), pltpu.VMEM((tok, 1), f32)],
-            compiler_params=pltpu.CompilerParams(vmem_limit_bytes=32 * mib),
+            out_specs=pl.BlockSpec((block, local_vocab), lambda k: (k, 0)),
+            compiler_params=pltpu.CompilerParams(vmem_limit_bytes=58 * mib),
             cost_estimate=pl.CostEstimate(
-                flops=2 * tok * model_width * local_vocab,
-                bytes_accessed=2 * model_width * local_vocab,
-                transcendentals=0,
+                flops=piece.size, bytes_accessed=4 * piece.size, transcendentals=0
             ),
-        )(
-            offset,
-            stream,
-            final_gain[None],
-            piece,
-            jnp.repeat(head_scales, tile_edge, axis=1).reshape(steps, -1, local_vocab),
-            targets[:, None],
-        )
+        )(piece, jnp.repeat(head_scales, tile_edge, axis=1).reshape(steps, -1, local_vocab))
+        stats = call(
+            head_kernel, jax.ShapeDtypeStruct((8, tok), f32), [vmem] * 4, 2 * tok * model_width * local_vocab,
+            steps={}, model_width=model_width,
+        )(offset, stream, final_gain[None], weight, targets[:, None])
 
     def merge(all_stats):
         tops, totals, picks = all_stats[:, 0], all_stats[:, 1], all_stats[:, 2]

time: 210 us -> 210 us (level)
  waiting for transfers between devices: 60.3 us -> 51.1 us
  Pallas kernels: 12.9 us -> 18.9 us
    all_to_all x2, waiting for transfers between devices: 24.5 us -> 0.01 us  [send_alike(): return lax.all_to_all(copies, axis, 0, 0, axis_index_groups=groups)]
    all_gather x1, waiting for transfers between devices: 0.01 us -> 16 us  [per_device(): piece = lax.all_gather(head_codes, 'dp', axis=0, tiled=True)]
    pallas_call x4 -> x5, Pallas kernels: 12.9 us -> 18.9 us  [the longest x1 9.33 us: per_device(): pl.pallas_call(unpack_head_kernel, out_shape=jax.ShapeDtypeStruct(piece.s...]
  transfers between devices with their start and end apart: 6 -> 6, of which waited for: 4 -> 4; matrix products, arithmetic and copies ran while one was open for 2% -> 3% of each run, Pallas kernels for 4% -> 8%
where the time goes in v3:
time: 210 us; the launch traced here: 209 us
  blocking collectives  86.1 us (41%)
  waiting for transfers between devices  51.1 us (24%)
  starting transfers between devices  27.2 us (13%)
  Pallas kernels  18.9 us (9%)
  between operations  14.3 us (7%)
  local copies, waits for them, and re-layouts  10.2 us (5%)
    all_to_all x3, blocking collectives, send_alike(): return lax.all_to_all(copies, axis, 0, 0, axis_index_groups=groups)  47.6 us
    all_gather x1, blocking collectives, per_device(): lax.all_gather(codes, ('dp', 'tensor'), axis=0, tiled=True, axis_index_gr...  38.5 us
    ppermute x2, waiting for transfers between devices, swap_hi(): return lax.ppermute(value, 'tensor', hi_pairs)  31.4 us
    ppermute x2, starting transfers between devices, swap_hi(): return lax.ppermute(value, 'tensor', hi_pairs)  16.6 us
    all_gather x1, waiting for transfers between devices, per_device(): piece = lax.all_gather(head_codes, 'dp', axis=0, tiled=True)  16 us
    pallas_call x1, Pallas kernels, per_device(): pl.pallas_call(unpack_head_kernel, out_shape=jax.ShapeDtypeStruct(piece.s...  9.33 us
    all_to_all x2, starting transfers between devices, send_alike(): return lax.all_to_all(copies, axis, 0, 0, axis_index_groups=groups)  8.65 us
    unnamed x22, local copies, waits for them, and re-layouts  4.82 us
  transfers between devices with their start and end apart: 6, of which 4 were waited for; matrix products, arithmetic and copies ran while one was open for 3% of the time, Pallas kernels for 8%

profile of v3, /device:TPU:6, one launch (start us, length us, event | category | flops | bytes accessed | tf_op | source)
XLA Modules:
  0.0 208.7 jit_solution(11600295193473026021)
XLA Ops:
  6.5 0.0 all-gather.2.cloned.1.call-start
  6.5 0.7 all-gather.2.cloned.1.call-update
  7.3 0.7 slice_bitcast_fusion.3
  8.0 0.7 slice_bitcast_fusion.2
  8.7 38.5 %all_gather.6 = bf16[128,2048]{1,0:T(8,128)(2,1)S(1)} all-gather(bf16[8,2048]{1,0:T(8,128)(2,1)S(1)} %pad_maximum_fusion), channel_id=1, replica_groups={{0,16,32,48,64,80,96,112,1,17,33,49,65,81,97,113},{2,18,34,50,66,82,98,..., dimensions={0}, use_global_device_ids=true | all-gather | bytes 557056 | tf_op jit(solution)/shard_map/codes_z/all_gather | solution.py:265
  47.2 1.6 broadcast_in_dim.14
  48.8 0.0 copy-start.4
  48.8 0.0 copy-start.5
  48.8 0.0 copy-start.6
  48.8 0.0 copy-start.2
  48.8 4.9 %all-to-all-start = ((bf16[4,128,2048]{2,1,0:T(8,128)(2,1)}), bf16[4,128,2048]{2,1,0:T(8,128)(2,1)S(1)}, u32[]{:S(2)}, u32[]{:S(2)}) async-start(bf16[4,128,2048]{2,1,0:T(8,128)(2,1)} %broadcast_in_dim.14), calls=%async_computation | async-start | bytes 4194304 | tf_op jit(solution)/shard_map/codes_x/all_to_all | solution.py:42
  53.8 0.0 copy-done.4
  53.8 0.1 concatenate.56
  53.8 0.0 copy-done.5
  53.9 0.1 concatenate.57
  53.9 0.0 copy-done.6
  54.0 0.1 concatenate.58
  54.1 0.0 copy-done.2
  54.2 6.9 %collective-permute-start = (bf16[272,512]{1,0:T(8,128)(2,1)S(1)}, bf16[272,512]{1,0:T(8,128)(2,1)S(1)}, u32[]{:S(2)}, u32[]{:S(2)}) collective-permute-start(bf16[272,512]{1,0:T(8,128)(2,1)S(1)} %fusion.1), channel_id=1, source_target_pairs={{0,1},{1,0},{2,3},{3,2},{4,5},{5,4},{6,7},{7,6},{8,9},{9,8},{10,11... | collective-permute-start | bytes 835592 | tf_op jit(solution)/shard_map/hidden_hi/ppermute | solution.py:50
  61.1 27.6 %collective-permute-done = bf16[272,512]{1,0:T(8,128)(2,1)S(1)} collective-permute-done((bf16[272,512]{1,0:T(8,128)(2,1)S(1)}, bf16[272,512]{1,0:T(8,128)(2,1)S(1)}, u32[]{:S(2)}, u32[]{:S(2)}) %collective-permute-start) | collective-permute-done | bytes 278560 | tf_op jit(solution)/shard_map/hidden_hi/ppermute | solution.py:50
  88.7 0.0 all-to-all-done.own_ref.up_own_ref.down_own_ref
  88.7 1.9 collective-permute-start.1
  90.6 0.1 reshape.238
  90.7 0.1 reshape.239
  90.8 0.1 concatenate.60
  90.8 0.1 pad_add_fusion.place_ref
  91.1 0.1 fusion.28
  91.1 0.1 split.29
  91.2 0.1 split.31
  91.3 0.1 split.33
  91.4 0.1 copy.31
  91.5 0.1 split.35
  91.6 0.1 copy.32
  91.8 0.1 copy.33
  91.9 0.1 broadcast_bitcast_fusion.scale_ref.up_scale_ref.down_scale_ref
  91.9 2.9 %collective-permute-done.1.other_ref.up_other_ref.down_other_ref = bf16[4,128,2048]{2,1,0:T(8,128)(2,1)} collective-permute-done((bf16[4,128,2048]{2,1,0:T(8,128)(2,1)S(1)}, bf16[4,128,2048]{2,1,0:T(8,128)(2,1)}, u32[]{:S(2)}, u32[]{:S(2)}) %collective-permute-start.1) | collective-permute-done | bytes 2097184 | tf_op jit(solution)/shard_map/codes_x/ppermute | solution.py:54
  94.8 1.9 down.1
  96.7 20.3 %all_to_all.25.parts_ref = bf16[4,272,512]{2,1,0:T(8,128)(2,1)S(1)} all-to-all(bf16[4,272,512]{2,1,0:T(8,128)(2,1)S(1)} %down.1), channel_id=1, replica_groups={{0,2,4,6},{1,3,5,7},{8,10,12,14},{9,11,13,15},{16,18,20,22},{17,19,21,2..., dimensions={0} | all-to-all | bytes 2228224 | tf_op jit(solution)/shard_map/down/all_to_all | solution.py:42
  117.0 3.0 %up_down.1 = (bf16[256,1024]{1,0:T(8,128)(2,1)S(1)}, bf16[4,272,512]{2,1,0:T(8,128)(2,1)S(1)}) custom-call(s32[2]{0:T(128)S(1)} %pad_add_fusion.place_ref, bf16[4,272,512]{2,1,0:T(8,128)(2,1)S(1)} %all_to_all.25.parts_ref, bf16[256,512]{1,0:T(8,128)(2,1)S(1)} %copy-done.2, bf16[256,512]{1,0:T(8,128)(2,1)S(1)} %slice.86.peer_ref, ...), custom_call_target="tpu_custom_call" | custom-call | flops 536870912 | bytes 4194304 | tf_op jit(solution)/shard_map/up_down/pallas_call | solution.py:319
  120.0 17.7 %all_to_all.26.parts_ref = bf16[4,272,512]{2,1,0:T(8,128)(2,1)S(1)} all-to-all(bf16[4,272,512]{2,1,0:T(8,128)(2,1)S(1)} %get-tuple-element.21), channel_id=1, replica_groups={{0,2,4,6},{1,3,5,7},{8,10,12,14},{9,11,13,15},{16,18,20,22},{17,19,21,2..., dimensions={0} | all-to-all | bytes 2228224 | tf_op jit(solution)/shard_map/up_down/all_to_all | solution.py:42
  137.7 2.0 up.1
  139.7 0.0 copy-start.1
  139.7 1.3 copy-done.1
  141.0 0.0 copy-start.7
  141.0 0.0 copy-start.8
  141.0 3.7 %all-to-all-start.3 = ((bf16[4,256,1024]{2,1,0:T(8,128)(2,1)}), bf16[4,256,1024]{2,1,0:T(8,128)(2,1)S(1)}, u32[]{:S(2)}, u32[]{:S(2)}) async-start(bf16[4,256,1024]{2,1,0:T(8,128)(2,1)} %copy-done.1), calls=%async_computation.3 | async-start | bytes 4194304 | tf_op jit(solution)/shard_map/up/all_to_all | solution.py:42
  144.8 0.0 copy-done.7
  144.8 0.1 copy.34
  144.8 0.1 broadcast_in_dim.32
  144.9 0.7 reshape.245.scale_ref
  145.6 0.0 copy-done.8
  145.6 0.1 copy.35.target_ref
  145.8 0.0 copy-start.3
  145.8 16.0 %all-gather.2.cloned.1.call-done.codes_ref = bf16[4096,1024]{1,0:T(8,128)(2,1)} async-done(((bf16[64,1024]{1,0:T(8,128)(2,1)}), bf16[4096,1024]{1,0:T(8,128)(2,1)}) %all-gather.2.cloned.1.call-update) | async-done | bytes 8388624 | tf_op jit(solution)/shard_map/head_rows/all_gather | solution.py:257
  161.8 9.3 %head.2.weight_ref = bf16[4096,1024]{1,0:T(8,128)(2,1)} custom-call(bf16[4096,1024]{1,0:T(8,128)(2,1)} %all-gather.2.cloned.1.call-done.codes_ref, f32[8,4,1024]{2,1,0:T(4,128)} %reshape.245.scale_ref), custom_call_target="tpu_custom_call" | custom-call | flops 4194304 | bytes 16777216 | tf_op jit(solution)/shard_map/head/pallas_call | solution.py:338
  171.2 0.0 all-to-all-done.3.stream_ref
  171.2 0.0 copy-done.3
  171.2 0.0 copy-start
  171.2 3.4 %copy-done = bf16[4096,1024]{1,0:T(8,128)(2,1)S(1)} copy-done((bf16[4096,1024]{1,0:T(8,128)(2,1)S(1)}, bf16[4096,1024]{1,0:T(8,128)(2,1)}, u32[]{:S(2)}) %copy-start) | copy-done | bytes 8388632
  174.6 2.7 %head.3 = f32[8,256]{1,0:T(8,128)S(1)} custom-call(s32[1]{0:T(128)} %bitcast.1.offset_ref, bf16[4,256,1024]{2,1,0:T(8,128)(2,1)S(1)} %all-to-all-done.3.stream_ref, f32[1,4096]{1,0:T(1,128)S(1)} %bitcast.57, bf16[4096,1024]{1,0:T(8,128)(2,1)S(1)} %copy-done, s32[256,1]{1,0:T(8,128)S(1)} %copy.35.target_ref), custom_call_target="tpu_custom_call" | custom-call | flops 2147483648 | bytes 4194304 | tf_op jit(solution)/shard_map/head/pallas_call | solution.py:352
  177.3 9.6 %all_to_all.27 = f32[4,3,256]{2,1,0:T(4,128)S(1)} all-to-all(f32[4,3,256]{2,1,0:T(4,128)S(1)} %broadcast_in_dim.34), channel_id=1, replica_groups={{0,2,4,6},{1,3,5,7},{8,10,12,14},{9,11,13,15},{16,18,20,22},{17,19,21,2..., dimensions={0} | all-to-all | bytes 24576 | tf_op jit(solution)/shard_map/stats/all_to_all | solution.py:42
  187.0 9.7 %collective-permute-start.2 = (f32[3,256]{1,0:T(4,128)S(1)}, f32[3,256]{1,0:T(4,128)S(1)}, u32[]{:S(2)}, u32[]{:S(2)}) collective-permute-start(f32[3,256]{1,0:T(4,128)S(1)} %get-tuple-element.46), channel_id=1, source_target_pairs={{0,1},{1,0},{2,3},{3,2},{4,5},{5,4},{6,7},{7,6},{8,9},{9,8},{10,11... | collective-permute-start | bytes 9224 | tf_op jit(solution)/shard_map/stats/ppermute | solution.py:50
  197.3 3.8 %collective-permute-done.2 = f32[3,256]{1,0:T(4,128)S(1)} collective-permute-done((f32[3,256]{1,0:T(4,128)S(1)}, f32[3,256]{1,0:T(4,128)S(1)}, u32[]{:S(2)}, u32[]{:S(2)}) %collective-permute-start.2) | collective-permute-done | bytes 3104 | tf_op jit(solution)/shard_map/stats/ppermute | solution.py:50
  201.2 0.6 compare_select_fusion
  (31 shorter events, 0.4 us)
Async XLA Ops:
  6.5 155.3 %all-gather.2.cloned.1.call-start = ((), (), s32[]{:S(2)}) async-start(), calls=%async_computation.5 | async-start | bytes 8519680 | tf_op jit(solution)/shard_map/head_rows/all_gather | solution.py:257
  48.8 4.9 %copy-start.4 = (f32[2,4,4]{2,1,0:T(4,128)S(1)}, f32[2,4,4]{2,1,0:T(4,128)}, u32[]{:S(2)}) copy-start(f32[2,4,4]{2,1,0:T(4,128)} %param.16) | copy-start | bytes 388
  48.8 5.0 %copy-start.5 = (f32[2,4,4]{2,1,0:T(4,128)S(1)}, f32[2,4,4]{2,1,0:T(4,128)}, u32[]{:S(2)}) copy-start(f32[2,4,4]{2,1,0:T(4,128)} %param.18) | copy-start | bytes 388
  48.8 5.1 %copy-start.6 = (f32[2,512]{1,0:T(2,128)S(1)}, f32[2,512]{1,0:T(2,128)}, u32[]{:S(2)}) copy-start(f32[2,512]{1,0:T(2,128)} %param.14) | copy-start | bytes 12292
  48.8 5.3 %copy-start.2 = (bf16[256,512]{1,0:T(8,128)(2,1)S(1)}, bf16[256,512]{1,0:T(8,128)(2,1)}, u32[]{:S(2)}) copy-start(bf16[256,512]{1,0:T(8,128)(2,1)} %hidden_ref.1) | copy-start | bytes 786436
  48.8 39.8 %all-to-all-start = ((bf16[4,128,2048]{2,1,0:T(8,128)(2,1)}), bf16[4,128,2048]{2,1,0:T(8,128)(2,1)S(1)}, u32[]{:S(2)}, u32[]{:S(2)}) async-start(bf16[4,128,2048]{2,1,0:T(8,128)(2,1)} %broadcast_in_dim.14), calls=%async_computation | async-start | bytes 4194304 | tf_op jit(solution)/shard_map/codes_x/all_to_all | solution.py:42
  54.2 34.5 %collective-permute-start = (bf16[272,512]{1,0:T(8,128)(2,1)S(1)}, bf16[272,512]{1,0:T(8,128)(2,1)S(1)}, u32[]{:S(2)}, u32[]{:S(2)}) collective-permute-start(bf16[272,512]{1,0:T(8,128)(2,1)S(1)} %fusion.1), channel_id=1, source_target_pairs={{0,1},{1,0},{2,3},{3,2},{4,5},{5,4},{6,7},{7,6},{8,9},{9,8},{10,11... | collective-permute-start | bytes 835592 | tf_op jit(solution)/shard_map/hidden_hi/ppermute | solution.py:50
  88.7 6.2 %collective-permute-start.1 = (bf16[4,128,2048]{2,1,0:T(8,128)(2,1)S(1)}, bf16[4,128,2048]{2,1,0:T(8,128)(2,1)}, u32[]{:S(2)}, u32[]{:S(2)}) collective-permute-start(bf16[4,128,2048]{2,1,0:T(8,128)(2,1)S(1)} %all-to-all-done.own_ref.up_own_ref.down_own_ref), channel_id=1, source_target_pairs={{0,8},{8,0},{16,24},{24,16},{32,40},{40,32},{48,56},{56,48},{64,72... | collective-permute-start | bytes 6291464 | tf_op jit(solution)/shard_map/codes_x/ppermute | solution.py:54
  139.7 1.3 copy-start.1
  141.0 3.8 %copy-start.7 = (f32[32,8]{0,1:T(8,128)S(1)}, f32[32,8]{0,1:T(8,128)}, u32[]{:S(2)}) copy-start(f32[32,8]{0,1:T(8,128)} %param.21) | copy-start | bytes 3076
  141.0 4.6 %copy-start.8 = (s32[256]{0:T(256)S(1)}, s32[256]{0:T(256)}, u32[]{:S(2)}) copy-start(s32[256]{0:T(256)} %param.12) | copy-start | bytes 3076
  141.0 30.2 %all-to-all-start.3 = ((bf16[4,256,1024]{2,1,0:T(8,128)(2,1)}), bf16[4,256,1024]{2,1,0:T(8,128)(2,1)S(1)}, u32[]{:S(2)}, u32[]{:S(2)}) async-start(bf16[4,256,1024]{2,1,0:T(8,128)(2,1)} %copy-done.1), calls=%async_computation.3 | async-start | bytes 4194304 | tf_op jit(solution)/shard_map/up/all_to_all | solution.py:42
  145.8 25.4 %copy-start.3 = (f32[4096]{0:T(1024)S(1)}, f32[4096]{0:T(1024)}, u32[]{:S(2)}) copy-start(f32[4096]{0:T(1024)} %param.19) | copy-start | bytes 49156
  171.2 3.4 %copy-start = (bf16[4096,1024]{1,0:T(8,128)(2,1)S(1)}, bf16[4096,1024]{1,0:T(8,128)(2,1)}, u32[]{:S(2)}) copy-start(bf16[4096,1024]{1,0:T(8,128)(2,1)} %head.2.weight_ref) | copy-start | bytes 25165828
  187.0 14.2 %collective-permute-start.2 = (f32[3,256]{1,0:T(4,128)S(1)}, f32[3,256]{1,0:T(4,128)S(1)}, u32[]{:S(2)}, u32[]{:S(2)}) collective-permute-start(f32[3,256]{1,0:T(4,128)S(1)} %get-tuple-element.46), channel_id=1, source_target_pairs={{0,1},{1,0},{2,3},{3,2},{4,5},{5,4},{6,7},{7,6},{8,9},{9,8},{10,11... | collective-permute-start | bytes 9224 | tf_op jit(solution)/shard_map/stats/ppermute | solution.py:50
Sparse Core Ops, SparseCore 0:
  9.5 152.2 all-gather.1

commit v4 on v2

--- a/solution.py
+++ b/solution.py
@@ -68,27 +68,32 @@
     return lax.dot_general(a, b, (((1,), (1,)), ((), ())), preferred_element_type=f32)
 
 
-def weight_rows(core, own_ref, other_ref, scale_ref, at, pair):
+def weight_rows(core, own_ref, other_ref, scale_ref, pair):
     blocks = []
-    rank = scale_ref.shape[2]
-    lanes = pl.ds(at * rank, rank)
     for block in (2 * pair, 2 * pair + 1):
         h, x = divmod(block, n_x)
         rows = pl.ds(h * tile_edge // n_core, tile_edge // n_core)
-        own = own_ref[x, rows, lanes].astype(f32)
-        other = other_ref[x, rows, lanes].astype(f32)
+        own = own_ref[x, rows, :].astype(f32)
+        other = other_ref[x, rows, :].astype(f32)
         zero = jnp.where(core == 0, own, other)
         one = jnp.where(core == 0, other, own)
         cols = own.shape[1]
         both = jnp.concatenate(
             [zero.reshape(n_z, 1, -1, cols), one.reshape(n_z, 1, -1, cols)], axis=1
         ).reshape(tile_edge, cols)
-        blocks.append((both * scale_ref[at, pl.ds(block, 1), :]).astype(bf16))
+        blocks.append((both * scale_ref[0, pl.ds(block, 1), :]).astype(bf16))
     return jnp.concatenate(blocks, axis=0)
 
 
+def hidden_columns(hi, own_ref, peer_ref, pair):
+    h, part = divmod(pair, own_ref.shape[1] // (2 * tile_edge))
+    cols = pl.ds(part * 2 * tile_edge, 2 * tile_edge)
+    own, peer = own_ref[:, cols].astype(f32), peer_ref[:, cols].astype(f32)
+    return jnp.where(hi == h, own, peer)
+
+
 def down_block(stream_block, gain_block, weight):
-    values = stream_block.astype(f32)
+    values = stream_block
     part = jnp.dot((values * gain_block).astype(bf16), weight, preferred_element_type=f32)
     square = values * values
     high = square.astype(bf16)
@@ -128,45 +133,45 @@
     return (value / (1.0 + jnp.exp(-value))).astype(bf16)
 
 
-def first_kernel(core_ref, stream_ref, gain_ref, own_ref, other_ref, scale_ref, out_ref):
-    core = core_ref[0]
-    part, squares = None, None
-    for pair in range(stream_ref.shape[1] // (2 * tile_edge)):
+def first_kernel(
+    place_ref, hidden_ref, peer_ref, gain_ref, own_ref, other_ref, scale_ref, out_ref
+):
+    part, squares = 0.0, 0.0
+    for pair in range(n_hi * hidden_ref.shape[1] // (2 * tile_edge)):
         cols = pl.ds(pair * 2 * tile_edge, 2 * tile_edge)
-        weight = weight_rows(core, own_ref, other_ref, scale_ref, 0, pair)
-        more, more_squares = down_block(stream_ref[:, cols], gain_ref[:, cols], weight)
-        part = more if part is None else part + more
-        squares = more_squares if squares is None else squares + more_squares
+        weight = weight_rows(place_ref[0], own_ref, other_ref, scale_ref, pair)
+        block = hidden_columns(place_ref[1], hidden_ref, peer_ref, pair)
+        more, more_squares = down_block(block, gain_ref[:, cols], weight)
+        part, squares = part + more, squares + more_squares
     write_part(out_ref, part, squares)
 
 
 def middle_kernel(
-    core_ref, parts_ref, stream_ref, gain_ref, own_ref, other_ref, scale_ref,
+    place_ref, parts_ref, hidden_ref, peer_ref, gain_ref,
+    up_own_ref, up_other_ref, up_scale_ref, down_own_ref, down_other_ref, down_scale_ref,
     next_ref, out_ref, *, model_width,
 ):
-    core = core_ref[0]
     act = read_act(parts_ref, model_width)
-    part, squares = None, None
-    for pair in range(stream_ref.shape[1] // (2 * tile_edge)):
+    part, squares = 0.0, 0.0
+    for pair in range(n_hi * hidden_ref.shape[1] // (2 * tile_edge)):
         cols = pl.ds(pair * 2 * tile_edge, 2 * tile_edge)
-        up = weight_rows(core, own_ref, other_ref, scale_ref, 1, pair)
-        block = (stream_ref[:, cols].astype(f32) + dot_nt(act, up)).astype(bf16)
+        up = weight_rows(place_ref[0], up_own_ref, up_other_ref, up_scale_ref, pair)
+        block = hidden_columns(place_ref[1], hidden_ref, peer_ref, pair)
+        block = (block + dot_nt(act, up)).astype(bf16)
         next_ref[:, cols] = block
-        down = weight_rows(core, own_ref, other_ref, scale_ref, 2, pair)
-        more, more_squares = down_block(block, gain_ref[:, cols], down)
-        part = more if part is None else part + more
-        squares = more_squares if squares is None else squares + more_squares
+        down = weight_rows(place_ref[0], down_own_ref, down_other_ref, down_scale_ref, pair)
+        more, more_squares = down_block(block.astype(f32), gain_ref[:, cols], down)
+        part, squares = part + more, squares + more_squares
     write_part(out_ref, part, squares)
 
 
 def last_kernel(
-    core_ref, parts_ref, stream_ref, own_ref, other_ref, scale_ref, out_ref, *, model_width
+    place_ref, parts_ref, stream_ref, own_ref, other_ref, scale_ref, out_ref, *, model_width
 ):
-    core = core_ref[0]
     act = read_act(parts_ref, model_width)
     for pair in range(stream_ref.shape[1] // (2 * tile_edge)):
         cols = pl.ds(pair * 2 * tile_edge, 2 * tile_edge)
-        up = weight_rows(core, own_ref, other_ref, scale_ref, 3, pair)
+        up = weight_rows(place_ref[0], own_ref, other_ref, scale_ref, pair)
         block = (stream_ref[:, cols].astype(f32) + dot_nt(act, up)).astype(bf16)
         for y in range(n_y):
             out_ref[y, :, cols] = block
@@ -220,11 +225,17 @@
 smem = pl.BlockSpec(memory_space=pltpu.SMEM)
 
 
-def call(kernel, out_shapes, n_operands, flops, **static):
+def matrix(at, rank):
+    codes = pl.BlockSpec((n_x, n_hi * tile_edge // n_core, rank), lambda i: (0, 0, at))
+    return [codes, codes, pl.BlockSpec((1, n_hi * n_x, rank), lambda i: (at, 0, 0))]
+
+
+def call(kernel, out_shapes, in_specs, flops, **static):
     return pl.pallas_call(
         functools.partial(kernel, **static),
         out_shape=out_shapes,
-        in_specs=[smem] + [vmem] * n_operands,
+        grid=(1,),
+        in_specs=[smem] + in_specs,
         out_specs=jax.tree.map(lambda _: vmem, out_shapes),
         compiler_params=pltpu.CompilerParams(vmem_limit_bytes=32 * mib),
         cost_estimate=pl.CostEstimate(flops=flops, bytes_accessed=4 * mib, transcendentals=0),
@@ -306,26 +317,29 @@
         scales = jnp.stack([down_s[0], up_s[0], down_s[1], up_s[1]])
         scales = jnp.repeat(scales, tile_edge, axis=2)
 
-    stream = jnp.concatenate(in_hi_order(hidden, hidden_peer, hi), axis=1)
+    place = jnp.concatenate([core, hi.reshape(1)])
     matmul = 2 * tok * width * rank
     parts_shape = jax.ShapeDtypeStruct((n_y, tok + extra_rows, rank), bf16)
     stream_shape = jax.ShapeDtypeStruct((tok, width), bf16)
     with jax.named_scope("down"):
-        parts = call(first_kernel, parts_shape, 5, matmul)(
-            core, stream, gain[0:1], codes, other, scales
+        parts = call(first_kernel, parts_shape, [vmem] * 3 + matrix(0, rank), matmul)(
+            place, hidden, hidden_peer, gain[0:1], codes, other, scales
         )
         parts = send_alike(parts, "tensor", y_groups)
     with jax.named_scope("up_down"):
         stream, parts = call(
-            middle_kernel, (stream_shape, parts_shape), 6, 2 * matmul,
-            model_width=model_width,
-        )(core, parts, stream, gain[1:2], codes, other, scales)
+            middle_kernel, (stream_shape, parts_shape),
+            [vmem] * 4 + matrix(1, rank) + matrix(2, rank), 2 * matmul, model_width=model_width,
+        )(
+            place, parts, hidden, hidden_peer, gain[1:2],
+            codes, other, scales, codes, other, scales,
+        )
         parts = send_alike(parts, "tensor", y_groups)
     with jax.named_scope("up"):
         stream = call(
-            last_kernel, jax.ShapeDtypeStruct((n_y, tok, width), bf16), 5, matmul,
-            model_width=model_width,
-        )(core, parts, stream, codes, other, scales)
+            last_kernel, jax.ShapeDtypeStruct((n_y, tok, width), bf16),
+            [vmem] * 2 + matrix(3, rank), matmul, model_width=model_width,
+        )(place, parts, stream, codes, other, scales)
         stream = send_alike(stream, "tensor", y_groups)
 
     with jax.named_scope("head"):

time: 210 us -> 208 us (level)
  transfers between devices with their start and end apart: 6 -> 6, of which waited for: 4 -> 4; matrix products, arithmetic and copies ran while one was open for 2% -> 2% of each run, Pallas kernels for 4% -> 3%
where the time goes in v4:
time: 208 us; the launch traced here: 207 us
  blocking collectives  84.2 us (40%)
  waiting for transfers between devices  59.9 us (29%)
  starting transfers between devices  26.6 us (13%)
  between operations  14.3 us (7%)
  Pallas kernels  11.6 us (6%)
  local copies, waits for them, and re-layouts  9.6 us (5%)
    all_to_all x3, blocking collectives, send_alike(): return lax.all_to_all(copies, axis, 0, 0, axis_index_groups=groups)  45.7 us
    all_gather x1, blocking collectives, per_device(): lax.all_gather(codes, ('dp', 'tensor'), axis=0, tiled=True, axis_index_gr...  38.5 us
    ppermute x2, waiting for transfers between devices, swap_hi(): return lax.ppermute(value, 'tensor', hi_pairs)  31.8 us
    all_to_all x2, waiting for transfers between devices, send_alike(): return lax.all_to_all(copies, axis, 0, 0, axis_index_groups=groups)  24.4 us
    ppermute x2, starting transfers between devices, swap_hi(): return lax.ppermute(value, 'tensor', hi_pairs)  16 us
    all_to_all x2, starting transfers between devices, send_alike(): return lax.all_to_all(copies, axis, 0, 0, axis_index_groups=groups)  8.66 us
    unnamed x22, local copies, waits for them, and re-layouts  4.85 us
    pallas_call x1, Pallas kernels, per_device(): pl.pallas_call(functools.partial(head_kernel, model_width=model_width), o...  4.71 us
  transfers between devices with their start and end apart: 6, of which 4 were waited for; matrix products, arithmetic and copies ran while one was open for 2% of the time, Pallas kernels for 3%

profile of v4, /device:TPU:6, one launch (start us, length us, event | category | flops | bytes accessed | tf_op | source)
XLA Modules:
  0.0 207.1 jit_solution(12245594851895976885)
XLA Ops:
  6.5 0.0 all-gather.2.cloned.1.call-start
  6.5 0.7 all-gather.2.cloned.1.call-update
  7.3 0.7 slice_bitcast_fusion.3
  8.0 0.7 slice_bitcast_fusion.2
  8.7 38.5 %all_gather.6 = bf16[128,2048]{1,0:T(8,128)(2,1)S(1)} all-gather(bf16[8,2048]{1,0:T(8,128)(2,1)S(1)} %pad_maximum_fusion), channel_id=1, replica_groups={{0,16,32,48,64,80,96,112,1,17,33,49,65,81,97,113},{2,18,34,50,66,82,98,..., dimensions={0}, use_global_device_ids=true | all-gather | bytes 557056 | tf_op jit(solution)/shard_map/codes_z/all_gather | solution.py:276
  47.2 1.6 broadcast_in_dim.14
  48.8 0.0 copy-start.6
  48.8 0.0 copy-start.4
  48.8 0.0 copy-start.5
  48.8 0.0 copy-start.2
  48.8 4.9 %all-to-all-start = ((bf16[4,128,2048]{2,1,0:T(8,128)(2,1)}), bf16[4,128,2048]{2,1,0:T(8,128)(2,1)S(1)}, u32[]{:S(2)}, u32[]{:S(2)}) async-start(bf16[4,128,2048]{2,1,0:T(8,128)(2,1)} %broadcast_in_dim.14), calls=%async_computation | async-start | bytes 4194304 | tf_op jit(solution)/shard_map/codes_x/all_to_all | solution.py:42
  53.8 0.0 copy-done.6
  53.8 0.0 copy-done.4
  53.8 0.1 concatenate.56
  53.9 0.0 copy-done.5
  53.9 0.1 concatenate.57
  54.0 0.1 concatenate.58
  54.1 0.0 copy-done.2
  54.2 6.9 %collective-permute-start = (bf16[272,512]{1,0:T(8,128)(2,1)S(1)}, bf16[272,512]{1,0:T(8,128)(2,1)S(1)}, u32[]{:S(2)}, u32[]{:S(2)}) collective-permute-start(bf16[272,512]{1,0:T(8,128)(2,1)S(1)} %fusion.1), channel_id=1, source_target_pairs={{0,1},{1,0},{2,3},{3,2},{4,5},{5,4},{6,7},{7,6},{8,9},{9,8},{10,11... | collective-permute-start | bytes 835592 | tf_op jit(solution)/shard_map/hidden_hi/ppermute | solution.py:50
  61.1 27.3 %collective-permute-done = bf16[272,512]{1,0:T(8,128)(2,1)S(1)} collective-permute-done((bf16[272,512]{1,0:T(8,128)(2,1)S(1)}, bf16[272,512]{1,0:T(8,128)(2,1)S(1)}, u32[]{:S(2)}, u32[]{:S(2)}) %collective-permute-start) | collective-permute-done | bytes 278560 | tf_op jit(solution)/shard_map/hidden_hi/ppermute | solution.py:50
  88.4 0.0 all-to-all-done.own_ref.up_own_ref.down_own_ref
  88.4 1.9 collective-permute-start.1
  90.3 0.1 reshape.238
  90.4 0.1 reshape.239
  90.5 0.1 concatenate.60
  90.5 0.1 pad_add_fusion.place_ref
  90.8 0.1 fusion.28
  90.8 0.1 split.29
  90.9 0.1 split.31
  91.0 0.1 split.33
  91.1 0.1 copy.31
  91.2 0.1 split.35
  91.3 0.1 copy.32
  91.4 0.1 copy.33
  91.6 0.1 broadcast_bitcast_fusion.scale_ref.up_scale_ref.down_scale_ref
  91.6 3.1 %collective-permute-done.1.other_ref.up_other_ref.down_other_ref = bf16[4,128,2048]{2,1,0:T(8,128)(2,1)} collective-permute-done((bf16[4,128,2048]{2,1,0:T(8,128)(2,1)S(1)}, bf16[4,128,2048]{2,1,0:T(8,128)(2,1)}, u32[]{:S(2)}, u32[]{:S(2)}) %collective-permute-start.1) | collective-permute-done | bytes 2097184 | tf_op jit(solution)/shard_map/codes_x/ppermute | solution.py:54
  94.7 1.9 down.1
  96.6 20.4 %all_to_all.25.parts_ref = bf16[4,272,512]{2,1,0:T(8,128)(2,1)S(1)} all-to-all(bf16[4,272,512]{2,1,0:T(8,128)(2,1)S(1)} %down.1), channel_id=1, replica_groups={{0,2,4,6},{1,3,5,7},{8,10,12,14},{9,11,13,15},{16,18,20,22},{17,19,21,2..., dimensions={0} | all-to-all | bytes 2228224 | tf_op jit(solution)/shard_map/down/all_to_all | solution.py:42
  117.0 3.0 %up_down.1 = (bf16[256,1024]{1,0:T(8,128)(2,1)S(1)}, bf16[4,272,512]{2,1,0:T(8,128)(2,1)S(1)}) custom-call(s32[2]{0:T(128)S(1)} %pad_add_fusion.place_ref, bf16[4,272,512]{2,1,0:T(8,128)(2,1)S(1)} %all_to_all.25.parts_ref, bf16[256,512]{1,0:T(8,128)(2,1)S(1)} %copy-done.2, bf16[256,512]{1,0:T(8,128)(2,1)S(1)} %slice.86.peer_ref, ...), custom_call_target="tpu_custom_call" | custom-call | flops 536870912 | bytes 4194304 | tf_op jit(solution)/shard_map/up_down/pallas_call | solution.py:330
  120.0 17.6 %all_to_all.26.parts_ref = bf16[4,272,512]{2,1,0:T(8,128)(2,1)S(1)} all-to-all(bf16[4,272,512]{2,1,0:T(8,128)(2,1)S(1)} %get-tuple-element.21), channel_id=1, replica_groups={{0,2,4,6},{1,3,5,7},{8,10,12,14},{9,11,13,15},{16,18,20,22},{17,19,21,2..., dimensions={0} | all-to-all | bytes 2228224 | tf_op jit(solution)/shard_map/up_down/all_to_all | solution.py:42
  137.6 2.0 up.1
  139.6 0.0 copy-start.1
  139.6 1.4 copy-done.1
  140.9 0.0 copy-start.7
  140.9 0.0 copy-start.8
  141.0 0.0 copy-start.3
  141.0 3.7 %all-to-all-start.3 = ((bf16[4,256,1024]{2,1,0:T(8,128)(2,1)}), bf16[4,256,1024]{2,1,0:T(8,128)(2,1)S(1)}, u32[]{:S(2)}, u32[]{:S(2)}) async-start(bf16[4,256,1024]{2,1,0:T(8,128)(2,1)} %copy-done.1), calls=%async_computation.3 | async-start | bytes 4194304 | tf_op jit(solution)/shard_map/up/all_to_all | solution.py:42
  144.7 0.0 copy-done.7
  144.7 0.1 copy.34
  144.8 0.1 broadcast_in_dim.32
  145.0 0.0 copy-done.8
  145.0 0.1 copy.35.target_ref
  145.1 24.4 %all-to-all-done.3.stream_ref = bf16[4,256,1024]{2,1,0:T(8,128)(2,1)S(1)} async-done(((bf16[4,256,1024]{2,1,0:T(8,128)(2,1)}), bf16[4,256,1024]{2,1,0:T(8,128)(2,1)S(1)}, u32[]{:S(2)}, u32[]{:S(2)}) %all-to-all-start.3) | async-done | bytes 2097184 | tf_op jit(solution)/shard_map/up/all_to_all | solution.py:42
  169.5 0.0 all-gather.2.cloned.1.call-done.codes_ref
  169.5 0.0 copy-done.3
  169.5 0.0 copy-start
  169.5 3.4 %copy-done = bf16[4096,1024]{1,0:T(8,128)(2,1)S(1)} copy-done((bf16[4096,1024]{1,0:T(8,128)(2,1)S(1)}, bf16[4096,1024]{1,0:T(8,128)(2,1)}, u32[]{:S(2)}) %copy-start) | copy-done | bytes 8388632
  172.9 4.7 %head.1 = f32[8,256]{1,0:T(8,128)S(1)} custom-call(s32[1]{0:T(128)} %bitcast.1.offset_ref, bf16[4,256,1024]{2,1,0:T(8,128)(2,1)S(1)} %all-to-all-done.3.stream_ref, f32[1,4096]{1,0:T(1,128)S(1)} %bitcast.57, bf16[4096,1024]{1,0:T(8,128)(2,1)S(1)} %copy-done, f32[8,4,1024]{2,1,0:T(4,128)S(1)} %reshape.245.scale_ref, s32[256,1]{1,0:T(8,128)S(1)} %copy.35.target_ref), custom_call_target="tpu_custom_call" | custom-call | flops 2147483648 | bytes 8388608 | tf_op jit(solution)/shard_map/head/pallas_call | solution.py:350
  177.6 7.7 %all_to_all.27 = f32[4,3,256]{2,1,0:T(4,128)S(1)} all-to-all(f32[4,3,256]{2,1,0:T(4,128)S(1)} %broadcast_in_dim.34), channel_id=1, replica_groups={{0,2,4,6},{1,3,5,7},{8,10,12,14},{9,11,13,15},{16,18,20,22},{17,19,21,2..., dimensions={0} | all-to-all | bytes 24576 | tf_op jit(solution)/shard_map/stats/all_to_all | solution.py:42
  185.4 9.1 %collective-permute-start.2 = (f32[3,256]{1,0:T(4,128)S(1)}, f32[3,256]{1,0:T(4,128)S(1)}, u32[]{:S(2)}, u32[]{:S(2)}) collective-permute-start(f32[3,256]{1,0:T(4,128)S(1)} %get-tuple-element.46), channel_id=1, source_target_pairs={{0,1},{1,0},{2,3},{3,2},{4,5},{5,4},{6,7},{7,6},{8,9},{9,8},{10,11... | collective-permute-start | bytes 9224 | tf_op jit(solution)/shard_map/stats/ppermute | solution.py:50
  195.1 4.5 %collective-permute-done.2 = f32[3,256]{1,0:T(4,128)S(1)} collective-permute-done((f32[3,256]{1,0:T(4,128)S(1)}, f32[3,256]{1,0:T(4,128)S(1)}, u32[]{:S(2)}, u32[]{:S(2)}) %collective-permute-start.2) | collective-permute-done | bytes 3104 | tf_op jit(solution)/shard_map/stats/ppermute | solution.py:50
  199.7 0.6 compare_select_fusion
  (32 shorter events, 0.4 us)
Async XLA Ops:
  6.5 163.0 %all-gather.2.cloned.1.call-start = ((), (), s32[]{:S(2)}) async-start(), calls=%async_computation.5 | async-start | bytes 8519680 | tf_op jit(solution)/shard_map/head_rows/all_gather | solution.py:268
  48.8 4.9 %copy-start.6 = (f32[2,512]{1,0:T(2,128)S(1)}, f32[2,512]{1,0:T(2,128)}, u32[]{:S(2)}) copy-start(f32[2,512]{1,0:T(2,128)} %param.14) | copy-start | bytes 12292
  48.8 4.9 %copy-start.4 = (f32[2,4,4]{2,1,0:T(4,128)S(1)}, f32[2,4,4]{2,1,0:T(4,128)}, u32[]{:S(2)}) copy-start(f32[2,4,4]{2,1,0:T(4,128)} %param.16) | copy-start | bytes 388
  48.8 5.0 %copy-start.5 = (f32[2,4,4]{2,1,0:T(4,128)S(1)}, f32[2,4,4]{2,1,0:T(4,128)}, u32[]{:S(2)}) copy-start(f32[2,4,4]{2,1,0:T(4,128)} %param.18) | copy-start | bytes 388
  48.8 5.3 %copy-start.2 = (bf16[256,512]{1,0:T(8,128)(2,1)S(1)}, bf16[256,512]{1,0:T(8,128)(2,1)}, u32[]{:S(2)}) copy-start(bf16[256,512]{1,0:T(8,128)(2,1)} %hidden_ref.1) | copy-start | bytes 786436
  48.8 39.5 %all-to-all-start = ((bf16[4,128,2048]{2,1,0:T(8,128)(2,1)}), bf16[4,128,2048]{2,1,0:T(8,128)(2,1)S(1)}, u32[]{:S(2)}, u32[]{:S(2)}) async-start(bf16[4,128,2048]{2,1,0:T(8,128)(2,1)} %broadcast_in_dim.14), calls=%async_computation | async-start | bytes 4194304 | tf_op jit(solution)/shard_map/codes_x/all_to_all | solution.py:42
  54.2 34.2 %collective-permute-start = (bf16[272,512]{1,0:T(8,128)(2,1)S(1)}, bf16[272,512]{1,0:T(8,128)(2,1)S(1)}, u32[]{:S(2)}, u32[]{:S(2)}) collective-permute-start(bf16[272,512]{1,0:T(8,128)(2,1)S(1)} %fusion.1), channel_id=1, source_target_pairs={{0,1},{1,0},{2,3},{3,2},{4,5},{5,4},{6,7},{7,6},{8,9},{9,8},{10,11... | collective-permute-start | bytes 835592 | tf_op jit(solution)/shard_map/hidden_hi/ppermute | solution.py:50
  88.4 6.4 %collective-permute-start.1 = (bf16[4,128,2048]{2,1,0:T(8,128)(2,1)S(1)}, bf16[4,128,2048]{2,1,0:T(8,128)(2,1)}, u32[]{:S(2)}, u32[]{:S(2)}) collective-permute-start(bf16[4,128,2048]{2,1,0:T(8,128)(2,1)S(1)} %all-to-all-done.own_ref.up_own_ref.down_own_ref), channel_id=1, source_target_pairs={{0,8},{8,0},{16,24},{24,16},{32,40},{40,32},{48,56},{56,48},{64,72... | collective-permute-start | bytes 6291464 | tf_op jit(solution)/shard_map/codes_x/ppermute | solution.py:54
  139.6 1.4 copy-start.1
  140.9 3.8 %copy-start.7 = (f32[32,8]{0,1:T(8,128)S(1)}, f32[32,8]{0,1:T(8,128)}, u32[]{:S(2)}) copy-start(f32[32,8]{0,1:T(8,128)} %param.21) | copy-start | bytes 3076
  140.9 4.0 %copy-start.8 = (s32[256]{0:T(256)S(1)}, s32[256]{0:T(256)}, u32[]{:S(2)}) copy-start(s32[256]{0:T(256)} %param.12) | copy-start | bytes 3076
  141.0 28.5 %copy-start.3 = (f32[4096]{0:T(1024)S(1)}, f32[4096]{0:T(1024)}, u32[]{:S(2)}) copy-start(f32[4096]{0:T(1024)} %param.19) | copy-start | bytes 49156
  141.0 28.5 %all-to-all-start.3 = ((bf16[4,256,1024]{2,1,0:T(8,128)(2,1)}), bf16[4,256,1024]{2,1,0:T(8,128)(2,1)S(1)}, u32[]{:S(2)}, u32[]{:S(2)}) async-start(bf16[4,256,1024]{2,1,0:T(8,128)(2,1)} %copy-done.1), calls=%async_computation.3 | async-start | bytes 4194304 | tf_op jit(solution)/shard_map/up/all_to_all | solution.py:42
  169.5 3.4 %copy-start = (bf16[4096,1024]{1,0:T(8,128)(2,1)S(1)}, bf16[4096,1024]{1,0:T(8,128)(2,1)}, u32[]{:S(2)}) copy-start(bf16[4096,1024]{1,0:T(8,128)(2,1)} %all-gather.2.cloned.1.call-done.codes_ref) | copy-start | bytes 25165828
  185.4 14.2 %collective-permute-start.2 = (f32[3,256]{1,0:T(4,128)S(1)}, f32[3,256]{1,0:T(4,128)S(1)}, u32[]{:S(2)}, u32[]{:S(2)}) collective-permute-start(f32[3,256]{1,0:T(4,128)S(1)} %get-tuple-element.46), channel_id=1, source_target_pairs={{0,1},{1,0},{2,3},{3,2},{4,5},{5,4},{6,7},{7,6},{8,9},{9,8},{10,11... | collective-permute-start | bytes 9224 | tf_op jit(solution)/shard_map/stats/ppermute | solution.py:50
Sparse Core Ops, SparseCore 0:
  9.5 151.9 all-gather.1

commit v5 on v3

--- a/solution.py
+++ b/solution.py
@@ -52,12 +52,6 @@
 
 def swap_core(value):
     return lax.ppermute(value, "dp", core_pairs)
-
-
-def in_pieces(value):
-    high = lax.reduce_precision(value, 8, 7)
-    middle = lax.reduce_precision(value - high, 8, 7)
-    return jnp.stack([high, middle, value - high - middle]).astype(bf16)
 
 
 def in_hi_order(own, peer, hi):
@@ -177,29 +171,23 @@
             out_ref[y, :, cols] = block
 
 
-def unpack_head_kernel(codes_ref, scale_ref, out_ref):
-    for at in range(codes_ref.shape[0] // tile_edge):
-        rows = pl.ds(at * tile_edge, tile_edge)
-        out_ref[rows, :] = (codes_ref[rows, :].astype(f32) * scale_ref[at : at + 1, :]).astype(bf16)
-
-
-chunk = 4 * tile_edge
-
-
-def chunks(width):
-    return [pl.ds(at * chunk, chunk) for at in range(width // chunk)]
-
-
-def head_kernel(offset_ref, stream_ref, gain_ref, weight_ref, target_ref, out_ref, *, model_width):
-    tok, width = stream_ref.shape[1:]
+def head_kernel(
+    offset_ref, stream_ref, gain_ref, codes_ref, scale_ref, target_ref, out_ref, *, model_width
+):
+    n_blocks, tok, width = stream_ref.shape
+    chunk = 4 * tile_edge
     logits, squares = 0.0, 0.0
-    for y in range(n_y):
-        for cols in chunks(width):
-            values = stream_ref[y, :, cols].astype(f32)
-            squares = squares + jnp.sum(values * values, axis=1, keepdims=True)
-            rows = pl.ds(y * width + cols.start, chunk)
-            final = (values * gain_ref[:, rows]).astype(bf16)
-            logits = logits + jnp.dot(final, weight_ref[rows, :], preferred_element_type=f32)
+    for at in range(model_width // chunk):
+        block, part = divmod(at * chunk, width)
+        values = stream_ref[block, :, pl.ds(part, chunk)].astype(f32)
+        squares = squares + jnp.sum(values * values, axis=1, keepdims=True)
+        final = (values * gain_ref[:, pl.ds(at * chunk, chunk)]).astype(bf16)
+        weight = []
+        for tile in range(at * chunk // tile_edge, (at + 1) * chunk // tile_edge):
+            codes = codes_ref[pl.ds(tile * tile_edge, tile_edge), :].astype(f32)
+            weight.append((codes * scale_ref[tile : tile + 1, :]).astype(bf16))
+        weight = jnp.concatenate(weight, axis=0)
+        logits = logits + jnp.dot(final, weight, preferred_element_type=f32)
     logits = logits * lax.rsqrt(squares / model_width + eps)
     columns = lax.broadcasted_iota(jnp.int32, logits.shape, 1) + offset_ref[0]
     picked = jnp.sum(jnp.where(columns == target_ref[...], logits, 0.0), axis=1, keepdims=True)
@@ -219,15 +207,15 @@
     return [codes, codes, pl.BlockSpec((1, n_hi * n_x, rank), lambda i: (at, 0, 0))]
 
 
-def call(kernel, out_shapes, in_specs, flops, steps={"grid": (1,)}, **static):
+def call(kernel, out_shapes, in_specs, flops, **static):
     return pl.pallas_call(
         functools.partial(kernel, **static),
         out_shape=out_shapes,
+        grid=(1,),
         in_specs=[smem] + in_specs,
         out_specs=jax.tree.map(lambda _: vmem, out_shapes),
         compiler_params=pltpu.CompilerParams(vmem_limit_bytes=32 * mib),
         cost_estimate=pl.CostEstimate(flops=flops, bytes_accessed=4 * mib, transcendentals=0),
-        **steps,
     )
 
 
@@ -270,22 +258,16 @@
         )
 
     with jax.named_scope("hidden_hi"):
+        hidden_peer = swap_hi(hidden)
+
+    with jax.named_scope("codes_x"):
+        codes = share(codes, "dp", x_groups)
         small = jnp.concatenate(
             [layer_gain.reshape(-1), down_scales.reshape(-1), up_scales.reshape(-1)]
         )
-        small_rows = -(-small.size // rank)
-        pieces = jnp.pad(in_pieces(small), ((0, 0), (0, small_rows * rank - small.size)))
-        pieces = pieces.reshape(-1, rank)
-        pieces = jnp.pad(pieces, ((0, -pieces.shape[0] % extra_rows), (0, 0)))
-        peer = swap_hi(jnp.concatenate([hidden, pieces], axis=0))
-
-    with jax.named_scope("codes_x"):
-        codes = share(codes, "dp", x_groups)
-        codes, peer = together((codes, peer))
+        small_peer = swap_hi(small)
+        codes, hidden_peer, small_peer = together((codes, hidden_peer, small_peer))
         other = swap_core(codes)
-        hidden_peer = peer[:tok]
-        small_peer = peer[tok : tok + 3 * small_rows].astype(f32).reshape(3, -1).sum(axis=0)
-        small_peer = small_peer[: small.size]
 
     with jax.named_scope("layer_scales"):
         def unpack(flat):
@@ -333,26 +315,25 @@
 
     with jax.named_scope("head"):
         offset = (lax.axis_index("tensor") * local_vocab).reshape(1)
-        block = 4 * tile_edge
-        steps = model_width // block
-        weight = pl.pallas_call(
-            unpack_head_kernel,
-            out_shape=jax.ShapeDtypeStruct(piece.shape, bf16),
-            grid=(steps,),
-            in_specs=[
-                pl.BlockSpec((block, local_vocab), lambda k: (k, 0)),
-                pl.BlockSpec((None, block // tile_edge, local_vocab), lambda k: (k, 0, 0)),
-            ],
-            out_specs=pl.BlockSpec((block, local_vocab), lambda k: (k, 0)),
-            compiler_params=pltpu.CompilerParams(vmem_limit_bytes=58 * mib),
+        stats = pl.pallas_call(
+            functools.partial(head_kernel, model_width=model_width),
+            out_shape=jax.ShapeDtypeStruct((8, tok), f32),
+            in_specs=[smem] + [vmem] * 5,
+            out_specs=vmem,
+            compiler_params=pltpu.CompilerParams(vmem_limit_bytes=32 * mib),
             cost_estimate=pl.CostEstimate(
-                flops=piece.size, bytes_accessed=4 * piece.size, transcendentals=0
+                flops=2 * tok * model_width * local_vocab,
+                bytes_accessed=2 * model_width * local_vocab,
+                transcendentals=0,
             ),
-        )(piece, jnp.repeat(head_scales, tile_edge, axis=1).reshape(steps, -1, local_vocab))
-        stats = call(
-            head_kernel, jax.ShapeDtypeStruct((8, tok), f32), [vmem] * 4, 2 * tok * model_width * local_vocab,
-            steps={}, model_width=model_width,
-        )(offset, stream, final_gain[None], weight, targets[:, None])
+        )(
+            offset,
+            stream,
+            final_gain[None],
+            piece,
+            jnp.repeat(head_scales, tile_edge, axis=1),
+            targets[:, None],
+        )
 
     def merge(all_stats):
         tops, totals, picks = all_stats[:, 0], all_stats[:, 1], all_stats[:, 2]

time: 210 us -> 206 us (0.981)
  Pallas kernels: 18.9 us -> 9.75 us
  starting transfers between devices: 27.2 us -> 33.2 us
    all_to_all x2, waiting for transfers between devices: 0.01 us -> 24.5 us  [send_alike(): return lax.all_to_all(copies, axis, 0, 0, axis_index_groups=groups)]
    all_gather x1, waiting for transfers between devices: 16 us -> 0.01 us  [per_device(): piece = lax.all_gather(head_codes, 'dp', axis=0, tiled=True)]
    pallas_call x2 -> x1, Pallas kernels: 12 us -> 2.9 us  [per_device(): pl.pallas_call(functools.partial(head_kernel, model_width=model_width), o...]
    ppermute x2 -> x3, waiting for transfers between devices: 31.4 us -> 24.6 us  [swap_hi(): return lax.ppermute(value, 'tensor', hi_pairs)]
    ppermute x2 -> x3, starting transfers between devices: 16.6 us -> 22.7 us  [swap_hi(): return lax.ppermute(value, 'tensor', hi_pairs)]
  transfers between devices with their start and end apart: 6 -> 7, of which waited for: 4 -> 4; matrix products, arithmetic and copies ran while one was open for 3% -> 2% of each run, Pallas kernels for 8% -> 3%
where the time goes in v5:
time: 206 us; the launch traced here: 205 us
  blocking collectives  84.7 us (41%)
  waiting for transfers between devices  53 us (26%)
  starting transfers between devices  33.2 us (16%)
  between operations  14.3 us (7%)
  Pallas kernels  9.75 us (5%)
  local copies, waits for them, and re-layouts  9.25 us (4%)
    all_to_all x3, blocking collectives, send_alike(): return lax.all_to_all(copies, axis, 0, 0, axis_index_groups=groups)  46.2 us
    all_gather x1, blocking collectives, per_device(): lax.all_gather(codes, ('dp', 'tensor'), axis=0, tiled=True, axis_index_gr...  38.5 us
    ppermute x3, waiting for transfers between devices, swap_hi(): return lax.ppermute(value, 'tensor', hi_pairs)  24.6 us
    all_to_all x2, waiting for transfers between devices, send_alike(): return lax.all_to_all(copies, axis, 0, 0, axis_index_groups=groups)  24.5 us
    ppermute x3, starting transfers between devices, swap_hi(): return lax.ppermute(value, 'tensor', hi_pairs)  22.7 us
    all_to_all x2, starting transfers between devices, send_alike(): return lax.all_to_all(copies, axis, 0, 0, axis_index_groups=groups)  8.65 us
    unnamed x22, local copies, waits for them, and re-layouts  4.88 us
  transfers between devices with their start and end apart: 7, of which 4 were waited for; matrix products, arithmetic and copies ran while one was open for 2% of the time, Pallas kernels for 3%

profile of v5, /device:TPU:6, one launch (start us, length us, event | category | flops | bytes accessed | tf_op | source)
XLA Modules:
  0.0 205.1 jit_solution(4814562737171618979)
XLA Ops:
  6.5 0.0 all-gather.2.cloned.1.call-start
  6.5 0.7 all-gather.2.cloned.1.call-update
  7.3 0.7 slice_bitcast_fusion.3
  8.0 0.7 slice_bitcast_fusion.2
  8.7 38.5 %all_gather.6 = bf16[128,2048]{1,0:T(8,128)(2,1)S(1)} all-gather(bf16[8,2048]{1,0:T(8,128)(2,1)S(1)} %pad_maximum_fusion), channel_id=1, replica_groups={{0,16,32,48,64,80,96,112,1,17,33,49,65,81,97,113},{2,18,34,50,66,82,98,..., dimensions={0}, use_global_device_ids=true | all-gather | bytes 557056 | tf_op jit(solution)/shard_map/codes_z/all_gather | solution.py:253
  47.2 1.6 broadcast_in_dim.14
  48.8 0.0 copy-start.2
  48.8 0.0 copy-start.7
  48.8 0.0 copy-start.5
  48.8 0.0 copy-start.6
  48.9 4.9 %all-to-all-start = ((bf16[4,128,2048]{2,1,0:T(8,128)(2,1)}), bf16[4,128,2048]{2,1,0:T(8,128)(2,1)S(1)}, u32[]{:S(2)}, u32[]{:S(2)}) async-start(bf16[4,128,2048]{2,1,0:T(8,128)(2,1)} %broadcast_in_dim.14), calls=%async_computation | async-start | bytes 4194304 | tf_op jit(solution)/shard_map/codes_x/all_to_all | solution.py:42
  53.8 0.0 copy-done.2
  53.8 6.9 %collective-permute-start = (bf16[256,512]{1,0:T(8,128)(2,1)S(1)}, bf16[256,512]{1,0:T(8,128)(2,1)S(1)}, u32[]{:S(2)}, u32[]{:S(2)}) collective-permute-start(bf16[256,512]{1,0:T(8,128)(2,1)S(1)} %copy-done.2), channel_id=1, source_target_pairs={{0,1},{1,0},{2,3},{3,2},{4,5},{5,4},{6,7},{7,6},{8,9},{9,8},{10,11... | collective-permute-start | bytes 786440 | tf_op jit(solution)/shard_map/hidden_hi/ppermute | solution.py:50
  60.7 0.0 copy-done.7
  60.7 0.0 copy-done.5
  60.7 0.1 reshape.74
  60.8 0.0 copy-done.6
  60.8 0.1 reshape.75
  60.9 0.1 concatenate.20
  61.0 7.6 %collective-permute-start.1 = (f32[1088]{0:T(1024)S(1)}, f32[1088]{0:T(1024)S(1)}, u32[]{:S(2)}, u32[]{:S(2)}) collective-permute-start(f32[1088]{0:T(1024)S(1)} %concatenate.20), channel_id=1, source_target_pairs={{0,1},{1,0},{2,3},{3,2},{4,5},{5,4},{6,7},{7,6},{8,9},{9,8},{10,11... | collective-permute-start | bytes 13064 | tf_op jit(solution)/shard_map/codes_x/ppermute | solution.py:50
  68.6 19.1 %collective-permute-done.1 = f32[1088]{0:T(1024)S(1)} collective-permute-done((f32[1088]{0:T(1024)S(1)}, f32[1088]{0:T(1024)S(1)}, u32[]{:S(2)}, u32[]{:S(2)}) %collective-permute-start.1) | collective-permute-done | bytes 4384 | tf_op jit(solution)/shard_map/codes_x/ppermute | solution.py:50
  87.8 0.0 collective-permute-done.peer_ref
  87.8 0.0 all-to-all-done.own_ref.up_own_ref.down_own_ref
  87.8 1.9 collective-permute-start.2
  89.7 0.1 pad_add_fusion.place_ref
  89.8 0.1 fusion.20
  89.9 0.1 split.29
  89.9 0.1 split.31
  90.0 0.1 split.33
  90.1 0.1 copy.31
  90.2 0.1 split.35
  90.3 0.1 copy.32
  90.5 0.1 copy.33
  90.6 0.1 broadcast_bitcast_fusion.scale_ref.up_scale_ref.down_scale_ref
  90.7 3.3 %collective-permute-done.2.other_ref.up_other_ref.down_other_ref = bf16[4,128,2048]{2,1,0:T(8,128)(2,1)} collective-permute-done((bf16[4,128,2048]{2,1,0:T(8,128)(2,1)S(1)}, bf16[4,128,2048]{2,1,0:T(8,128)(2,1)}, u32[]{:S(2)}, u32[]{:S(2)}) %collective-permute-start.2) | collective-permute-done | bytes 2097184 | tf_op jit(solution)/shard_map/codes_x/ppermute | solution.py:54
  94.0 1.9 down.1
  95.9 20.8 %all_to_all.25.parts_ref = bf16[4,272,512]{2,1,0:T(8,128)(2,1)S(1)} all-to-all(bf16[4,272,512]{2,1,0:T(8,128)(2,1)S(1)} %down.1), channel_id=1, replica_groups={{0,2,4,6},{1,3,5,7},{8,10,12,14},{9,11,13,15},{16,18,20,22},{17,19,21,2..., dimensions={0} | all-to-all | bytes 2228224 | tf_op jit(solution)/shard_map/down/all_to_all | solution.py:42
  116.7 3.0 %up_down.1 = (bf16[256,1024]{1,0:T(8,128)(2,1)S(1)}, bf16[4,272,512]{2,1,0:T(8,128)(2,1)S(1)}) custom-call(s32[2]{0:T(128)S(1)} %pad_add_fusion.place_ref, bf16[4,272,512]{2,1,0:T(8,128)(2,1)S(1)} %all_to_all.25.parts_ref, bf16[256,512]{1,0:T(8,128)(2,1)S(1)} %copy-done.2, bf16[256,512]{1,0:T(8,128)(2,1)S(1)} %collective-permute-done.peer_ref, ...), custom_call_target="tpu_custom_call" | custom-call | flops 536870912 | bytes 4194304 | tf_op jit(solution)/shard_map/up_down/pallas_call | solution.py:301
  119.7 17.7 %all_to_all.26.parts_ref = bf16[4,272,512]{2,1,0:T(8,128)(2,1)S(1)} all-to-all(bf16[4,272,512]{2,1,0:T(8,128)(2,1)S(1)} %get-tuple-element.23), channel_id=1, replica_groups={{0,2,4,6},{1,3,5,7},{8,10,12,14},{9,11,13,15},{16,18,20,22},{17,19,21,2..., dimensions={0} | all-to-all | bytes 2228224 | tf_op jit(solution)/shard_map/up_down/all_to_all | solution.py:42
  137.4 2.0 up.1
  139.4 0.0 copy-start.1
  139.4 1.4 copy-done.1
  140.7 0.0 copy-start.4
  140.7 0.0 copy-start.8
  140.7 0.0 copy-start.3
  140.7 3.7 %all-to-all-start.3 = ((bf16[4,256,1024]{2,1,0:T(8,128)(2,1)}), bf16[4,256,1024]{2,1,0:T(8,128)(2,1)S(1)}, u32[]{:S(2)}, u32[]{:S(2)}) async-start(bf16[4,256,1024]{2,1,0:T(8,128)(2,1)} %copy-done.1), calls=%async_computation.3 | async-start | bytes 4194304 | tf_op jit(solution)/shard_map/up/all_to_all | solution.py:42
  144.5 0.0 copy-done.4
  144.5 0.1 copy.34
  144.6 0.1 broadcast_in_dim.32
  144.7 0.0 copy-done.8
  144.7 0.1 copy.35.target_ref
  144.9 24.5 %all-to-all-done.3.stream_ref = bf16[4,256,1024]{2,1,0:T(8,128)(2,1)S(1)} async-done(((bf16[4,256,1024]{2,1,0:T(8,128)(2,1)}), bf16[4,256,1024]{2,1,0:T(8,128)(2,1)S(1)}, u32[]{:S(2)}, u32[]{:S(2)}) %all-to-all-start.3) | async-done | bytes 2097184 | tf_op jit(solution)/shard_map/up/all_to_all | solution.py:42
  169.3 0.0 all-gather.2.cloned.1.call-done.codes_ref
  169.3 0.0 copy-done.3
  169.3 0.0 copy-start
  169.3 3.4 %copy-done = bf16[4096,1024]{1,0:T(8,128)(2,1)S(1)} copy-done((bf16[4096,1024]{1,0:T(8,128)(2,1)S(1)}, bf16[4096,1024]{1,0:T(8,128)(2,1)}, u32[]{:S(2)}) %copy-start) | copy-done | bytes 8388632
  172.7 2.9 %head.1 = f32[8,256]{1,0:T(8,128)S(1)} custom-call(s32[1]{0:T(128)} %bitcast.1.offset_ref, bf16[4,256,1024]{2,1,0:T(8,128)(2,1)S(1)} %all-to-all-done.3.stream_ref, f32[1,4096]{1,0:T(1,128)S(1)} %bitcast.59, bf16[4096,1024]{1,0:T(8,128)(2,1)S(1)} %copy-done, f32[32,1024]{1,0:T(8,128)S(1)} %bitcast.58, s32[256,1]{1,0:T(8,128)S(1)} %copy.35.target_ref), custom_call_target="tpu_custom_call" | custom-call | flops 2147483648 | bytes 8388608 | tf_op jit(solution)/shard_map/head/pallas_call | solution.py:318
  175.6 7.7 %all_to_all.27 = f32[4,3,256]{2,1,0:T(4,128)S(1)} all-to-all(f32[4,3,256]{2,1,0:T(4,128)S(1)} %broadcast_in_dim.34), channel_id=1, replica_groups={{0,2,4,6},{1,3,5,7},{8,10,12,14},{9,11,13,15},{16,18,20,22},{17,19,21,2..., dimensions={0} | all-to-all | bytes 24576 | tf_op jit(solution)/shard_map/stats/all_to_all | solution.py:42
  183.4 8.1 %collective-permute-start.3 = (f32[3,256]{1,0:T(4,128)S(1)}, f32[3,256]{1,0:T(4,128)S(1)}, u32[]{:S(2)}, u32[]{:S(2)}) collective-permute-start(f32[3,256]{1,0:T(4,128)S(1)} %get-tuple-element.45), channel_id=1, source_target_pairs={{0,1},{1,0},{2,3},{3,2},{4,5},{5,4},{6,7},{7,6},{8,9},{9,8},{10,11... | collective-permute-start | bytes 9224 | tf_op jit(solution)/shard_map/stats/ppermute | solution.py:50
  192.2 5.4 %collective-permute-done.3 = f32[3,256]{1,0:T(4,128)S(1)} collective-permute-done((f32[3,256]{1,0:T(4,128)S(1)}, f32[3,256]{1,0:T(4,128)S(1)}, u32[]{:S(2)}, u32[]{:S(2)}) %collective-permute-start.3) | collective-permute-done | bytes 3104 | tf_op jit(solution)/shard_map/stats/ppermute | solution.py:50
  197.7 0.6 compare_select_fusion
  (23 shorter events, 0.3 us)
Async XLA Ops:
  6.5 162.8 %all-gather.2.cloned.1.call-start = ((), (), s32[]{:S(2)}) async-start(), calls=%async_computation.5 | async-start | bytes 8519680 | tf_op jit(solution)/shard_map/head_rows/all_gather | solution.py:245
  48.8 4.9 %copy-start.2 = (bf16[256,512]{1,0:T(8,128)(2,1)S(1)}, bf16[256,512]{1,0:T(8,128)(2,1)}, u32[]{:S(2)}) copy-start(bf16[256,512]{1,0:T(8,128)(2,1)} %hidden_ref.1) | copy-start | bytes 786436
  48.8 11.8 %copy-start.7 = (f32[2,512]{1,0:T(2,128)S(1)}, f32[2,512]{1,0:T(2,128)}, u32[]{:S(2)}) copy-start(f32[2,512]{1,0:T(2,128)} %param.14) | copy-start | bytes 12292
  48.8 11.9 %copy-start.5 = (f32[2,4,4]{2,1,0:T(4,128)S(1)}, f32[2,4,4]{2,1,0:T(4,128)}, u32[]{:S(2)}) copy-start(f32[2,4,4]{2,1,0:T(4,128)} %param.16) | copy-start | bytes 388
  48.8 11.9 %copy-start.6 = (f32[2,4,4]{2,1,0:T(4,128)S(1)}, f32[2,4,4]{2,1,0:T(4,128)}, u32[]{:S(2)}) copy-start(f32[2,4,4]{2,1,0:T(4,128)} %param.18) | copy-start | bytes 388
  48.9 38.9 %all-to-all-start = ((bf16[4,128,2048]{2,1,0:T(8,128)(2,1)}), bf16[4,128,2048]{2,1,0:T(8,128)(2,1)S(1)}, u32[]{:S(2)}, u32[]{:S(2)}) async-start(bf16[4,128,2048]{2,1,0:T(8,128)(2,1)} %broadcast_in_dim.14), calls=%async_computation | async-start | bytes 4194304 | tf_op jit(solution)/shard_map/codes_x/all_to_all | solution.py:42
  53.8 34.0 %collective-permute-start = (bf16[256,512]{1,0:T(8,128)(2,1)S(1)}, bf16[256,512]{1,0:T(8,128)(2,1)S(1)}, u32[]{:S(2)}, u32[]{:S(2)}) collective-permute-start(bf16[256,512]{1,0:T(8,128)(2,1)S(1)} %copy-done.2), channel_id=1, source_target_pairs={{0,1},{1,0},{2,3},{3,2},{4,5},{5,4},{6,7},{7,6},{8,9},{9,8},{10,11... | collective-permute-start | bytes 786440 | tf_op jit(solution)/shard_map/hidden_hi/ppermute | solution.py:50
  61.0 26.8 %collective-permute-start.1 = (f32[1088]{0:T(1024)S(1)}, f32[1088]{0:T(1024)S(1)}, u32[]{:S(2)}, u32[]{:S(2)}) collective-permute-start(f32[1088]{0:T(1024)S(1)} %concatenate.20), channel_id=1, source_target_pairs={{0,1},{1,0},{2,3},{3,2},{4,5},{5,4},{6,7},{7,6},{8,9},{9,8},{10,11... | collective-permute-start | bytes 13064 | tf_op jit(solution)/shard_map/codes_x/ppermute | solution.py:50
  87.8 6.2 %collective-permute-start.2 = (bf16[4,128,2048]{2,1,0:T(8,128)(2,1)S(1)}, bf16[4,128,2048]{2,1,0:T(8,128)(2,1)}, u32[]{:S(2)}, u32[]{:S(2)}) collective-permute-start(bf16[4,128,2048]{2,1,0:T(8,128)(2,1)S(1)} %all-to-all-done.own_ref.up_own_ref.down_own_ref), channel_id=1, source_target_pairs={{0,8},{8,0},{16,24},{24,16},{32,40},{40,32},{48,56},{56,48},{64,72... | collective-permute-start | bytes 6291464 | tf_op jit(solution)/shard_map/codes_x/ppermute | solution.py:54
  139.4 1.4 copy-start.1
  140.7 3.8 %copy-start.4 = (f32[32,8]{0,1:T(8,128)S(1)}, f32[32,8]{0,1:T(8,128)}, u32[]{:S(2)}) copy-start(f32[32,8]{0,1:T(8,128)} %param.21) | copy-start | bytes 3076
  140.7 4.0 %copy-start.8 = (s32[256]{0:T(256)S(1)}, s32[256]{0:T(256)}, u32[]{:S(2)}) copy-start(s32[256]{0:T(256)} %param.12) | copy-start | bytes 3076
  140.7 28.6 %copy-start.3 = (f32[4096]{0:T(1024)S(1)}, f32[4096]{0:T(1024)}, u32[]{:S(2)}) copy-start(f32[4096]{0:T(1024)} %param.19) | copy-start | bytes 49156
  140.7 28.6 %all-to-all-start.3 = ((bf16[4,256,1024]{2,1,0:T(8,128)(2,1)}), bf16[4,256,1024]{2,1,0:T(8,128)(2,1)S(1)}, u32[]{:S(2)}, u32[]{:S(2)}) async-start(bf16[4,256,1024]{2,1,0:T(8,128)(2,1)} %copy-done.1), calls=%async_computation.3 | async-start | bytes 4194304 | tf_op jit(solution)/shard_map/up/all_to_all | solution.py:42
  169.3 3.4 %copy-start = (bf16[4096,1024]{1,0:T(8,128)(2,1)S(1)}, bf16[4096,1024]{1,0:T(8,128)(2,1)}, u32[]{:S(2)}) copy-start(bf16[4096,1024]{1,0:T(8,128)(2,1)} %all-gather.2.cloned.1.call-done.codes_ref) | copy-start | bytes 25165828
  183.4 14.2 %collective-permute-start.3 = (f32[3,256]{1,0:T(4,128)S(1)}, f32[3,256]{1,0:T(4,128)S(1)}, u32[]{:S(2)}, u32[]{:S(2)}) collective-permute-start(f32[3,256]{1,0:T(4,128)S(1)} %get-tuple-element.45), channel_id=1, source_target_pairs={{0,1},{1,0},{2,3},{3,2},{4,5},{5,4},{6,7},{7,6},{8,9},{9,8},{10,11... | collective-permute-start | bytes 9224 | tf_op jit(solution)/shard_map/stats/ppermute | solution.py:50
Sparse Core Ops, SparseCore 0:
  9.5 149.7 all-gather.1

commit v6 on v5

--- a/solution.py
+++ b/solution.py
@@ -190,7 +190,8 @@
         logits = logits + jnp.dot(final, weight, preferred_element_type=f32)
     logits = logits * lax.rsqrt(squares / model_width + eps)
     columns = lax.broadcasted_iota(jnp.int32, logits.shape, 1) + offset_ref[0]
-    picked = jnp.sum(jnp.where(columns == target_ref[...], logits, 0.0), axis=1, keepdims=True)
+    target = jnp.broadcast_to(target_ref[...].astype(f32), (128, tok)).T[:, :1].astype(jnp.int32)
+    picked = jnp.sum(jnp.where(columns == target, logits, 0.0), axis=1, keepdims=True)
     top = jnp.max(logits, axis=1, keepdims=True)
     total = jnp.sum(jnp.exp(logits - top), axis=1, keepdims=True)
     lane = lax.broadcasted_iota(jnp.int32, (tok, 128), 1)
@@ -247,9 +248,8 @@
     together = lax.optimization_barrier
 
     with jax.named_scope("codes_z"):
-        codes = jnp.concatenate(
-            [down_codes[0], up_codes[0].T, down_codes[1], up_codes[1].T], axis=1
-        )
+        codes = jnp.stack([down_codes, jnp.swapaxes(up_codes, 1, 2)], axis=1)
+        codes = codes.reshape(-1, rank)
         codes = lax.all_gather(
             codes, ("dp", "tensor"), axis=0, tiled=True, axis_index_groups=z_groups
         )
@@ -261,12 +261,19 @@
         hidden_peer = swap_hi(hidden)
 
     with jax.named_scope("codes_x"):
-        codes = share(codes, "dp", x_groups)
+        codes = codes.reshape(n_hi * n_z, 2 * layers, rows, rank).swapaxes(1, 2)
+        codes = share(codes.reshape(-1, 2 * layers * rank), "dp", x_groups)
         small = jnp.concatenate(
             [layer_gain.reshape(-1), down_scales.reshape(-1), up_scales.reshape(-1)]
         )
         small_peer = swap_hi(small)
-        codes, hidden_peer, small_peer = together((codes, hidden_peer, small_peer))
+        target_row = targets[None]
+        head_rows = jnp.repeat(head_scales, tile_edge, axis=1)
+        offset = (lax.axis_index("tensor") * local_vocab).reshape(1)
+        final_row = final_gain[None]
+        codes, hidden_peer, small_peer, target_row, head_rows, offset, final_row = together(
+            (codes, hidden_peer, small_peer, target_row, head_rows, offset, final_row)
+        )
         other = swap_core(codes)
 
     with jax.named_scope("layer_scales"):
@@ -314,7 +321,6 @@
         stream = send_alike(stream, "tensor", y_groups)
 
     with jax.named_scope("head"):
-        offset = (lax.axis_index("tensor") * local_vocab).reshape(1)
         stats = pl.pallas_call(
             functools.partial(head_kernel, model_width=model_width),
             out_shape=jax.ShapeDtypeStruct((8, tok), f32),
@@ -329,10 +335,10 @@
         )(
             offset,
             stream,
-            final_gain[None],
+            final_row,
             piece,
-            jnp.repeat(head_scales, tile_edge, axis=1),
-            targets[:, None],
+            head_rows,
+            target_row,
         )
 
     def merge(all_stats):

time: 206 us -> 202 us (0.981)
  blocking collectives: 84.7 us -> 113 us
  waiting for transfers between devices: 53 us -> 27.9 us
  starting transfers between devices: 33.2 us -> 28.7 us
  local copies, waits for them, and re-layouts: 9.25 us -> 6.32 us
    all_to_all x3 -> x4, blocking collectives: 46.2 us -> 74.6 us  [send_alike(): return lax.all_to_all(copies, axis, 0, 0, axis_index_groups=groups)]
    all_to_all x2 -> x1, waiting for transfers between devices: 24.5 us -> 0.01 us  [send_alike(): return lax.all_to_all(copies, axis, 0, 0, axis_index_groups=groups)]
    all_to_all x2 -> x1, starting transfers between devices: 8.65 us -> 4.91 us  [send_alike(): return lax.all_to_all(copies, axis, 0, 0, axis_index_groups=groups)]
    unnamed x22 -> x20, local copies, waits for them, and re-layouts: 4.88 us -> 3.52 us
  transfers between devices with their start and end apart: 7 -> 6, of which waited for: 4 -> 3; matrix products, arithmetic and copies ran while one was open for 2% -> 2% of each run, Pallas kernels for 3% -> 3%
where the time goes in v6:
time: 202 us
  blocking collectives  113 us (56%)
  starting transfers between devices  28.7 us (14%)
  waiting for transfers between devices  27.9 us (14%)
  between operations  14.3 us (7%)
  Pallas kernels  9.77 us (5%)
  local copies, waits for them, and re-layouts  6.32 us (3%)
    all_to_all x4, blocking collectives, send_alike(): return lax.all_to_all(copies, axis, 0, 0, axis_index_groups=groups)  74.6 us
    all_gather x1, blocking collectives, per_device(): lax.all_gather(codes, ('dp', 'tensor'), axis=0, tiled=True, axis_index_gr...  38.5 us
    ppermute x3, waiting for transfers between devices, swap_hi(): return lax.ppermute(value, 'tensor', hi_pairs)  23.8 us
    ppermute x3, starting transfers between devices, swap_hi(): return lax.ppermute(value, 'tensor', hi_pairs)  21.8 us
    all_to_all x1, starting transfers between devices, send_alike(): return lax.all_to_all(copies, axis, 0, 0, axis_index_groups=groups)  4.91 us
  transfers between devices with their start and end apart: 6, of which 3 were waited for; matrix products, arithmetic and copies ran while one was open for 2% of the time, Pallas kernels for 3%

profile of v6, /device:TPU:6, one launch (start us, length us, event | category | flops | bytes accessed | tf_op | source)
XLA Modules:
  0.0 201.6 jit_solution(18057901743649761595)
XLA Ops:
  6.5 0.0 all-gather.2.cloned.1.call-start
  6.5 0.7 all-gather.2.cloned.1.call-update
  7.3 0.7 pad_maximum_fusion
  8.0 38.5 %all_gather.6 = bf16[512,512]{1,0:T(8,128)(2,1)S(1)} all-gather(bf16[32,512]{1,0:T(8,128)(2,1)S(1)} %bitcast.61), channel_id=1, replica_groups={{0,16,32,48,64,80,96,112,1,17,33,49,65,81,97,113},{2,18,34,50,66,82,98,..., dimensions={0}, use_global_device_ids=true | all-gather | bytes 557056 | tf_op jit(solution)/shard_map/codes_z/all_gather | solution.py:253
  46.5 1.6 broadcast_in_dim.31
  48.1 0.0 copy-start.1
  48.1 0.0 copy-start.7
  48.1 0.0 copy-start.5
  48.1 0.0 copy-start.6
  48.1 0.0 copy-start.4
  48.2 4.9 %all-to-all-start = ((bf16[4,128,2048]{2,1,0:T(8,128)(2,1)}), bf16[4,128,2048]{2,1,0:T(8,128)(2,1)S(1)}, u32[]{:S(2)}, u32[]{:S(2)}) async-start(bf16[4,128,2048]{2,1,0:T(8,128)(2,1)} %broadcast_in_dim.31), calls=%async_computation | async-start | bytes 4194304 | tf_op jit(solution)/shard_map/codes_x/all_to_all | solution.py:42
  53.1 0.0 copy-done.1
  53.1 6.9 %collective-permute-start = (bf16[256,512]{1,0:T(8,128)(2,1)S(1)}, bf16[256,512]{1,0:T(8,128)(2,1)S(1)}, u32[]{:S(2)}, u32[]{:S(2)}) collective-permute-start(bf16[256,512]{1,0:T(8,128)(2,1)S(1)} %copy-done.1), channel_id=1, source_target_pairs={{0,1},{1,0},{2,3},{3,2},{4,5},{5,4},{6,7},{7,6},{8,9},{9,8},{10,11... | collective-permute-start | bytes 786440 | tf_op jit(solution)/shard_map/hidden_hi/ppermute | solution.py:50
  60.0 0.0 copy-done.7
  60.0 0.0 copy-done.5
  60.0 0.1 reshape.80
  60.1 0.0 copy-done.6
  60.1 0.1 reshape.81
  60.2 0.1 concatenate.15
  60.3 7.6 %collective-permute-start.1 = (f32[1088]{0:T(1024)S(1)}, f32[1088]{0:T(1024)S(1)}, u32[]{:S(2)}, u32[]{:S(2)}) collective-permute-start(f32[1088]{0:T(1024)S(1)} %concatenate.15), channel_id=1, source_target_pairs={{0,1},{1,0},{2,3},{3,2},{4,5},{5,4},{6,7},{7,6},{8,9},{9,8},{10,11... | collective-permute-start | bytes 13064 | tf_op jit(solution)/shard_map/codes_x/ppermute | solution.py:50
  67.9 0.0 copy-done.4
  67.9 0.1 copy.29
  68.0 0.1 broadcast_in_dim.33
  68.1 17.5 %collective-permute-done.1 = f32[1088]{0:T(1024)S(1)} collective-permute-done((f32[1088]{0:T(1024)S(1)}, f32[1088]{0:T(1024)S(1)}, u32[]{:S(2)}, u32[]{:S(2)}) %collective-permute-start.1) | collective-permute-done | bytes 4384 | tf_op jit(solution)/shard_map/codes_x/ppermute | solution.py:50
  85.6 0.0 collective-permute-done.peer_ref
  85.7 0.0 all-to-all-done.own_ref.up_own_ref.down_own_ref
  85.7 1.9 collective-permute-start.2
  87.6 0.1 pad_add_fusion.place_ref
  87.7 0.1 fusion.20
  87.8 0.1 split.29
  87.8 0.1 split.31
  87.9 0.1 split.33
  88.0 0.1 copy.30
  88.1 0.1 split.35
  88.2 0.1 copy.31
  88.4 0.1 copy.32
  88.5 0.1 broadcast_bitcast_fusion.scale_ref.up_scale_ref.down_scale_ref
  88.6 3.4 %collective-permute-done.2.other_ref.up_other_ref.down_other_ref = bf16[4,128,2048]{2,1,0:T(8,128)(2,1)} collective-permute-done((bf16[4,128,2048]{2,1,0:T(8,128)(2,1)S(1)}, bf16[4,128,2048]{2,1,0:T(8,128)(2,1)}, u32[]{:S(2)}, u32[]{:S(2)}) %collective-permute-start.2) | collective-permute-done | bytes 2097184 | tf_op jit(solution)/shard_map/codes_x/ppermute | solution.py:54
  92.0 1.9 down.1
  93.9 21.9 %all_to_all.25.parts_ref = bf16[4,272,512]{2,1,0:T(8,128)(2,1)S(1)} all-to-all(bf16[4,272,512]{2,1,0:T(8,128)(2,1)S(1)} %down.1), channel_id=1, replica_groups={{0,2,4,6},{1,3,5,7},{8,10,12,14},{9,11,13,15},{16,18,20,22},{17,19,21,2..., dimensions={0} | all-to-all | bytes 2228224 | tf_op jit(solution)/shard_map/down/all_to_all | solution.py:42
  115.8 3.0 %up_down.1 = (bf16[256,1024]{1,0:T(8,128)(2,1)S(1)}, bf16[4,272,512]{2,1,0:T(8,128)(2,1)S(1)}) custom-call(s32[2]{0:T(128)S(1)} %pad_add_fusion.place_ref, bf16[4,272,512]{2,1,0:T(8,128)(2,1)S(1)} %all_to_all.25.parts_ref, bf16[256,512]{1,0:T(8,128)(2,1)S(1)} %copy-done.1, bf16[256,512]{1,0:T(8,128)(2,1)S(1)} %collective-permute-done.peer_ref, ...), custom_call_target="tpu_custom_call" | custom-call | flops 536870912 | bytes 4194304 | tf_op jit(solution)/shard_map/up_down/pallas_call | solution.py:308
  118.8 17.6 %all_to_all.26.parts_ref = bf16[4,272,512]{2,1,0:T(8,128)(2,1)S(1)} all-to-all(bf16[4,272,512]{2,1,0:T(8,128)(2,1)S(1)} %get-tuple-element.28), channel_id=1, replica_groups={{0,2,4,6},{1,3,5,7},{8,10,12,14},{9,11,13,15},{16,18,20,22},{17,19,21,2..., dimensions={0} | all-to-all | bytes 2228224 | tf_op jit(solution)/shard_map/up_down/all_to_all | solution.py:42
  136.5 2.0 up.1
  138.4 0.0 copy-start.2
  138.5 0.0 copy-start.3
  138.5 27.3 %all_to_all.27.stream_ref = bf16[4,256,1024]{2,1,0:T(8,128)(2,1)S(1)} all-to-all(bf16[4,256,1024]{2,1,0:T(8,128)(2,1)S(1)} %up.1), channel_id=1, replica_groups={{0,2,4,6},{1,3,5,7},{8,10,12,14},{9,11,13,15},{16,18,20,22},{17,19,21,2..., dimensions={0} | all-to-all | bytes 4194304 | tf_op jit(solution)/shard_map/up/all_to_all | solution.py:42
  165.8 0.0 all-gather.2.cloned.1.call-done.codes_ref
  165.8 0.0 copy-done.2
  165.8 0.0 copy-done.3
  165.8 0.0 copy-start
  165.8 3.4 %copy-done = bf16[4096,1024]{1,0:T(8,128)(2,1)S(1)} copy-done((bf16[4096,1024]{1,0:T(8,128)(2,1)S(1)}, bf16[4096,1024]{1,0:T(8,128)(2,1)}, u32[]{:S(2)}) %copy-start) | copy-done | bytes 8388632
  169.2 2.9 %head.1 = f32[8,256]{1,0:T(8,128)S(1)} custom-call(s32[1]{0:T(128)} %bitcast.9.offset_ref, bf16[4,256,1024]{2,1,0:T(8,128)(2,1)S(1)} %all_to_all.27.stream_ref, f32[1,4096]{1,0:T(1,128)S(1)} %bitcast.57, bf16[4096,1024]{1,0:T(8,128)(2,1)S(1)} %copy-done, f32[32,1024]{1,0:T(8,128)S(1)} %bitcast.56, s32[1,256]{1,0:T(1,128)S(1)} %bitcast.58), custom_call_target="tpu_custom_call" | custom-call | flops 2147483648 | bytes 8388608 | tf_op jit(solution)/shard_map/head/pallas_call | solution.py:324
  172.1 7.7 %all_to_all.28 = f32[4,3,256]{2,1,0:T(4,128)S(1)} all-to-all(f32[4,3,256]{2,1,0:T(4,128)S(1)} %broadcast_in_dim.36), channel_id=1, replica_groups={{0,2,4,6},{1,3,5,7},{8,10,12,14},{9,11,13,15},{16,18,20,22},{17,19,21,2..., dimensions={0} | all-to-all | bytes 24576 | tf_op jit(solution)/shard_map/stats/all_to_all | solution.py:42
  179.9 7.3 %collective-permute-start.3 = (f32[3,256]{1,0:T(4,128)S(1)}, f32[3,256]{1,0:T(4,128)S(1)}, u32[]{:S(2)}, u32[]{:S(2)}) collective-permute-start(f32[3,256]{1,0:T(4,128)S(1)} %get-tuple-element.49), channel_id=1, source_target_pairs={{0,1},{1,0},{2,3},{3,2},{4,5},{5,4},{6,7},{7,6},{8,9},{9,8},{10,11... | collective-permute-start | bytes 9224 | tf_op jit(solution)/shard_map/stats/ppermute | solution.py:50
  187.8 6.3 %collective-permute-done.3 = f32[3,256]{1,0:T(4,128)S(1)} collective-permute-done((f32[3,256]{1,0:T(4,128)S(1)}, f32[3,256]{1,0:T(4,128)S(1)}, u32[]{:S(2)}, u32[]{:S(2)}) %collective-permute-start.3) | collective-permute-done | bytes 3104 | tf_op jit(solution)/shard_map/stats/ppermute | solution.py:50
  194.1 0.6 compare_select_fusion
  (22 shorter events, 0.2 us)
Async XLA Ops:
  6.5 159.2 %all-gather.2.cloned.1.call-start = ((), (), s32[]{:S(2)}) async-start(), calls=%async_computation.5 | async-start | bytes 8519680 | tf_op jit(solution)/shard_map/head_rows/all_gather | solution.py:246
  48.1 4.9 %copy-start.1 = (bf16[256,512]{1,0:T(8,128)(2,1)S(1)}, bf16[256,512]{1,0:T(8,128)(2,1)}, u32[]{:S(2)}) copy-start(bf16[256,512]{1,0:T(8,128)(2,1)} %hidden_ref.1) | copy-start | bytes 786436
  48.1 11.9 %copy-start.7 = (f32[2,512]{1,0:T(2,128)S(1)}, f32[2,512]{1,0:T(2,128)}, u32[]{:S(2)}) copy-start(f32[2,512]{1,0:T(2,128)} %param.14) | copy-start | bytes 12292
  48.1 11.9 %copy-start.5 = (f32[2,4,4]{2,1,0:T(4,128)S(1)}, f32[2,4,4]{2,1,0:T(4,128)}, u32[]{:S(2)}) copy-start(f32[2,4,4]{2,1,0:T(4,128)} %param.16) | copy-start | bytes 388
  48.1 12.0 %copy-start.6 = (f32[2,4,4]{2,1,0:T(4,128)S(1)}, f32[2,4,4]{2,1,0:T(4,128)}, u32[]{:S(2)}) copy-start(f32[2,4,4]{2,1,0:T(4,128)} %param.18) | copy-start | bytes 388
  48.1 19.8 %copy-start.4 = (f32[32,8]{0,1:T(8,128)S(1)}, f32[32,8]{0,1:T(8,128)}, u32[]{:S(2)}) copy-start(f32[32,8]{0,1:T(8,128)} %param.21) | copy-start | bytes 3076
  48.2 37.5 %all-to-all-start = ((bf16[4,128,2048]{2,1,0:T(8,128)(2,1)}), bf16[4,128,2048]{2,1,0:T(8,128)(2,1)S(1)}, u32[]{:S(2)}, u32[]{:S(2)}) async-start(bf16[4,128,2048]{2,1,0:T(8,128)(2,1)} %broadcast_in_dim.31), calls=%async_computation | async-start | bytes 4194304 | tf_op jit(solution)/shard_map/codes_x/all_to_all | solution.py:42
  53.1 32.6 %collective-permute-start = (bf16[256,512]{1,0:T(8,128)(2,1)S(1)}, bf16[256,512]{1,0:T(8,128)(2,1)S(1)}, u32[]{:S(2)}, u32[]{:S(2)}) collective-permute-start(bf16[256,512]{1,0:T(8,128)(2,1)S(1)} %copy-done.1), channel_id=1, source_target_pairs={{0,1},{1,0},{2,3},{3,2},{4,5},{5,4},{6,7},{7,6},{8,9},{9,8},{10,11... | collective-permute-start | bytes 786440 | tf_op jit(solution)/shard_map/hidden_hi/ppermute | solution.py:50
  60.3 25.4 %collective-permute-start.1 = (f32[1088]{0:T(1024)S(1)}, f32[1088]{0:T(1024)S(1)}, u32[]{:S(2)}, u32[]{:S(2)}) collective-permute-start(f32[1088]{0:T(1024)S(1)} %concatenate.15), channel_id=1, source_target_pairs={{0,1},{1,0},{2,3},{3,2},{4,5},{5,4},{6,7},{7,6},{8,9},{9,8},{10,11... | collective-permute-start | bytes 13064 | tf_op jit(solution)/shard_map/codes_x/ppermute | solution.py:50
  85.7 6.4 %collective-permute-start.2 = (bf16[4,128,2048]{2,1,0:T(8,128)(2,1)S(1)}, bf16[4,128,2048]{2,1,0:T(8,128)(2,1)}, u32[]{:S(2)}, u32[]{:S(2)}) collective-permute-start(bf16[4,128,2048]{2,1,0:T(8,128)(2,1)S(1)} %all-to-all-done.own_ref.up_own_ref.down_own_ref), channel_id=1, source_target_pairs={{0,8},{8,0},{16,24},{24,16},{32,40},{40,32},{48,56},{56,48},{64,72... | collective-permute-start | bytes 6291464 | tf_op jit(solution)/shard_map/codes_x/ppermute | solution.py:54
  138.4 27.3 %copy-start.2 = (f32[4096]{0:T(1024)S(1)}, f32[4096]{0:T(1024)}, u32[]{:S(2)}) copy-start(f32[4096]{0:T(1024)} %param.19) | copy-start | bytes 49156
  138.5 27.3 %copy-start.3 = (s32[256]{0:T(256)S(1)}, s32[256]{0:T(256)}, u32[]{:S(2)}) copy-start(s32[256]{0:T(256)} %param.12) | copy-start | bytes 3076
  165.8 3.4 %copy-start = (bf16[4096,1024]{1,0:T(8,128)(2,1)S(1)}, bf16[4096,1024]{1,0:T(8,128)(2,1)}, u32[]{:S(2)}) copy-start(bf16[4096,1024]{1,0:T(8,128)(2,1)} %all-gather.2.cloned.1.call-done.codes_ref) | copy-start | bytes 25165828
  179.9 14.2 %collective-permute-start.3 = (f32[3,256]{1,0:T(4,128)S(1)}, f32[3,256]{1,0:T(4,128)S(1)}, u32[]{:S(2)}, u32[]{:S(2)}) collective-permute-start(f32[3,256]{1,0:T(4,128)S(1)} %get-tuple-element.49), channel_id=1, source_target_pairs={{0,1},{1,0},{2,3},{3,2},{4,5},{5,4},{6,7},{7,6},{8,9},{9,8},{10,11... | collective-permute-start | bytes 9224 | tf_op jit(solution)/shard_map/stats/ppermute | solution.py:50
Sparse Core Ops, SparseCore 0:
  9.5 149.1 all-gather.1

commit v7 on v6

--- a/solution.py
+++ b/solution.py
@@ -22,6 +22,7 @@
 
 
 x_groups = [[dp_of(x, z, c) for x in range(n_x)] for z in range(n_z) for c in range(n_core)]
+sum_groups = [[y * n_hi + h for y in (0, 2, 1, 3)] for h in range(n_hi)]
 y_groups = [[y * n_hi + h for y in range(n_y)] for h in range(n_hi)]
 z_groups = [
     [dp_of(x, z, c) * n_y * n_hi + y * n_hi + h for h in range(n_hi) for z in range(n_z)]
@@ -303,7 +304,7 @@
         parts = call(first_kernel, parts_shape, [vmem] * 3 + matrix(0, rank), matmul)(
             place, hidden, hidden_peer, gain[0:1], codes, other, scales
         )
-        parts = send_alike(parts, "tensor", y_groups)
+        parts = send_alike(parts, "tensor", sum_groups)
     with jax.named_scope("up_down"):
         stream, parts = call(
             middle_kernel, (stream_shape, parts_shape),
@@ -312,7 +313,7 @@
             place, parts, hidden, hidden_peer, gain[1:2],
             codes, other, scales, codes, other, scales,
         )
-        parts = send_alike(parts, "tensor", y_groups)
+        parts = send_alike(parts, "tensor", sum_groups)
     with jax.named_scope("up"):
         stream = call(
             last_kernel, jax.ShapeDtypeStruct((n_y, tok, width), bf16),

time: 202 us -> 201 us (level)
  no operation moved by 1% of the time
where the time goes in v7:
time: 201 us
  blocking collectives  112 us (56%)
  starting transfers between devices  28.9 us (14%)
  waiting for transfers between devices  27.7 us (14%)
  between operations  14.3 us (7%)
  Pallas kernels  9.78 us (5%)
  local copies, waits for them, and re-layouts  6.32 us (3%)
    all_to_all x4, blocking collectives, send_alike(): return lax.all_to_all(copies, axis, 0, 0, axis_index_groups=groups)  73.6 us
    all_gather x1, blocking collectives, per_device(): lax.all_gather(codes, ('dp', 'tensor'), axis=0, tiled=True, axis_index_gr...  38.5 us
    ppermute x3, waiting for transfers between devices, swap_hi(): return lax.ppermute(value, 'tensor', hi_pairs)  23.6 us
    ppermute x3, starting transfers between devices, swap_hi(): return lax.ppermute(value, 'tensor', hi_pairs)  22 us
    all_to_all x1, starting transfers between devices, send_alike(): return lax.all_to_all(copies, axis, 0, 0, axis_index_groups=groups)  4.91 us
  transfers between devices with their start and end apart: 6, of which 3 were waited for; matrix products, arithmetic and copies ran while one was open for 2% of the time, Pallas kernels for 3%

profile of v7, /device:TPU:6, one launch (start us, length us, event | category | flops | bytes accessed | tf_op | source)
XLA Modules:
  0.0 200.6 jit_solution(15127796922378640547)
XLA Ops:
  6.5 0.0 all-gather.2.cloned.1.call-start
  6.5 0.7 all-gather.2.cloned.1.call-update
  7.3 0.7 pad_maximum_fusion
  8.0 38.5 %all_gather.6 = bf16[512,512]{1,0:T(8,128)(2,1)S(1)} all-gather(bf16[32,512]{1,0:T(8,128)(2,1)S(1)} %bitcast.61), channel_id=1, replica_groups={{0,16,32,48,64,80,96,112,1,17,33,49,65,81,97,113},{2,18,34,50,66,82,98,..., dimensions={0}, use_global_device_ids=true | all-gather | bytes 557056 | tf_op jit(solution)/shard_map/codes_z/all_gather | solution.py:254
  46.5 1.6 broadcast_in_dim.31
  48.1 0.0 copy-start.1
  48.1 0.0 copy-start.7
  48.1 0.0 copy-start.5
  48.1 0.0 copy-start.6
  48.1 0.0 copy-start.4
  48.2 4.9 %all-to-all-start = ((bf16[4,128,2048]{2,1,0:T(8,128)(2,1)}), bf16[4,128,2048]{2,1,0:T(8,128)(2,1)S(1)}, u32[]{:S(2)}, u32[]{:S(2)}) async-start(bf16[4,128,2048]{2,1,0:T(8,128)(2,1)} %broadcast_in_dim.31), calls=%async_computation | async-start | bytes 4194304 | tf_op jit(solution)/shard_map/codes_x/all_to_all | solution.py:43
  53.1 0.0 copy-done.1
  53.1 6.9 %collective-permute-start = (bf16[256,512]{1,0:T(8,128)(2,1)S(1)}, bf16[256,512]{1,0:T(8,128)(2,1)S(1)}, u32[]{:S(2)}, u32[]{:S(2)}) collective-permute-start(bf16[256,512]{1,0:T(8,128)(2,1)S(1)} %copy-done.1), channel_id=1, source_target_pairs={{0,1},{1,0},{2,3},{3,2},{4,5},{5,4},{6,7},{7,6},{8,9},{9,8},{10,11... | collective-permute-start | bytes 786440 | tf_op jit(solution)/shard_map/hidden_hi/ppermute | solution.py:51
  60.0 0.0 copy-done.7
  60.0 0.0 copy-done.5
  60.0 0.1 reshape.80
  60.1 0.0 copy-done.6
  60.1 0.1 reshape.81
  60.2 0.1 concatenate.15
  60.3 7.6 %collective-permute-start.1 = (f32[1088]{0:T(1024)S(1)}, f32[1088]{0:T(1024)S(1)}, u32[]{:S(2)}, u32[]{:S(2)}) collective-permute-start(f32[1088]{0:T(1024)S(1)} %concatenate.15), channel_id=1, source_target_pairs={{0,1},{1,0},{2,3},{3,2},{4,5},{5,4},{6,7},{7,6},{8,9},{9,8},{10,11... | collective-permute-start | bytes 13064 | tf_op jit(solution)/shard_map/codes_x/ppermute | solution.py:51
  67.9 0.0 copy-done.4
  67.9 0.1 copy.29
  68.0 0.1 broadcast_in_dim.33
  68.1 17.5 %collective-permute-done.1 = f32[1088]{0:T(1024)S(1)} collective-permute-done((f32[1088]{0:T(1024)S(1)}, f32[1088]{0:T(1024)S(1)}, u32[]{:S(2)}, u32[]{:S(2)}) %collective-permute-start.1) | collective-permute-done | bytes 4384 | tf_op jit(solution)/shard_map/codes_x/ppermute | solution.py:51
  85.6 0.0 collective-permute-done.peer_ref
  85.7 0.0 all-to-all-done.own_ref.up_own_ref.down_own_ref
  85.7 1.9 collective-permute-start.2
  87.6 0.1 pad_add_fusion.place_ref
  87.7 0.1 fusion.20
  87.8 0.1 split.29
  87.8 0.1 split.31
  87.9 0.1 split.33
  88.0 0.1 copy.30
  88.1 0.1 split.35
  88.2 0.1 copy.31
  88.4 0.1 copy.32
  88.5 0.1 broadcast_bitcast_fusion.scale_ref.up_scale_ref.down_scale_ref
  88.6 3.4 %collective-permute-done.2.other_ref.up_other_ref.down_other_ref = bf16[4,128,2048]{2,1,0:T(8,128)(2,1)} collective-permute-done((bf16[4,128,2048]{2,1,0:T(8,128)(2,1)S(1)}, bf16[4,128,2048]{2,1,0:T(8,128)(2,1)}, u32[]{:S(2)}, u32[]{:S(2)}) %collective-permute-start.2) | collective-permute-done | bytes 2097184 | tf_op jit(solution)/shard_map/codes_x/ppermute | solution.py:55
  92.0 1.9 down.1
  93.9 21.7 %all_to_all.25.parts_ref = bf16[4,272,512]{2,1,0:T(8,128)(2,1)S(1)} all-to-all(bf16[4,272,512]{2,1,0:T(8,128)(2,1)S(1)} %down.1), channel_id=1, replica_groups={{0,4,2,6},{1,5,3,7},{8,12,10,14},{9,13,11,15},{16,20,18,22},{17,21,19,2..., dimensions={0} | all-to-all | bytes 2228224 | tf_op jit(solution)/shard_map/down/all_to_all | solution.py:43
  115.7 3.0 %up_down.1 = (bf16[256,1024]{1,0:T(8,128)(2,1)S(1)}, bf16[4,272,512]{2,1,0:T(8,128)(2,1)S(1)}) custom-call(s32[2]{0:T(128)S(1)} %pad_add_fusion.place_ref, bf16[4,272,512]{2,1,0:T(8,128)(2,1)S(1)} %all_to_all.25.parts_ref, bf16[256,512]{1,0:T(8,128)(2,1)S(1)} %copy-done.1, bf16[256,512]{1,0:T(8,128)(2,1)S(1)} %collective-permute-done.peer_ref, ...), custom_call_target="tpu_custom_call" | custom-call | flops 536870912 | bytes 4194304 | tf_op jit(solution)/shard_map/up_down/pallas_call | solution.py:309
  118.7 17.2 %all_to_all.26.parts_ref = bf16[4,272,512]{2,1,0:T(8,128)(2,1)S(1)} all-to-all(bf16[4,272,512]{2,1,0:T(8,128)(2,1)S(1)} %get-tuple-element.28), channel_id=1, replica_groups={{0,4,2,6},{1,5,3,7},{8,12,10,14},{9,13,11,15},{16,20,18,22},{17,21,19,2..., dimensions={0} | all-to-all | bytes 2228224 | tf_op jit(solution)/shard_map/up_down/all_to_all | solution.py:43
  135.9 2.0 up.1
  137.9 0.0 copy-start.2
  137.9 0.0 copy-start.3
  137.9 26.9 %all_to_all.27.stream_ref = bf16[4,256,1024]{2,1,0:T(8,128)(2,1)S(1)} all-to-all(bf16[4,256,1024]{2,1,0:T(8,128)(2,1)S(1)} %up.1), channel_id=1, replica_groups={{0,2,4,6},{1,3,5,7},{8,10,12,14},{9,11,13,15},{16,18,20,22},{17,19,21,2..., dimensions={0} | all-to-all | bytes 4194304 | tf_op jit(solution)/shard_map/up/all_to_all | solution.py:43
  164.8 0.0 all-gather.2.cloned.1.call-done.codes_ref
  164.8 0.0 copy-done.2
  164.8 0.0 copy-done.3
  164.8 0.0 copy-start
  164.8 3.4 %copy-done = bf16[4096,1024]{1,0:T(8,128)(2,1)S(1)} copy-done((bf16[4096,1024]{1,0:T(8,128)(2,1)S(1)}, bf16[4096,1024]{1,0:T(8,128)(2,1)}, u32[]{:S(2)}) %copy-start) | copy-done | bytes 8388632
  168.2 2.9 %head.1 = f32[8,256]{1,0:T(8,128)S(1)} custom-call(s32[1]{0:T(128)} %bitcast.9.offset_ref, bf16[4,256,1024]{2,1,0:T(8,128)(2,1)S(1)} %all_to_all.27.stream_ref, f32[1,4096]{1,0:T(1,128)S(1)} %bitcast.57, bf16[4096,1024]{1,0:T(8,128)(2,1)S(1)} %copy-done, f32[32,1024]{1,0:T(8,128)S(1)} %bitcast.56, s32[1,256]{1,0:T(1,128)S(1)} %bitcast.58), custom_call_target="tpu_custom_call" | custom-call | flops 2147483648 | bytes 8388608 | tf_op jit(solution)/shard_map/head/pallas_call | solution.py:325
  171.1 7.7 %all_to_all.28 = f32[4,3,256]{2,1,0:T(4,128)S(1)} all-to-all(f32[4,3,256]{2,1,0:T(4,128)S(1)} %broadcast_in_dim.36), channel_id=1, replica_groups={{0,2,4,6},{1,3,5,7},{8,10,12,14},{9,11,13,15},{16,18,20,22},{17,19,21,2..., dimensions={0} | all-to-all | bytes 24576 | tf_op jit(solution)/shard_map/stats/all_to_all | solution.py:43
  178.9 7.5 %collective-permute-start.3 = (f32[3,256]{1,0:T(4,128)S(1)}, f32[3,256]{1,0:T(4,128)S(1)}, u32[]{:S(2)}, u32[]{:S(2)}) collective-permute-start(f32[3,256]{1,0:T(4,128)S(1)} %get-tuple-element.49), channel_id=1, source_target_pairs={{0,1},{1,0},{2,3},{3,2},{4,5},{5,4},{6,7},{7,6},{8,9},{9,8},{10,11... | collective-permute-start | bytes 9224 | tf_op jit(solution)/shard_map/stats/ppermute | solution.py:51
  187.1 6.1 %collective-permute-done.3 = f32[3,256]{1,0:T(4,128)S(1)} collective-permute-done((f32[3,256]{1,0:T(4,128)S(1)}, f32[3,256]{1,0:T(4,128)S(1)}, u32[]{:S(2)}, u32[]{:S(2)}) %collective-permute-start.3) | collective-permute-done | bytes 3104 | tf_op jit(solution)/shard_map/stats/ppermute | solution.py:51
  193.2 0.6 compare_select_fusion
  (22 shorter events, 0.2 us)
Async XLA Ops:
  6.5 158.3 %all-gather.2.cloned.1.call-start = ((), (), s32[]{:S(2)}) async-start(), calls=%async_computation.5 | async-start | bytes 8519680 | tf_op jit(solution)/shard_map/head_rows/all_gather | solution.py:247
  48.1 4.9 %copy-start.1 = (bf16[256,512]{1,0:T(8,128)(2,1)S(1)}, bf16[256,512]{1,0:T(8,128)(2,1)}, u32[]{:S(2)}) copy-start(bf16[256,512]{1,0:T(8,128)(2,1)} %hidden_ref.1) | copy-start | bytes 786436
  48.1 11.9 %copy-start.7 = (f32[2,512]{1,0:T(2,128)S(1)}, f32[2,512]{1,0:T(2,128)}, u32[]{:S(2)}) copy-start(f32[2,512]{1,0:T(2,128)} %param.14) | copy-start | bytes 12292
  48.1 11.9 %copy-start.5 = (f32[2,4,4]{2,1,0:T(4,128)S(1)}, f32[2,4,4]{2,1,0:T(4,128)}, u32[]{:S(2)}) copy-start(f32[2,4,4]{2,1,0:T(4,128)} %param.16) | copy-start | bytes 388
  48.1 12.0 %copy-start.6 = (f32[2,4,4]{2,1,0:T(4,128)S(1)}, f32[2,4,4]{2,1,0:T(4,128)}, u32[]{:S(2)}) copy-start(f32[2,4,4]{2,1,0:T(4,128)} %param.18) | copy-start | bytes 388
  48.1 19.8 %copy-start.4 = (f32[32,8]{0,1:T(8,128)S(1)}, f32[32,8]{0,1:T(8,128)}, u32[]{:S(2)}) copy-start(f32[32,8]{0,1:T(8,128)} %param.21) | copy-start | bytes 3076
  48.2 37.5 %all-to-all-start = ((bf16[4,128,2048]{2,1,0:T(8,128)(2,1)}), bf16[4,128,2048]{2,1,0:T(8,128)(2,1)S(1)}, u32[]{:S(2)}, u32[]{:S(2)}) async-start(bf16[4,128,2048]{2,1,0:T(8,128)(2,1)} %broadcast_in_dim.31), calls=%async_computation | async-start | bytes 4194304 | tf_op jit(solution)/shard_map/codes_x/all_to_all | solution.py:43
  53.1 32.6 %collective-permute-start = (bf16[256,512]{1,0:T(8,128)(2,1)S(1)}, bf16[256,512]{1,0:T(8,128)(2,1)S(1)}, u32[]{:S(2)}, u32[]{:S(2)}) collective-permute-start(bf16[256,512]{1,0:T(8,128)(2,1)S(1)} %copy-done.1), channel_id=1, source_target_pairs={{0,1},{1,0},{2,3},{3,2},{4,5},{5,4},{6,7},{7,6},{8,9},{9,8},{10,11... | collective-permute-start | bytes 786440 | tf_op jit(solution)/shard_map/hidden_hi/ppermute | solution.py:51
  60.3 25.4 %collective-permute-start.1 = (f32[1088]{0:T(1024)S(1)}, f32[1088]{0:T(1024)S(1)}, u32[]{:S(2)}, u32[]{:S(2)}) collective-permute-start(f32[1088]{0:T(1024)S(1)} %concatenate.15), channel_id=1, source_target_pairs={{0,1},{1,0},{2,3},{3,2},{4,5},{5,4},{6,7},{7,6},{8,9},{9,8},{10,11... | collective-permute-start | bytes 13064 | tf_op jit(solution)/shard_map/codes_x/ppermute | solution.py:51
  85.7 6.4 %collective-permute-start.2 = (bf16[4,128,2048]{2,1,0:T(8,128)(2,1)S(1)}, bf16[4,128,2048]{2,1,0:T(8,128)(2,1)}, u32[]{:S(2)}, u32[]{:S(2)}) collective-permute-start(bf16[4,128,2048]{2,1,0:T(8,128)(2,1)S(1)} %all-to-all-done.own_ref.up_own_ref.down_own_ref), channel_id=1, source_target_pairs={{0,8},{8,0},{16,24},{24,16},{32,40},{40,32},{48,56},{56,48},{64,72... | collective-permute-start | bytes 6291464 | tf_op jit(solution)/shard_map/codes_x/ppermute | solution.py:55
  137.9 26.9 %copy-start.2 = (f32[4096]{0:T(1024)S(1)}, f32[4096]{0:T(1024)}, u32[]{:S(2)}) copy-start(f32[4096]{0:T(1024)} %param.19) | copy-start | bytes 49156
  137.9 26.9 %copy-start.3 = (s32[256]{0:T(256)S(1)}, s32[256]{0:T(256)}, u32[]{:S(2)}) copy-start(s32[256]{0:T(256)} %param.12) | copy-start | bytes 3076
  164.8 3.4 %copy-start = (bf16[4096,1024]{1,0:T(8,128)(2,1)S(1)}, bf16[4096,1024]{1,0:T(8,128)(2,1)}, u32[]{:S(2)}) copy-start(bf16[4096,1024]{1,0:T(8,128)(2,1)} %all-gather.2.cloned.1.call-done.codes_ref) | copy-start | bytes 25165828
  178.9 14.2 %collective-permute-start.3 = (f32[3,256]{1,0:T(4,128)S(1)}, f32[3,256]{1,0:T(4,128)S(1)}, u32[]{:S(2)}, u32[]{:S(2)}) collective-permute-start(f32[3,256]{1,0:T(4,128)S(1)} %get-tuple-element.49), channel_id=1, source_target_pairs={{0,1},{1,0},{2,3},{3,2},{4,5},{5,4},{6,7},{7,6},{8,9},{9,8},{10,11... | collective-permute-start | bytes 9224 | tf_op jit(solution)/shard_map/stats/ppermute | solution.py:51
Sparse Core Ops, SparseCore 0:
  9.5 149.2 all-gather.1

commit v8 on v6

--- a/solution.py
+++ b/solution.py
@@ -22,7 +22,8 @@
 
 
 x_groups = [[dp_of(x, z, c) for x in range(n_x)] for z in range(n_z) for c in range(n_core)]
-y_groups = [[y * n_hi + h for y in range(n_y)] for h in range(n_hi)]
+y_order = (0, 2, 1, 3)
+y_groups = [[y * n_hi + h for y in y_order] for h in range(n_hi)]
 z_groups = [
     [dp_of(x, z, c) * n_y * n_hi + y * n_hi + h for h in range(n_hi) for z in range(n_z)]
     for x in range(n_x)
@@ -179,7 +180,7 @@
     logits, squares = 0.0, 0.0
     for at in range(model_width // chunk):
         block, part = divmod(at * chunk, width)
-        values = stream_ref[block, :, pl.ds(part, chunk)].astype(f32)
+        values = stream_ref[y_order[block], :, pl.ds(part, chunk)].astype(f32)
         squares = squares + jnp.sum(values * values, axis=1, keepdims=True)
         final = (values * gain_ref[:, pl.ds(at * chunk, chunk)]).astype(bf16)
         weight = []

time: 202 us -> 201 us (level)
  no operation moved by 1% of the time
where the time goes in v8:
time: 201 us; the launch traced here: 200 us
  blocking collectives  112 us (56%)
  starting transfers between devices  28.9 us (14%)
  waiting for transfers between devices  27.7 us (14%)
  between operations  14.3 us (7%)
  Pallas kernels  9.78 us (5%)
  local copies, waits for them, and re-layouts  6.32 us (3%)
    all_to_all x4, blocking collectives, send_alike(): return lax.all_to_all(copies, axis, 0, 0, axis_index_groups=groups)  73.4 us
    all_gather x1, blocking collectives, per_device(): lax.all_gather(codes, ('dp', 'tensor'), axis=0, tiled=True, axis_index_gr...  38.5 us
    ppermute x3, waiting for transfers between devices, swap_hi(): return lax.ppermute(value, 'tensor', hi_pairs)  23.6 us
    ppermute x3, starting transfers between devices, swap_hi(): return lax.ppermute(value, 'tensor', hi_pairs)  22 us
    all_to_all x1, starting transfers between devices, send_alike(): return lax.all_to_all(copies, axis, 0, 0, axis_index_groups=groups)  4.91 us
  transfers between devices with their start and end apart: 6, of which 3 were waited for; matrix products, arithmetic and copies ran while one was open for 2% of the time, Pallas kernels for 3%

profile of v8, /device:TPU:6, one launch (start us, length us, event | category | flops | bytes accessed | tf_op | source)
XLA Modules:
  0.0 200.5 jit_solution(13469508941834317918)
XLA Ops:
  6.5 0.0 all-gather.2.cloned.1.call-start
  6.5 0.7 all-gather.2.cloned.1.call-update
  7.3 0.7 pad_maximum_fusion
  8.0 38.5 %all_gather.6 = bf16[512,512]{1,0:T(8,128)(2,1)S(1)} all-gather(bf16[32,512]{1,0:T(8,128)(2,1)S(1)} %bitcast.61), channel_id=1, replica_groups={{0,16,32,48,64,80,96,112,1,17,33,49,65,81,97,113},{2,18,34,50,66,82,98,..., dimensions={0}, use_global_device_ids=true | all-gather | bytes 557056 | tf_op jit(solution)/shard_map/codes_z/all_gather | solution.py:254
  46.5 1.6 broadcast_in_dim.31
  48.1 0.0 copy-start.1
  48.1 0.0 copy-start.7
  48.1 0.0 copy-start.5
  48.1 0.0 copy-start.6
  48.1 0.0 copy-start.4
  48.2 4.9 %all-to-all-start = ((bf16[4,128,2048]{2,1,0:T(8,128)(2,1)}), bf16[4,128,2048]{2,1,0:T(8,128)(2,1)S(1)}, u32[]{:S(2)}, u32[]{:S(2)}) async-start(bf16[4,128,2048]{2,1,0:T(8,128)(2,1)} %broadcast_in_dim.31), calls=%async_computation | async-start | bytes 4194304 | tf_op jit(solution)/shard_map/codes_x/all_to_all | solution.py:43
  53.1 0.0 copy-done.1
  53.1 6.9 %collective-permute-start = (bf16[256,512]{1,0:T(8,128)(2,1)S(1)}, bf16[256,512]{1,0:T(8,128)(2,1)S(1)}, u32[]{:S(2)}, u32[]{:S(2)}) collective-permute-start(bf16[256,512]{1,0:T(8,128)(2,1)S(1)} %copy-done.1), channel_id=1, source_target_pairs={{0,1},{1,0},{2,3},{3,2},{4,5},{5,4},{6,7},{7,6},{8,9},{9,8},{10,11... | collective-permute-start | bytes 786440 | tf_op jit(solution)/shard_map/hidden_hi/ppermute | solution.py:51
  60.0 0.0 copy-done.7
  60.0 0.0 copy-done.5
  60.0 0.1 reshape.80
  60.1 0.0 copy-done.6
  60.1 0.1 reshape.81
  60.2 0.1 concatenate.15
  60.3 7.6 %collective-permute-start.1 = (f32[1088]{0:T(1024)S(1)}, f32[1088]{0:T(1024)S(1)}, u32[]{:S(2)}, u32[]{:S(2)}) collective-permute-start(f32[1088]{0:T(1024)S(1)} %concatenate.15), channel_id=1, source_target_pairs={{0,1},{1,0},{2,3},{3,2},{4,5},{5,4},{6,7},{7,6},{8,9},{9,8},{10,11... | collective-permute-start | bytes 13064 | tf_op jit(solution)/shard_map/codes_x/ppermute | solution.py:51
  67.9 0.0 copy-done.4
  67.9 0.1 copy.29
  68.0 0.1 broadcast_in_dim.33
  68.1 17.5 %collective-permute-done.1 = f32[1088]{0:T(1024)S(1)} collective-permute-done((f32[1088]{0:T(1024)S(1)}, f32[1088]{0:T(1024)S(1)}, u32[]{:S(2)}, u32[]{:S(2)}) %collective-permute-start.1) | collective-permute-done | bytes 4384 | tf_op jit(solution)/shard_map/codes_x/ppermute | solution.py:51
  85.6 0.0 collective-permute-done.peer_ref
  85.7 0.0 all-to-all-done.own_ref.up_own_ref.down_own_ref
  85.7 1.9 collective-permute-start.2
  87.6 0.1 pad_add_fusion.place_ref
  87.7 0.1 fusion.20
  87.8 0.1 split.29
  87.8 0.1 split.31
  87.9 0.1 split.33
  88.0 0.1 copy.30
  88.1 0.1 split.35
  88.2 0.1 copy.31
  88.4 0.1 copy.32
  88.5 0.1 broadcast_bitcast_fusion.scale_ref.up_scale_ref.down_scale_ref
  88.6 3.4 %collective-permute-done.2.other_ref.up_other_ref.down_other_ref = bf16[4,128,2048]{2,1,0:T(8,128)(2,1)} collective-permute-done((bf16[4,128,2048]{2,1,0:T(8,128)(2,1)S(1)}, bf16[4,128,2048]{2,1,0:T(8,128)(2,1)}, u32[]{:S(2)}, u32[]{:S(2)}) %collective-permute-start.2) | collective-permute-done | bytes 2097184 | tf_op jit(solution)/shard_map/codes_x/ppermute | solution.py:55
  92.0 1.9 down.1
  93.9 21.7 %all_to_all.25.parts_ref = bf16[4,272,512]{2,1,0:T(8,128)(2,1)S(1)} all-to-all(bf16[4,272,512]{2,1,0:T(8,128)(2,1)S(1)} %down.1), channel_id=1, replica_groups={{0,4,2,6},{1,5,3,7},{8,12,10,14},{9,13,11,15},{16,20,18,22},{17,21,19,2..., dimensions={0} | all-to-all | bytes 2228224 | tf_op jit(solution)/shard_map/down/all_to_all | solution.py:43
  115.7 3.0 %up_down.1 = (bf16[256,1024]{1,0:T(8,128)(2,1)S(1)}, bf16[4,272,512]{2,1,0:T(8,128)(2,1)S(1)}) custom-call(s32[2]{0:T(128)S(1)} %pad_add_fusion.place_ref, bf16[4,272,512]{2,1,0:T(8,128)(2,1)S(1)} %all_to_all.25.parts_ref, bf16[256,512]{1,0:T(8,128)(2,1)S(1)} %copy-done.1, bf16[256,512]{1,0:T(8,128)(2,1)S(1)} %collective-permute-done.peer_ref, ...), custom_call_target="tpu_custom_call" | custom-call | flops 536870912 | bytes 4194304 | tf_op jit(solution)/shard_map/up_down/pallas_call | solution.py:309
  118.7 17.2 %all_to_all.26.parts_ref = bf16[4,272,512]{2,1,0:T(8,128)(2,1)S(1)} all-to-all(bf16[4,272,512]{2,1,0:T(8,128)(2,1)S(1)} %get-tuple-element.28), channel_id=1, replica_groups={{0,4,2,6},{1,5,3,7},{8,12,10,14},{9,13,11,15},{16,20,18,22},{17,21,19,2..., dimensions={0} | all-to-all | bytes 2228224 | tf_op jit(solution)/shard_map/up_down/all_to_all | solution.py:43
  135.9 2.0 up.1
  137.9 0.0 copy-start.2
  137.9 0.0 copy-start.3
  137.9 26.6 %all_to_all.27.stream_ref = bf16[4,256,1024]{2,1,0:T(8,128)(2,1)S(1)} all-to-all(bf16[4,256,1024]{2,1,0:T(8,128)(2,1)S(1)} %up.1), channel_id=1, replica_groups={{0,4,2,6},{1,5,3,7},{8,12,10,14},{9,13,11,15},{16,20,18,22},{17,21,19,2..., dimensions={0} | all-to-all | bytes 4194304 | tf_op jit(solution)/shard_map/up/all_to_all | solution.py:43
  164.5 0.0 all-gather.2.cloned.1.call-done.codes_ref
  164.5 0.0 copy-done.2
  164.5 0.0 copy-done.3
  164.5 0.0 copy-start
  164.5 3.4 %copy-done = bf16[4096,1024]{1,0:T(8,128)(2,1)S(1)} copy-done((bf16[4096,1024]{1,0:T(8,128)(2,1)S(1)}, bf16[4096,1024]{1,0:T(8,128)(2,1)}, u32[]{:S(2)}) %copy-start) | copy-done | bytes 8388632
  167.9 2.9 %head.1 = f32[8,256]{1,0:T(8,128)S(1)} custom-call(s32[1]{0:T(128)} %bitcast.9.offset_ref, bf16[4,256,1024]{2,1,0:T(8,128)(2,1)S(1)} %all_to_all.27.stream_ref, f32[1,4096]{1,0:T(1,128)S(1)} %bitcast.57, bf16[4096,1024]{1,0:T(8,128)(2,1)S(1)} %copy-done, f32[32,1024]{1,0:T(8,128)S(1)} %bitcast.56, s32[1,256]{1,0:T(1,128)S(1)} %bitcast.58), custom_call_target="tpu_custom_call" | custom-call | flops 2147483648 | bytes 8388608 | tf_op jit(solution)/shard_map/head/pallas_call | solution.py:325
  170.8 7.8 %all_to_all.28 = f32[4,3,256]{2,1,0:T(4,128)S(1)} all-to-all(f32[4,3,256]{2,1,0:T(4,128)S(1)} %broadcast_in_dim.36), channel_id=1, replica_groups={{0,4,2,6},{1,5,3,7},{8,12,10,14},{9,13,11,15},{16,20,18,22},{17,21,19,2..., dimensions={0} | all-to-all | bytes 24576 | tf_op jit(solution)/shard_map/stats/all_to_all | solution.py:43
  178.8 7.5 %collective-permute-start.3 = (f32[3,256]{1,0:T(4,128)S(1)}, f32[3,256]{1,0:T(4,128)S(1)}, u32[]{:S(2)}, u32[]{:S(2)}) collective-permute-start(f32[3,256]{1,0:T(4,128)S(1)} %get-tuple-element.49), channel_id=1, source_target_pairs={{0,1},{1,0},{2,3},{3,2},{4,5},{5,4},{6,7},{7,6},{8,9},{9,8},{10,11... | collective-permute-start | bytes 9224 | tf_op jit(solution)/shard_map/stats/ppermute | solution.py:51
  186.9 6.1 %collective-permute-done.3 = f32[3,256]{1,0:T(4,128)S(1)} collective-permute-done((f32[3,256]{1,0:T(4,128)S(1)}, f32[3,256]{1,0:T(4,128)S(1)}, u32[]{:S(2)}, u32[]{:S(2)}) %collective-permute-start.3) | collective-permute-done | bytes 3104 | tf_op jit(solution)/shard_map/stats/ppermute | solution.py:51
  193.0 0.6 compare_select_fusion
  (22 shorter events, 0.2 us)
Async XLA Ops:
  6.5 158.0 %all-gather.2.cloned.1.call-start = ((), (), s32[]{:S(2)}) async-start(), calls=%async_computation.5 | async-start | bytes 8519680 | tf_op jit(solution)/shard_map/head_rows/all_gather | solution.py:247
  48.1 4.9 %copy-start.1 = (bf16[256,512]{1,0:T(8,128)(2,1)S(1)}, bf16[256,512]{1,0:T(8,128)(2,1)}, u32[]{:S(2)}) copy-start(bf16[256,512]{1,0:T(8,128)(2,1)} %hidden_ref.1) | copy-start | bytes 786436
  48.1 11.9 %copy-start.7 = (f32[2,512]{1,0:T(2,128)S(1)}, f32[2,512]{1,0:T(2,128)}, u32[]{:S(2)}) copy-start(f32[2,512]{1,0:T(2,128)} %param.14) | copy-start | bytes 12292
  48.1 11.9 %copy-start.5 = (f32[2,4,4]{2,1,0:T(4,128)S(1)}, f32[2,4,4]{2,1,0:T(4,128)}, u32[]{:S(2)}) copy-start(f32[2,4,4]{2,1,0:T(4,128)} %param.16) | copy-start | bytes 388
  48.1 12.0 %copy-start.6 = (f32[2,4,4]{2,1,0:T(4,128)S(1)}, f32[2,4,4]{2,1,0:T(4,128)}, u32[]{:S(2)}) copy-start(f32[2,4,4]{2,1,0:T(4,128)} %param.18) | copy-start | bytes 388
  48.1 19.8 %copy-start.4 = (f32[32,8]{0,1:T(8,128)S(1)}, f32[32,8]{0,1:T(8,128)}, u32[]{:S(2)}) copy-start(f32[32,8]{0,1:T(8,128)} %param.21) | copy-start | bytes 3076
  48.2 37.5 %all-to-all-start = ((bf16[4,128,2048]{2,1,0:T(8,128)(2,1)}), bf16[4,128,2048]{2,1,0:T(8,128)(2,1)S(1)}, u32[]{:S(2)}, u32[]{:S(2)}) async-start(bf16[4,128,2048]{2,1,0:T(8,128)(2,1)} %broadcast_in_dim.31), calls=%async_computation | async-start | bytes 4194304 | tf_op jit(solution)/shard_map/codes_x/all_to_all | solution.py:43
  53.1 32.6 %collective-permute-start = (bf16[256,512]{1,0:T(8,128)(2,1)S(1)}, bf16[256,512]{1,0:T(8,128)(2,1)S(1)}, u32[]{:S(2)}, u32[]{:S(2)}) collective-permute-start(bf16[256,512]{1,0:T(8,128)(2,1)S(1)} %copy-done.1), channel_id=1, source_target_pairs={{0,1},{1,0},{2,3},{3,2},{4,5},{5,4},{6,7},{7,6},{8,9},{9,8},{10,11... | collective-permute-start | bytes 786440 | tf_op jit(solution)/shard_map/hidden_hi/ppermute | solution.py:51
  60.3 25.4 %collective-permute-start.1 = (f32[1088]{0:T(1024)S(1)}, f32[1088]{0:T(1024)S(1)}, u32[]{:S(2)}, u32[]{:S(2)}) collective-permute-start(f32[1088]{0:T(1024)S(1)} %concatenate.15), channel_id=1, source_target_pairs={{0,1},{1,0},{2,3},{3,2},{4,5},{5,4},{6,7},{7,6},{8,9},{9,8},{10,11... | collective-permute-start | bytes 13064 | tf_op jit(solution)/shard_map/codes_x/ppermute | solution.py:51
  85.7 6.4 %collective-permute-start.2 = (bf16[4,128,2048]{2,1,0:T(8,128)(2,1)S(1)}, bf16[4,128,2048]{2,1,0:T(8,128)(2,1)}, u32[]{:S(2)}, u32[]{:S(2)}) collective-permute-start(bf16[4,128,2048]{2,1,0:T(8,128)(2,1)S(1)} %all-to-all-done.own_ref.up_own_ref.down_own_ref), channel_id=1, source_target_pairs={{0,8},{8,0},{16,24},{24,16},{32,40},{40,32},{48,56},{56,48},{64,72... | collective-permute-start | bytes 6291464 | tf_op jit(solution)/shard_map/codes_x/ppermute | solution.py:55
  137.9 26.7 %copy-start.2 = (f32[4096]{0:T(1024)S(1)}, f32[4096]{0:T(1024)}, u32[]{:S(2)}) copy-start(f32[4096]{0:T(1024)} %param.19) | copy-start | bytes 49156
  137.9 26.6 %copy-start.3 = (s32[256]{0:T(256)S(1)}, s32[256]{0:T(256)}, u32[]{:S(2)}) copy-start(s32[256]{0:T(256)} %param.12) | copy-start | bytes 3076
  164.5 3.4 %copy-start = (bf16[4096,1024]{1,0:T(8,128)(2,1)S(1)}, bf16[4096,1024]{1,0:T(8,128)(2,1)}, u32[]{:S(2)}) copy-start(bf16[4096,1024]{1,0:T(8,128)(2,1)} %all-gather.2.cloned.1.call-done.codes_ref) | copy-start | bytes 25165828
  178.8 14.2 %collective-permute-start.3 = (f32[3,256]{1,0:T(4,128)S(1)}, f32[3,256]{1,0:T(4,128)S(1)}, u32[]{:S(2)}, u32[]{:S(2)}) collective-permute-start(f32[3,256]{1,0:T(4,128)S(1)} %get-tuple-element.49), channel_id=1, source_target_pairs={{0,1},{1,0},{2,3},{3,2},{4,5},{5,4},{6,7},{7,6},{8,9},{9,8},{10,11... | collective-permute-start | bytes 9224 | tf_op jit(solution)/shard_map/stats/ppermute | solution.py:51
Sparse Core Ops, SparseCore 0:
  9.5 149.2 all-gather.1
